TPU v7x, 128 devices: a whole 4x4x4 slice. The times are simulated.
128 devices in a mesh: dp: 8 (over y_lo, z), gene: 16 (over x, y_hi, core).
Axes of the slice: x: 4, y: 4 (y_hi: 2, y_lo: 2; y = y_hi * 2 + y_lo), z: 4, core: 2. Of those that a mesh axis runs over, the one named last changes fastest.
Arguments:
- y_pool: bfloat16 [8192, 16384], P('dp', 'gene'), may hold values from -40 to 40
- cell_index: int32 [2048], P('dp'), may hold values from 0 to 8191, as said below
- latent_mean: float32 [32, 2048], P(None, 'dp'), may hold values from -4 to 4
- latent_logvar: float32 [32, 2048], P(None, 'dp'), may hold values from -3 to 0.5
- inducing: float32 [32, 1024], replicated, may hold values from -4 to 4
- length_sq: float32 [32], replicated, may hold values from 8 to 64
- log_var: float32 [1], replicated, may hold values from -0.5 to 0.5
- log_beta: float32 [1], replicated, may hold values from -0.5 to 0.5
- proj_mean: float32 [1024, 16384], P(None, 'gene'), may hold values from -0.0625 to 0.0625
- second_moment: float32 [1024, 1024], P('gene'), may hold values from -0.3 to 0.3
Outputs:
- grad_latent: float32 [2, 32, 2048], P(None, None, 'dp')
- grad_proj: float32 [1024, 16384], P('dp', 'gene')
- grad_logbeta: float32 [1], replicated
Inputs may be any that keep to these rules, and one draw needn't show every extreme that they name: The 256 entries of each aligned block of cell_index are distinct rows of the matching aligned block of 1024 rows of y_pool; each block names that block's first and last row.
All inputs are finite; a program needn't handle non-finite values.
Results may differ from a plain program's by a relative error of at most 0.0049.
Values may be sent and summed in bfloat16 or wider, within the bound.
A program may use at most 64 MiB of HBM per device.

v0:
```python
import jax
import jax.numpy as jnp
from jax import lax
from jax.sharding import PartitionSpec as P

CELL_BLOCK = 32


def psi_first(mean_arg, logvar_arg, inducing, length_sq, kernel_log):
    spread = length_sq[:, None] + jnp.exp(logvar_arg)
    inverse = 1.0 / spread
    quad_first = jnp.dot((inducing * inducing).T, inverse, precision=lax.Precision.HIGHEST)
    quad_cross = jnp.dot(inducing.T, mean_arg * inverse, precision=lax.Precision.HIGHEST)
    quad_last = jnp.sum(mean_arg * mean_arg * inverse, axis=0)
    prefix = kernel_log + 0.5 * jnp.sum(jnp.log(length_sq[:, None] * inverse), axis=0)
    return jnp.exp(prefix[None, :] - 0.5 * (quad_first - 2.0 * quad_cross + quad_last[None, :]))


def pair_log(rows_z, inducing, length_sq):
    factor = 0.5 / jnp.sqrt(length_sq)
    left_side = rows_z * factor[:, None]
    right_side = inducing * factor[:, None]
    cross_prod = jnp.dot(left_side.T, right_side, precision=lax.Precision.HIGHEST)
    return (
        2.0 * cross_prod
        - jnp.sum(left_side * left_side, axis=0)[:, None]
        - jnp.sum(right_side * right_side, axis=0)[None, :]
    )


def cell_block_value(
    mean_slice, logvar_slice, rows_z, inducing, length_sq, kernel_log, pair_term, weight
):
    cell_width = length_sq[:, None] + 2.0 * jnp.exp(logvar_slice)
    root_width = jnp.sqrt(2.0 * cell_width)
    left_side = (rows_z[None, :, :] - mean_slice.T[:, :, None]) / root_width.T[:, :, None]
    right_side = (inducing[None, :, :] - mean_slice.T[:, :, None]) / root_width.T[:, :, None]
    inner_prod = jnp.einsum("bqr,bqm->brm", left_side, right_side, precision=lax.Precision.HIGHEST)
    exponent = -(
        0.5 * jnp.sum(left_side * left_side, axis=1)[:, :, None]
        + 0.5 * jnp.sum(right_side * right_side, axis=1)[:, None, :]
        + inner_prod
    )
    prefix = 2.0 * kernel_log + 0.5 * jnp.sum(jnp.log(length_sq[:, None] / cell_width), axis=0)
    cells_psi = jnp.exp(prefix[:, None, None] + pair_term[None, :, :] + exponent)
    block_value = jnp.sum(cells_psi * weight[None, :, :])
    return (block_value, jnp.sum(cells_psi, axis=0))


def cell_scan(
    latent_mean,
    latent_logvar,
    rows_z,
    inducing,
    length_sq,
    kernel_log,
    pair_term,
    weight,
    block_size,
):
    latent_dims, cell_count = latent_mean.shape
    step_count = cell_count // block_size
    mean_blocks = latent_mean.reshape(latent_dims, step_count, block_size).transpose(1, 0, 2)
    logvar_blocks = latent_logvar.reshape(latent_dims, step_count, block_size).transpose(1, 0, 2)
    value_grad = jax.value_and_grad(cell_block_value, argnums=(0, 1), has_aux=True)

    def scan_step(running, slices):
        (block_value, psi_sum), grad_pair = value_grad(
            slices[0], slices[1], rows_z, inducing, length_sq, kernel_log, pair_term, weight
        )
        return ((running[0] + psi_sum, running[1] + block_value), grad_pair)

    start_state = (
        jnp.zeros((rows_z.shape[1], inducing.shape[1]), jnp.float32),
        jnp.zeros((), jnp.float32),
    )
    (psi_sum, trace_sum), (grad_mean, grad_logvar) = lax.scan(
        scan_step, start_state, (mean_blocks, logvar_blocks)
    )
    grad_mean = grad_mean.transpose(1, 0, 2).reshape(latent_dims, cell_count)
    grad_logvar = grad_logvar.transpose(1, 0, 2).reshape(latent_dims, cell_count)
    return (psi_sum, grad_mean, grad_logvar, trace_sum)


def on_device(
    y_pool,
    cell_index,
    latent_mean,
    latent_logvar,
    inducing,
    length_sq,
    log_var,
    log_beta,
    proj_mean,
    second_moment,
):
    pool_rows = y_pool.shape[0]
    local_index = cell_index - lax.axis_index("dp") * pool_rows
    cell_rows = jnp.take(y_pool, local_index, axis=0)
    noise_prec = jnp.exp(log_beta[0])
    kernel_log = log_var[0]
    inducing_count = inducing.shape[1]
    row_share = inducing_count // lax.axis_size("gene")
    rows_z = lax.dynamic_slice_in_dim(inducing, lax.axis_index("gene") * row_share, row_share, 1)
    proj_low = proj_mean.astype(jnp.bfloat16)
    second_rows = (
        lax.psum_scatter(
            lax.dot_general(
                proj_low, proj_low, (((1,), (1,)), ((), ())), preferred_element_type=jnp.float32
            ).astype(jnp.bfloat16),
            "gene",
            scatter_dimension=0,
            tiled=True,
        ).astype(jnp.float32)
        + second_moment
    )

    def first_stat(mean_arg, logvar_arg):
        return psi_first(mean_arg, logvar_arg, inducing, length_sq, kernel_log)

    psi_one, pull_back = jax.vjp(first_stat, latent_mean, latent_logvar)
    cross_term = lax.dot_general(
        proj_low, cell_rows, (((1,), (1,)), ((), ())), preferred_element_type=jnp.float32
    )
    grad_mean_one, grad_logvar_one = pull_back(noise_prec * cross_term)
    total_cross = jnp.sum(psi_one * cross_term)
    total_square = jnp.sum(jnp.square(cell_rows.astype(jnp.float32)))
    pair_term = pair_log(rows_z, inducing, length_sq)
    psi_two_rows, grad_mean_two, grad_logvar_two, trace_sum = cell_scan(
        latent_mean,
        latent_logvar,
        rows_z,
        inducing,
        length_sq,
        kernel_log,
        pair_term,
        second_rows,
        CELL_BLOCK,
    )
    psi_part = psi_two_rows.astype(jnp.bfloat16)
    partial_grad = jnp.stack(
        [
            noise_prec * grad_mean_one - 0.5 * noise_prec * grad_mean_two,
            noise_prec * grad_logvar_one - 0.5 * noise_prec * grad_logvar_two,
        ]
    )
    partial_totals = jnp.stack([total_cross, total_square, trace_sum])
    latent_sum = lax.psum(partial_grad, "gene")
    grand_total = lax.psum(partial_totals, ("dp", "gene"))
    variance = jnp.exp(latent_logvar)
    grad_latent = latent_sum + jnp.stack([-latent_mean, -0.5 * (variance - 1.0)])
    batch_size = cell_index.shape[0] * lax.axis_size("dp")
    gene_count = proj_mean.shape[1] * lax.axis_size("gene")
    grad_logbeta = (
        noise_prec
        / (batch_size * gene_count)
        * (grand_total[0] - 0.5 * grand_total[1] - 0.5 * grand_total[2])
        - 0.5 * noise_prec * jnp.exp(kernel_log)
        + 0.5
    )
    psi_low = psi_one.astype(jnp.bfloat16)
    grad_scale = noise_prec / batch_size
    psi_two_full = lax.all_gather(psi_part, "gene", axis=0, tiled=True)
    data_part = jnp.dot(psi_low, cell_rows, preferred_element_type=jnp.float32)
    stat_part = jnp.dot(psi_two_full, proj_low, preferred_element_type=jnp.float32)
    grad_proj = lax.psum_scatter(
        grad_scale * (data_part - stat_part), "dp", scatter_dimension=0, tiled=True
    )
    return (grad_latent, grad_proj, grad_logbeta.reshape(1))


def solution(mesh):
    in_specs = (
        P("dp", "gene"),
        P("dp"),
        P(None, "dp"),
        P(None, "dp"),
        P(),
        P(),
        P(),
        P(),
        P(None, "gene"),
        P("gene", None),
    )
    out_specs = (P(None, None, "dp"), P("dp", "gene"), P())
    return jax.shard_map(
        on_device, mesh=mesh, in_specs=in_specs, out_specs=out_specs, check_vma=False
    )
```

profile of v0, /device:TPU:1, one launch (start us, length us, event | category | flops | bytes accessed | tf_op | source)
XLA Modules:
  0.0 614.3 jit_solution(15857131044781296139)
XLA Ops:
  17.0 70.0 %reduce-scatter.3.cloned.1.call-done = bf16[64,1024]{1,0:T(8,128)(2,1)} async-done(((bf16[1024,1024]{1,0:T(8,128)(2,1)}), bf16[64,1024]{1,0:T(8,128)(2,1)}) %reduce-scatter.3.cloned.1.call-update) | async-done | bytes 131088 | tf_op jit(solution)/shard_map/reduce_scatter | solution.py:107
  88.6 284.1 %while.19 = (s32[]{:T(128)}, f32[64,1024]{1,0:T(8,128)S(1)}, f32[]{:T(128)}, f32[8,32,32]{1,2,0:T(8,128)}, f32[8,32,32]{1,2,0:T(8,128)}, /*index=5*/f32[]{:T(128...) while((s32[]{:T(128)}, f32[64,1024]{1,0:T(8,128)S(1)}, ...), condition=%wide.region_19.20_spmd.clone, body=%wide.region_6.19_spmd.clone.sunk | while | flops 2467556352 | bytes 63748076 | solution.py:77
  90.4 15.5 %multiply_reduce_fusion.16 = (f32[32]{0:T(128)S(1)}, f32[32,1024]{1,0:T(8,128)S(1)}, f32[32,64]{1,0:T(8,128)S(1)}, f32[]{:T(128)}, f32[64,1024]{1,0:T(8,128)S(1)}, /*index=5*/f32[32,64,1024]{2,1,0:T(8,128)}) fusion(f32[64,1024]{1,0:T(8,128)} %get-tuple-element.446, f32[32,32]{1,0:T(8,128)S(1)} %copy.57, ...), kind=kOutput, calls=%fused_computation.9.clone.1 | convolution fusion | flops 830502912 | bytes 9601284 | tf_op jit(solution)/shard_map/while/body/eval_jaxpr/jvp(bqr,bqm->brm)/dot_general | solution.py:38
  106.0 8.7 %fusion.83 = (f32[32,32]{1,0:T(8,128)S(1)}, f32[32,32]{1,0:T(8,128)S(1)}) fusion(f32[32,32]{1,0:T(8,128)S(1)} %copy.58, f32[32,32]{1,0:T(8,128)S(1)} %dynamic-slice_bitcast_fusion.2, f32[32,1024]{1,0:T(8,128)S(1)} %get-tuple-element.445, f32[32,32]{1,0:T(8,128)S(1)} %copy.57, f32[32,64,1024]{2,1,0:T(8,128)} %get-tuple-element.393, ...), kind=kOutput, calls=%fused_computation.14.clone.1 | convolution fusion | flops 820115456 | bytes 8941568 | tf_op jit(solution)/shard_map/while/body/eval_jaxpr/transpose(jvp(bqr,bqm->brm))/dot_general | solution.py:38
  125.9 15.5 %multiply_reduce_fusion.16 = (f32[32]{0:T(128)S(1)}, f32[32,1024]{1,0:T(8,128)S(1)}, f32[32,64]{1,0:T(8,128)S(1)}, f32[]{:T(128)}, f32[64,1024]{1,0:T(8,128)S(1)}, /*index=5*/f32[32,64,1024]{2,1,0:T(8,128)}) fusion(f32[64,1024]{1,0:T(8,128)} %get-tuple-element.446, f32[32,32]{1,0:T(8,128)S(1)} %copy.57, ...), kind=kOutput, calls=%fused_computation.9.clone.1 | convolution fusion | flops 830502912 | bytes 9601284 | tf_op jit(solution)/shard_map/while/body/eval_jaxpr/jvp(bqr,bqm->brm)/dot_general | solution.py:38
  141.5 8.7 %fusion.83 = (f32[32,32]{1,0:T(8,128)S(1)}, f32[32,32]{1,0:T(8,128)S(1)}) fusion(f32[32,32]{1,0:T(8,128)S(1)} %copy.58, f32[32,32]{1,0:T(8,128)S(1)} %dynamic-slice_bitcast_fusion.2, f32[32,1024]{1,0:T(8,128)S(1)} %get-tuple-element.445, f32[32,32]{1,0:T(8,128)S(1)} %copy.57, f32[32,64,1024]{2,1,0:T(8,128)} %get-tuple-element.393, ...), kind=kOutput, calls=%fused_computation.14.clone.1 | convolution fusion | flops 820115456 | bytes 8941568 | tf_op jit(solution)/shard_map/while/body/eval_jaxpr/transpose(jvp(bqr,bqm->brm))/dot_general | solution.py:38
  161.3 15.5 %multiply_reduce_fusion.16 = (f32[32]{0:T(128)S(1)}, f32[32,1024]{1,0:T(8,128)S(1)}, f32[32,64]{1,0:T(8,128)S(1)}, f32[]{:T(128)}, f32[64,1024]{1,0:T(8,128)S(1)}, /*index=5*/f32[32,64,1024]{2,1,0:T(8,128)}) fusion(f32[64,1024]{1,0:T(8,128)} %get-tuple-element.446, f32[32,32]{1,0:T(8,128)S(1)} %copy.57, ...), kind=kOutput, calls=%fused_computation.9.clone.1 | convolution fusion | flops 830502912 | bytes 9601284 | tf_op jit(solution)/shard_map/while/body/eval_jaxpr/jvp(bqr,bqm->brm)/dot_general | solution.py:38
  177.0 8.7 %fusion.83 = (f32[32,32]{1,0:T(8,128)S(1)}, f32[32,32]{1,0:T(8,128)S(1)}) fusion(f32[32,32]{1,0:T(8,128)S(1)} %copy.58, f32[32,32]{1,0:T(8,128)S(1)} %dynamic-slice_bitcast_fusion.2, f32[32,1024]{1,0:T(8,128)S(1)} %get-tuple-element.445, f32[32,32]{1,0:T(8,128)S(1)} %copy.57, f32[32,64,1024]{2,1,0:T(8,128)} %get-tuple-element.393, ...), kind=kOutput, calls=%fused_computation.14.clone.1 | convolution fusion | flops 820115456 | bytes 8941568 | tf_op jit(solution)/shard_map/while/body/eval_jaxpr/transpose(jvp(bqr,bqm->brm))/dot_general | solution.py:38
  196.8 15.5 %multiply_reduce_fusion.16 = (f32[32]{0:T(128)S(1)}, f32[32,1024]{1,0:T(8,128)S(1)}, f32[32,64]{1,0:T(8,128)S(1)}, f32[]{:T(128)}, f32[64,1024]{1,0:T(8,128)S(1)}, /*index=5*/f32[32,64,1024]{2,1,0:T(8,128)}) fusion(f32[64,1024]{1,0:T(8,128)} %get-tuple-element.446, f32[32,32]{1,0:T(8,128)S(1)} %copy.57, ...), kind=kOutput, calls=%fused_computation.9.clone.1 | convolution fusion | flops 830502912 | bytes 9601284 | tf_op jit(solution)/shard_map/while/body/eval_jaxpr/jvp(bqr,bqm->brm)/dot_general | solution.py:38
  212.5 8.7 %fusion.83 = (f32[32,32]{1,0:T(8,128)S(1)}, f32[32,32]{1,0:T(8,128)S(1)}) fusion(f32[32,32]{1,0:T(8,128)S(1)} %copy.58, f32[32,32]{1,0:T(8,128)S(1)} %dynamic-slice_bitcast_fusion.2, f32[32,1024]{1,0:T(8,128)S(1)} %get-tuple-element.445, f32[32,32]{1,0:T(8,128)S(1)} %copy.57, f32[32,64,1024]{2,1,0:T(8,128)} %get-tuple-element.393, ...), kind=kOutput, calls=%fused_computation.14.clone.1 | convolution fusion | flops 820115456 | bytes 8941568 | tf_op jit(solution)/shard_map/while/body/eval_jaxpr/transpose(jvp(bqr,bqm->brm))/dot_general | solution.py:38
  221.2 7.9 %fusion.82 = (f32[32,32]{1,0:T(8,128)S(1)}, f32[32,32]{1,0:T(8,128)S(1)}) fusion(f32[32,32]{1,0:T(8,128)S(1)} %copy.58, f32[32,32]{1,0:T(8,128)S(1)} %dynamic-slice_bitcast_fusion.2, f32[32,64]{1,0:T(8,128)S(1)} %get-tuple-element.443, f32[32,32]{1,0:T(8,128)S(1)} %copy.57, f32[32,64,1024]{2,1,0:T(8,128)S(1)} %copy-done.13, ...), kind=kOutput, calls=%fused_computation.29.clone.1 | convolution fusion | flops 812251136 | bytes 8818688 | tf_op jit(solution)/shard_map/while/body/eval_jaxpr/transpose(jvp(bqr,bqm->brm))/dot_general | solution.py:38
  232.3 15.5 %multiply_reduce_fusion.16 = (f32[32]{0:T(128)S(1)}, f32[32,1024]{1,0:T(8,128)S(1)}, f32[32,64]{1,0:T(8,128)S(1)}, f32[]{:T(128)}, f32[64,1024]{1,0:T(8,128)S(1)}, /*index=5*/f32[32,64,1024]{2,1,0:T(8,128)}) fusion(f32[64,1024]{1,0:T(8,128)} %get-tuple-element.446, f32[32,32]{1,0:T(8,128)S(1)} %copy.57, ...), kind=kOutput, calls=%fused_computation.9.clone.1 | convolution fusion | flops 830502912 | bytes 9601284 | tf_op jit(solution)/shard_map/while/body/eval_jaxpr/jvp(bqr,bqm->brm)/dot_general | solution.py:38
  248.0 8.7 %fusion.83 = (f32[32,32]{1,0:T(8,128)S(1)}, f32[32,32]{1,0:T(8,128)S(1)}) fusion(f32[32,32]{1,0:T(8,128)S(1)} %copy.58, f32[32,32]{1,0:T(8,128)S(1)} %dynamic-slice_bitcast_fusion.2, f32[32,1024]{1,0:T(8,128)S(1)} %get-tuple-element.445, f32[32,32]{1,0:T(8,128)S(1)} %copy.57, f32[32,64,1024]{2,1,0:T(8,128)} %get-tuple-element.393, ...), kind=kOutput, calls=%fused_computation.14.clone.1 | convolution fusion | flops 820115456 | bytes 8941568 | tf_op jit(solution)/shard_map/while/body/eval_jaxpr/transpose(jvp(bqr,bqm->brm))/dot_general | solution.py:38
  267.8 15.5 %multiply_reduce_fusion.16 = (f32[32]{0:T(128)S(1)}, f32[32,1024]{1,0:T(8,128)S(1)}, f32[32,64]{1,0:T(8,128)S(1)}, f32[]{:T(128)}, f32[64,1024]{1,0:T(8,128)S(1)}, /*index=5*/f32[32,64,1024]{2,1,0:T(8,128)}) fusion(f32[64,1024]{1,0:T(8,128)} %get-tuple-element.446, f32[32,32]{1,0:T(8,128)S(1)} %copy.57, ...), kind=kOutput, calls=%fused_computation.9.clone.1 | convolution fusion | flops 830502912 | bytes 9601284 | tf_op jit(solution)/shard_map/while/body/eval_jaxpr/jvp(bqr,bqm->brm)/dot_general | solution.py:38
  283.4 8.7 %fusion.83 = (f32[32,32]{1,0:T(8,128)S(1)}, f32[32,32]{1,0:T(8,128)S(1)}) fusion(f32[32,32]{1,0:T(8,128)S(1)} %copy.58, f32[32,32]{1,0:T(8,128)S(1)} %dynamic-slice_bitcast_fusion.2, f32[32,1024]{1,0:T(8,128)S(1)} %get-tuple-element.445, f32[32,32]{1,0:T(8,128)S(1)} %copy.57, f32[32,64,1024]{2,1,0:T(8,128)} %get-tuple-element.393, ...), kind=kOutput, calls=%fused_computation.14.clone.1 | convolution fusion | flops 820115456 | bytes 8941568 | tf_op jit(solution)/shard_map/while/body/eval_jaxpr/transpose(jvp(bqr,bqm->brm))/dot_general | solution.py:38
  292.2 7.9 %fusion.82 = (f32[32,32]{1,0:T(8,128)S(1)}, f32[32,32]{1,0:T(8,128)S(1)}) fusion(f32[32,32]{1,0:T(8,128)S(1)} %copy.58, f32[32,32]{1,0:T(8,128)S(1)} %dynamic-slice_bitcast_fusion.2, f32[32,64]{1,0:T(8,128)S(1)} %get-tuple-element.443, f32[32,32]{1,0:T(8,128)S(1)} %copy.57, f32[32,64,1024]{2,1,0:T(8,128)S(1)} %copy-done.13, ...), kind=kOutput, calls=%fused_computation.29.clone.1 | convolution fusion | flops 812251136 | bytes 8818688 | tf_op jit(solution)/shard_map/while/body/eval_jaxpr/transpose(jvp(bqr,bqm->brm))/dot_general | solution.py:38
  303.3 15.5 %multiply_reduce_fusion.16 = (f32[32]{0:T(128)S(1)}, f32[32,1024]{1,0:T(8,128)S(1)}, f32[32,64]{1,0:T(8,128)S(1)}, f32[]{:T(128)}, f32[64,1024]{1,0:T(8,128)S(1)}, /*index=5*/f32[32,64,1024]{2,1,0:T(8,128)}) fusion(f32[64,1024]{1,0:T(8,128)} %get-tuple-element.446, f32[32,32]{1,0:T(8,128)S(1)} %copy.57, ...), kind=kOutput, calls=%fused_computation.9.clone.1 | convolution fusion | flops 830502912 | bytes 9601284 | tf_op jit(solution)/shard_map/while/body/eval_jaxpr/jvp(bqr,bqm->brm)/dot_general | solution.py:38
  318.9 8.7 %fusion.83 = (f32[32,32]{1,0:T(8,128)S(1)}, f32[32,32]{1,0:T(8,128)S(1)}) fusion(f32[32,32]{1,0:T(8,128)S(1)} %copy.58, f32[32,32]{1,0:T(8,128)S(1)} %dynamic-slice_bitcast_fusion.2, f32[32,1024]{1,0:T(8,128)S(1)} %get-tuple-element.445, f32[32,32]{1,0:T(8,128)S(1)} %copy.57, f32[32,64,1024]{2,1,0:T(8,128)} %get-tuple-element.393, ...), kind=kOutput, calls=%fused_computation.14.clone.1 | convolution fusion | flops 820115456 | bytes 8941568 | tf_op jit(solution)/shard_map/while/body/eval_jaxpr/transpose(jvp(bqr,bqm->brm))/dot_general | solution.py:38
  338.8 15.5 %multiply_reduce_fusion.16 = (f32[32]{0:T(128)S(1)}, f32[32,1024]{1,0:T(8,128)S(1)}, f32[32,64]{1,0:T(8,128)S(1)}, f32[]{:T(128)}, f32[64,1024]{1,0:T(8,128)S(1)}, /*index=5*/f32[32,64,1024]{2,1,0:T(8,128)}) fusion(f32[64,1024]{1,0:T(8,128)} %get-tuple-element.446, f32[32,32]{1,0:T(8,128)S(1)} %copy.57, ...), kind=kOutput, calls=%fused_computation.9.clone.1 | convolution fusion | flops 830502912 | bytes 9601284 | tf_op jit(solution)/shard_map/while/body/eval_jaxpr/jvp(bqr,bqm->brm)/dot_general | solution.py:38
  354.4 8.7 %fusion.83 = (f32[32,32]{1,0:T(8,128)S(1)}, f32[32,32]{1,0:T(8,128)S(1)}) fusion(f32[32,32]{1,0:T(8,128)S(1)} %copy.58, f32[32,32]{1,0:T(8,128)S(1)} %dynamic-slice_bitcast_fusion.2, f32[32,1024]{1,0:T(8,128)S(1)} %get-tuple-element.445, f32[32,32]{1,0:T(8,128)S(1)} %copy.57, f32[32,64,1024]{2,1,0:T(8,128)} %get-tuple-element.393, ...), kind=kOutput, calls=%fused_computation.14.clone.1 | convolution fusion | flops 820115456 | bytes 8941568 | tf_op jit(solution)/shard_map/while/body/eval_jaxpr/transpose(jvp(bqr,bqm->brm))/dot_general | solution.py:38
  389.6 33.7 %all-gather.2.cloned.1.call-done = bf16[1024,1024]{1,0:T(8,128)(2,1)} async-done(((bf16[64,1024]{1,0:T(8,128)(2,1)}), bf16[1024,1024]{1,0:T(8,128)(2,1)}) %all-gather.2.cloned.1.call-update) | async-done | bytes 2097168 | tf_op jit(solution)/shard_map/all_gather | solution.py:163
  433.6 65.7 %psum.15 = f32[3]{0:T(128)S(1)} all-reduce(f32[3]{0:T(128)S(1)} %pad_maximum_fusion.1), channel_id=1, replica_groups=mesh['dp'=8,'gene'=16] {'dp','gene'}, use_global_device_ids=true, to_apply=%region_25.26 | all-reduce | flops 3 | bytes 24 | tf_op jit(solution)/shard_map/psum | solution.py:149
  501.8 48.9 %all-reduce.2.cloned.1.call-done = f32[2,32,256]{2,1,0:T(8,128)} async-done(((f32[2,32,256]{2,1,0:T(8,128)}), f32[2,32,256]{2,1,0:T(8,128)}) %all-reduce.2.cloned.1.call-update) | async-done | bytes 65552 | tf_op jit(solution)/shard_map/psum | solution.py:148
  552.2 54.5 %reduce-scatter.5.cloned.1.call-done = f32[128,1024]{1,0:T(8,128)} async-done(((f32[1024,1024]{1,0:T(8,128)}), f32[128,1024]{1,0:T(8,128)}) %reduce-scatter.5.cloned.1.call-update) | async-done | bytes 524304 | tf_op jit(solution)/shard_map/reduce_scatter | solution.py:166
  (264 shorter events, 107.8 us)
Async XLA Ops:
  7.2 367.1 %copy-start = (bf16[1024,1024]{1,0:T(8,128)(2,1)S(1)}, bf16[1024,1024]{1,0:T(8,128)(2,1)}, u32[]{:S(2)}) copy-start(bf16[1024,1024]{1,0:T(8,128)(2,1)} %param.12) | copy-start | bytes 6291460
  7.2 79.7 %copy-start.9 = (f32[64,1024]{1,0:T(8,128)S(1)}, f32[64,1024]{1,0:T(8,128)}, u32[]{:S(2)}) copy-start(f32[64,1024]{1,0:T(8,128)} %param.21) | copy-start | bytes 786436
  7.2 79.7 %reduce-scatter.3.cloned.1.call-start = ((), (), s32[]{:S(2)}) async-start(), calls=%async_computation.2 | async-start | bytes 2228224 | tf_op jit(solution)/shard_map/reduce_scatter | solution.py:107
  14.6 408.7 %all-gather.2.cloned.1.call-start = ((), (), s32[]{:S(2)}) async-start(), calls=%async_computation.4 | async-start | bytes 2228224 | tf_op jit(solution)/shard_map/all_gather | solution.py:163
  88.6 285.6 %copy-start.12 = (s32[256]{0:T(256)S(1)}, s32[256]{0:T(256)}, u32[]{:S(2)}) copy-start(s32[256]{0:T(256)} %param.13) | copy-start | bytes 3076
  106.0 8.7 %copy-start.10 = (f32[64,1024]{1,0:T(8,128)S(1)}, f32[64,1024]{1,0:T(8,128)}, u32[]{:S(2)}) copy-start(f32[64,1024]{1,0:T(8,128)} %get-tuple-element.446) | copy-start | bytes 786436 | tf_op jit(solution)/shard_map/while
  106.0 8.7 %copy-start.13 = (f32[32,64,1024]{2,1,0:T(8,128)S(1)}, f32[32,64,1024]{2,1,0:T(8,128)}, u32[]{:S(2)}) copy-start(f32[32,64,1024]{2,1,0:T(8,128)} %get-tuple-element.393) | copy-start | bytes 25165828 | tf_op jit(solution)/shard_map/while
  141.5 8.7 %copy-start.10 = (f32[64,1024]{1,0:T(8,128)S(1)}, f32[64,1024]{1,0:T(8,128)}, u32[]{:S(2)}) copy-start(f32[64,1024]{1,0:T(8,128)} %get-tuple-element.446) | copy-start | bytes 786436 | tf_op jit(solution)/shard_map/while
  141.5 8.7 %copy-start.13 = (f32[32,64,1024]{2,1,0:T(8,128)S(1)}, f32[32,64,1024]{2,1,0:T(8,128)}, u32[]{:S(2)}) copy-start(f32[32,64,1024]{2,1,0:T(8,128)} %get-tuple-element.393) | copy-start | bytes 25165828 | tf_op jit(solution)/shard_map/while
  177.0 8.7 %copy-start.10 = (f32[64,1024]{1,0:T(8,128)S(1)}, f32[64,1024]{1,0:T(8,128)}, u32[]{:S(2)}) copy-start(f32[64,1024]{1,0:T(8,128)} %get-tuple-element.446) | copy-start | bytes 786436 | tf_op jit(solution)/shard_map/while
  177.0 8.7 %copy-start.13 = (f32[32,64,1024]{2,1,0:T(8,128)S(1)}, f32[32,64,1024]{2,1,0:T(8,128)}, u32[]{:S(2)}) copy-start(f32[32,64,1024]{2,1,0:T(8,128)} %get-tuple-element.393) | copy-start | bytes 25165828 | tf_op jit(solution)/shard_map/while
  212.5 8.7 %copy-start.10 = (f32[64,1024]{1,0:T(8,128)S(1)}, f32[64,1024]{1,0:T(8,128)}, u32[]{:S(2)}) copy-start(f32[64,1024]{1,0:T(8,128)} %get-tuple-element.446) | copy-start | bytes 786436 | tf_op jit(solution)/shard_map/while
  212.5 8.7 %copy-start.13 = (f32[32,64,1024]{2,1,0:T(8,128)S(1)}, f32[32,64,1024]{2,1,0:T(8,128)}, u32[]{:S(2)}) copy-start(f32[32,64,1024]{2,1,0:T(8,128)} %get-tuple-element.393) | copy-start | bytes 25165828 | tf_op jit(solution)/shard_map/while
  247.9 8.7 %copy-start.10 = (f32[64,1024]{1,0:T(8,128)S(1)}, f32[64,1024]{1,0:T(8,128)}, u32[]{:S(2)}) copy-start(f32[64,1024]{1,0:T(8,128)} %get-tuple-element.446) | copy-start | bytes 786436 | tf_op jit(solution)/shard_map/while
  247.9 8.7 %copy-start.13 = (f32[32,64,1024]{2,1,0:T(8,128)S(1)}, f32[32,64,1024]{2,1,0:T(8,128)}, u32[]{:S(2)}) copy-start(f32[32,64,1024]{2,1,0:T(8,128)} %get-tuple-element.393) | copy-start | bytes 25165828 | tf_op jit(solution)/shard_map/while
  283.4 8.7 %copy-start.10 = (f32[64,1024]{1,0:T(8,128)S(1)}, f32[64,1024]{1,0:T(8,128)}, u32[]{:S(2)}) copy-start(f32[64,1024]{1,0:T(8,128)} %get-tuple-element.446) | copy-start | bytes 786436 | tf_op jit(solution)/shard_map/while
  283.4 8.7 %copy-start.13 = (f32[32,64,1024]{2,1,0:T(8,128)S(1)}, f32[32,64,1024]{2,1,0:T(8,128)}, u32[]{:S(2)}) copy-start(f32[32,64,1024]{2,1,0:T(8,128)} %get-tuple-element.393) | copy-start | bytes 25165828 | tf_op jit(solution)/shard_map/while
  318.9 8.7 %copy-start.13 = (f32[32,64,1024]{2,1,0:T(8,128)S(1)}, f32[32,64,1024]{2,1,0:T(8,128)}, u32[]{:S(2)}) copy-start(f32[32,64,1024]{2,1,0:T(8,128)} %get-tuple-element.393) | copy-start | bytes 25165828 | tf_op jit(solution)/shard_map/while
  354.4 8.7 %copy-start.10 = (f32[64,1024]{1,0:T(8,128)S(1)}, f32[64,1024]{1,0:T(8,128)}, u32[]{:S(2)}) copy-start(f32[64,1024]{1,0:T(8,128)} %get-tuple-element.446) | copy-start | bytes 786436 | tf_op jit(solution)/shard_map/while
  354.4 8.7 %copy-start.13 = (f32[32,64,1024]{2,1,0:T(8,128)S(1)}, f32[32,64,1024]{2,1,0:T(8,128)}, u32[]{:S(2)}) copy-start(f32[32,64,1024]{2,1,0:T(8,128)} %get-tuple-element.393) | copy-start | bytes 25165828 | tf_op jit(solution)/shard_map/while
  373.4 177.2 %all-reduce.2.cloned.1.call-start = ((), (), s32[]{:S(2)}) async-start(), calls=%async_computation.3 | async-start | bytes 131072 | tf_op jit(solution)/shard_map/psum | solution.py:148
  389.5 39.0 %copy-start.3 = (bf16[256,1024]{1,0:T(8,128)(2,1)S(1)}, bf16[256,1024]{1,0:T(8,128)(2,1)}, u32[]{:S(2)}) copy-start(bf16[256,1024]{1,0:T(8,128)(2,1)} %copy-done.2) | copy-start | bytes 1572868
  389.5 39.0 %copy-start.4 = (bf16[1024,256]{0,1:T(8,128)(2,1)S(1)}, bf16[1024,256]{0,1:T(8,128)(2,1)}, u32[]{:S(2)}) copy-start(bf16[1024,256]{0,1:T(8,128)(2,1)} %get-tuple-element.285) | copy-start | bytes 1572868
  389.6 217.1 %reduce-scatter.5.cloned.1.call-start = ((), (), s32[]{:S(2)}) async-start(), calls=%async_computation.5 | async-start | bytes 4718592 | tf_op jit(solution)/shard_map/reduce_scatter | solution.py:166
  (8 other events, 51.4 us)
Sparse Core Ops, SparseCore 0:
  14.7 72.1 reduce-scatter.2
  373.6 49.7 all-gather.1
  426.4 124.2 all-reduce.1
  553.6 52.9 reduce-scatter.4
where the time goes:
time: 615 us; the launch traced here: 614 us
  matrix products  283 us (46%)
  waiting for transfers between devices  207 us (34%)
  blocking collectives  65.7 us (11%)
  other arithmetic  26.8 us (4%)
  between operations  18.5 us (3%)
  local copies, waits for them, and re-layouts  6.8 us (1%)
    dot_general x24, matrix products, cell_block_value(): jnp.einsum('bqr,bqm->brm', left_side, right_side, precision=lax.Precision...  257 us
    reduce_scatter x1, waiting for transfers between devices, on_device(): lax.psum_scatter(lax.dot_general(proj_low, proj_low, (((1,), (1,)), ((),...  70 us
    psum x1, blocking collectives, on_device(): grand_total = lax.psum(partial_totals, ('dp', 'gene'))  65.7 us
    reduce_scatter x1, waiting for transfers between devices, on_device(): lax.psum_scatter(grad_scale * (data_part - stat_part), 'dp', scatter_dime...  54.5 us
    psum x1, waiting for transfers between devices, on_device(): latent_sum = lax.psum(partial_grad, 'gene')  48.9 us
    all_gather x1, waiting for transfers between devices, on_device(): psi_two_full = lax.all_gather(psi_part, 'gene', axis=0, tiled=True)  33.7 us
  transfers between devices with their start and end apart: 4, of which 4 were waited for; matrix products, arithmetic and copies ran while one was open for 5% of the time, Pallas kernels for 0%

commit v1 on v0

v1 whole, which is shorter than its diff:
```python
import functools

import jax
import jax.numpy as jnp
from jax import lax
from jax.experimental import pallas as pl
from jax.experimental.pallas import tpu as pltpu
from jax.sharding import PartitionSpec as P

F32 = jnp.float32
BF16 = jnp.bfloat16
LOG2E = 1.4426950408889634
MESH = pl.DeviceIdType.MESH

DP = 8
GENE = 16
CELLS = 256
LAT = 32
IND = 1024
GENES = 1024
BLOCK = IND // DP
ROWS = BLOCK // GENE
SPAN = 5
WIDTH = SPAN * BLOCK
STEPS = 4
PAIRS = ROWS * WIDTH // STEPS
DEPTH = 256
USED = 208
BLOCK_WEIGHT = (1.0, 2.0, 2.0, 2.0, 1.0)


def each(count, body):
    def step(k, carry):
        body(k)
        return carry

    lax.fori_loop(0, count, step, 0)


def split_two(value):
    high = value.astype(BF16).astype(F32)
    return high, (value - high).astype(BF16).astype(F32)


def split_three(value):
    high = value.astype(BF16).astype(F32)
    rest = value - high
    mid = rest.astype(BF16).astype(F32)
    return high, mid, (rest - mid).astype(BF16).astype(F32)


def special(rows, width):
    place = lax.broadcasted_iota(jnp.int32, (64, width), 0)
    total = jnp.zeros((64, width), F32)
    for at, row in enumerate(rows):
        total = jnp.where(place == at, jnp.broadcast_to(row, (64, width)), total)
    return total


def point_features(value, extra):
    width = value.shape[1]
    high, low = split_two(value)
    square_high, square_low = split_two(value * value)
    ones = jnp.ones((1, width), F32)
    rows = [ones, ones, ones] + list(extra)
    return jnp.concatenate(
        [high, square_high, low, square_low, high, square_high, special(rows, width)], axis=0
    )


def cell_coefficients(linear, square, constant, extra):
    width = linear.shape[1]
    high, low = split_two(linear)
    square_high, square_low = split_two(square)
    rows = list(split_three(constant)) + [jnp.ones((1, width), F32)] * extra
    return jnp.concatenate(
        [high, square_high, high, square_high, low, square_low, special(rows, width)], axis=0
    )


def moments(table):
    return table[192:193], table[0:32] + table[64:96], table[32:64] + table[96:128]


def dot(left, right, left_dim, right_dim):
    return lax.dot_general(
        left, right, (((left_dim,), (right_dim,)), ((), ())), preferred_element_type=F32
    )


def kernel(
    y_hbm,
    index_ref,
    mean_ref,
    logvar_ref,
    inducing_ref,
    length_ref,
    log_var_ref,
    log_beta_ref,
    proj_hbm,
    moment_ref,
    latent_out,
    proj_out,
    total_out,
    proj_f32,
    proj_low,
    y_ref,
    cell_ref,
    psi_low_ref,
    lat_all,
    gram_send,
    gram_recv,
    data_send,
    data_recv,
    data_own,
    pair_feat,
    cell_coef,
    inv_width,
    weight_ref,
    psi_acc,
    first_ref,
    trace_ref,
    grad_send,
    grad_recv,
    psi_send,
    psi_recv,
    part_send,
    part_recv,
    sum_all,
    block_send,
    block_recv,
    total_recv,
    local_sem,
    dp_sems,
    gene_sems,
):
    d = lax.axis_index("dp")
    g = lax.axis_index("gene")

    def remote(src, dst, axis, send_sem, recv_sem, peer):
        return pltpu.make_async_remote_copy(
            src_ref=src,
            dst_ref=dst,
            send_sem=send_sem,
            recv_sem=recv_sem,
            device_id={axis: peer},
            device_id_type=MESH,
        )

    def dp_peer(k):
        return lax.rem(d + 1 + k, DP)

    def gene_peer(k):
        return lax.rem(g + 1 + k, GENE)

    def dp_copy(kind, src, dst, peer, slot):
        return remote(src, dst, "dp", dp_sems.at[kind, 0, peer], dp_sems.at[kind, 1, slot], peer)

    def gene_copy(kind, src, dst, peer, slot):
        return remote(
            src, dst, "gene", gene_sems.at[kind, 0, peer], gene_sems.at[kind, 1, slot], peer
        )

    quarter = IND // 4
    proj_copies = [
        pltpu.make_async_copy(
            proj_hbm.at[pl.ds(quarter * k, quarter)],
            proj_f32.at[pl.ds(quarter * k, quarter)],
            local_sem.at[k],
        )
        for k in range(4)
    ]
    y_copy = pltpu.make_async_copy(y_hbm, y_ref, local_sem.at[4])
    for copy in proj_copies:
        copy.start()
    y_copy.start()

    barrier = pltpu.get_barrier_semaphore()
    each(
        DP - 1,
        lambda k: pl.semaphore_signal(
            barrier, inc=1, device_id={"dp": dp_peer(k)}, device_id_type=MESH
        ),
    )
    each(
        GENE - 1,
        lambda k: pl.semaphore_signal(
            barrier, inc=1, device_id={"gene": gene_peer(k)}, device_id_type=MESH
        ),
    )
    lat_all[d, 0:LAT] = mean_ref[...]
    lat_all[d, LAT : 2 * LAT] = logvar_ref[...]
    pl.semaphore_wait(barrier, DP + GENE - 2)

    def latent_copy(peer, slot):
        return dp_copy(0, lat_all.at[d], lat_all.at[slot], peer, slot)

    each(DP - 1, lambda k: latent_copy(dp_peer(k), d).start())

    for k in range(4):
        proj_copies[k].wait()
        proj_low[quarter * k : quarter * (k + 1)] = proj_f32[
            quarter * k : quarter * (k + 1)
        ].astype(BF16)

    own_rows = proj_low[pl.ds(pl.multiple_of(BLOCK * d, BLOCK), BLOCK)]
    row_of = lax.broadcasted_iota(jnp.int32, (BLOCK, 64), 0) + BLOCK * d
    col_of = lax.broadcasted_iota(jnp.int32, (BLOCK, 64), 1) + 64 * g
    pick_rows = jnp.where(row_of == col_of, 1.0, 0.0).astype(BF16)
    moment_cols = moment_ref[:, pl.ds(pl.multiple_of(BLOCK * d, BLOCK), BLOCK)].astype(BF16)
    for o in range(SPAN):
        at = lax.rem(d + o, DP)
        start = pl.multiple_of(BLOCK * at, BLOCK)
        gram = dot(own_rows, proj_low[pl.ds(start, BLOCK)], 1, 1)
        moment_rows = dot(pick_rows, moment_ref[:, pl.ds(start, BLOCK)].astype(BF16), 1, 0)
        place_row = lax.broadcasted_iota(jnp.int32, (64, BLOCK), 0) + 64 * g
        place_col = lax.broadcasted_iota(jnp.int32, (64, BLOCK), 1) + BLOCK * at
        place = jnp.where(place_row == place_col, 1.0, 0.0).astype(BF16)
        moment_part = moment_rows + dot(moment_cols, place, 0, 0)
        block = BLOCK_WEIGHT[o] * (gram + 0.5 * moment_part)
        gram_send[:, :, BLOCK * o : BLOCK * (o + 1)] = block.reshape(GENE, ROWS, BLOCK)

    def gram_copy(peer, slot):
        return gene_copy(0, gram_send.at[peer], gram_recv.at[slot], peer, slot)

    each(GENE - 1, lambda k: gram_copy(gene_peer(k), g).start())
    gram_recv[g] = gram_send[g]

    kernel_log = log_var_ref[0]
    eye = lax.broadcasted_iota(jnp.int32, (LAT, LAT), 0) == lax.broadcasted_iota(
        jnp.int32, (LAT, LAT), 1
    )
    length = jnp.sum(
        jnp.where(eye, jnp.broadcast_to(length_ref[...], (LAT, LAT)), 0.0), axis=1, keepdims=True
    )
    mean = mean_ref[...]
    variance = jnp.exp(logvar_ref[...])
    inverse = 1.0 / (length + variance)
    constant = kernel_log + 0.5 * jnp.sum(
        jnp.log(length * inverse) - mean * mean * inverse, axis=0, keepdims=True
    )
    coef = cell_coefficients(
        LOG2E * mean * inverse, (-0.5 * LOG2E) * inverse, LOG2E * constant, 0
    ).astype(BF16)
    features = point_features(inducing_ref[...], []).astype(BF16)
    psi_one = jnp.exp2(dot(features, coef, 0, 0))
    psi_low_ref[...] = psi_one.astype(BF16)

    eye_cells = lax.broadcasted_iota(jnp.int32, (CELLS, CELLS), 0) == lax.broadcasted_iota(
        jnp.int32, (CELLS, CELLS), 1
    )
    local_index = (index_ref[...] - d * IND).astype(F32)
    index_col = jnp.sum(
        jnp.where(eye_cells, jnp.broadcast_to(local_index, (CELLS, CELLS)), 0.0),
        axis=1,
        keepdims=True,
    )
    row_number = lax.broadcasted_iota(jnp.int32, (CELLS, IND), 1).astype(F32)
    one_hot = jnp.where(row_number == index_col, 1.0, 0.0).astype(BF16)
    y_copy.wait()
    cell_rows = dot(one_hot, y_ref[...], 1, 0)
    cell_ref[...] = cell_rows.astype(BF16)
    squares = jnp.sum((cell_rows * cell_rows).reshape(CELLS // 8, 8, GENES), axis=0)
    square_tile = functools.reduce(
        jnp.add, [squares[:, 128 * k : 128 * (k + 1)] for k in range(GENES // 128)]
    )

    def data_copy(peer, slot):
        return dp_copy(1, data_send.at[peer], data_recv.at[slot], peer, slot)

    def data_step(k):
        peer = dp_peer(k)
        rows = psi_low_ref[pl.ds(pl.multiple_of(BLOCK * peer, BLOCK), BLOCK)]
        data_send[peer] = dot(rows, cell_ref[...], 1, 0).astype(BF16)
        data_copy(peer, d).start()

    each(DP - 1, data_step)
    data_own[...] = dot(
        psi_low_ref[pl.ds(pl.multiple_of(BLOCK * d, BLOCK), BLOCK)], cell_ref[...], 1, 0
    )

    cross = dot(proj_low[...], cell_ref[...], 1, 1)
    product = psi_one * cross
    sum_0, sum_1, sum_2 = moments(dot(features, product.astype(BF16), 1, 0))
    beta = jnp.exp(jnp.full((1, CELLS), log_beta_ref[0], F32))
    beta_sq = beta * beta
    first_ref[0:LAT] = beta_sq * inverse * (sum_1 - mean * sum_0)
    first_ref[LAT : 2 * LAT] = (
        beta_sq
        * 0.5
        * variance
        * inverse
        * (inverse * (sum_2 - 2.0 * mean * sum_1 + mean * mean * sum_0) - sum_0)
    )

    base = inducing_ref[:, pl.ds(pl.multiple_of(BLOCK * d, BLOCK), BLOCK)]
    lane = lax.broadcasted_iota(jnp.int32, (LAT, BLOCK), 1)
    quarter_inv = (-0.25 * LOG2E) / length

    def feature_step(i):
        column = jnp.sum(jnp.where(lane == ROWS * g + i, base, 0.0), axis=1, keepdims=True)
        for o in range(SPAN):
            at = lax.rem(d + o, DP)
            points = inducing_ref[:, pl.ds(pl.multiple_of(BLOCK * at, BLOCK), BLOCK)]
            gap = points - column
            pair = jnp.sum(gap * gap * quarter_inv, axis=0, keepdims=True)
            block = point_features(0.5 * (points + column), split_three(pair))
            offset = pl.multiple_of(lax.rem(i, 2) * WIDTH + BLOCK * o, BLOCK)
            pair_feat[lax.div(i, 2), :, pl.ds(offset, BLOCK)] = block.astype(BF16)

    each(ROWS, feature_step)

    def coefficient_step(k):
        at = dp_peer(k)

        @pl.when(k < DP - 1)
        def _():
            latent_copy(at, at).wait_recv()

        cell_mean = lat_all[at, 0:LAT]
        cell_var = jnp.exp(lat_all[at, LAT : 2 * LAT])
        inverse_w = 1.0 / (length + 2.0 * cell_var)
        inv_width[at] = inverse_w
        const = 2.0 * kernel_log + jnp.sum(
            0.5 * jnp.log(length * inverse_w) - cell_mean * cell_mean * inverse_w,
            axis=0,
            keepdims=True,
        )
        block = cell_coefficients(
            (2.0 * LOG2E) * cell_mean * inverse_w, -LOG2E * inverse_w, LOG2E * const, 3
        )
        cell_coef[at] = block.T.astype(BF16)

    each(DP, coefficient_step)

    each(GENE - 1, lambda k: gram_copy(gene_peer(k), gene_peer(k)).wait_recv())
    weight = jnp.sum(gram_recv[...], axis=0)
    for i in range(ROWS):
        weight_ref[i // 2, :, WIDTH * (i % 2) : WIDTH * (i % 2 + 1)] = jnp.broadcast_to(
            weight[i : i + 1], (8, WIDTH)
        )

    psi_acc[...] = jnp.zeros_like(psi_acc)
    trace_ref[...] = jnp.zeros_like(trace_ref)

    def grad_copy(peer, slot):
        return dp_copy(2, grad_send.at[peer], grad_recv.at[slot], peer, slot)

    def cell_step(k):
        at = dp_peer(k)
        table = jnp.zeros((USED, CELLS), F32)
        for s in range(STEPS):
            psi = jnp.exp2(dot(cell_coef[at], pair_feat[s], 1, 0))
            psi = psi.reshape(CELLS // 8, 8, PAIRS)
            psi_acc[s] += jnp.sum(psi, axis=0)
            weighted = (psi * weight_ref[s][None]).reshape(CELLS, PAIRS).astype(BF16)
            table = table + dot(pair_feat[s, 0:USED], weighted, 1, 1)
        mom_0, mom_1, mom_2 = moments(table)
        cell_mean = lat_all[at, 0:LAT]
        cell_var = jnp.exp(lat_all[at, LAT : 2 * LAT])
        inverse_w = inv_width[at]
        trace_ref[...] += mom_0
        grad_send[at, 0:LAT] = -beta * inverse_w * (mom_1 - cell_mean * mom_0)
        grad_send[at, LAT : 2 * LAT] = (
            -beta
            * cell_var
            * inverse_w
            * (
                inverse_w * (mom_2 - 2.0 * cell_mean * mom_1 + cell_mean * cell_mean * mom_0)
                - 0.5 * mom_0
            )
        )

        @pl.when(k < DP - 1)
        def _():
            grad_copy(at, d).start()

    each(DP, cell_step)

    total_row = sum_0 - 0.5 * trace_ref[...]
    total_row = total_row[:, 0:128] + total_row[:, 128:256]
    first_row = lax.broadcasted_iota(jnp.int32, (8, 128), 0) == 0
    total_tile = jnp.where(first_row, jnp.broadcast_to(total_row, (8, 128)), 0.0) - (
        0.5 * square_tile
    )
    for i in range(ROWS):
        row = jnp.sum(
            psi_acc[i // 2, :, WIDTH * (i % 2) : WIDTH * (i % 2 + 1)], axis=0, keepdims=True
        )
        psi_send[i : i + 1, 0:WIDTH] = row
    psi_send[:, WIDTH : WIDTH + 128] = total_tile

    def psi_copy(peer, slot):
        return gene_copy(1, psi_send, psi_recv.at[slot], peer, slot)

    each(GENE - 1, lambda k: psi_copy(gene_peer(k), g).start())
    psi_recv[g] = psi_send[...]

    each(DP - 1, lambda k: grad_copy(dp_peer(k), dp_peer(k)).wait_recv())
    grad_recv[d] = grad_send[d]
    own_grad = first_ref[...] + jnp.sum(grad_recv[...], axis=0)
    for p in range(GENE):
        part_send[p] = own_grad[
            8 * (p // 2) : 8 * (p // 2 + 1), 128 * (p % 2) : 128 * (p % 2 + 1)
        ]

    def part_copy(peer, slot):
        return gene_copy(2, part_send.at[peer], part_recv.at[slot], peer, slot)

    each(GENE - 1, lambda k: part_copy(gene_peer(k), g).start())
    part_recv[g] = part_send[g]

    each(GENE - 1, lambda k: psi_copy(gene_peer(k), gene_peer(k)).wait_recv())
    total_recv[d] = jnp.sum(psi_recv[:, :, WIDTH : WIDTH + 128], axis=0)
    psi_rows = [
        psi_recv[:, :, BLOCK * o : BLOCK * (o + 1)].reshape(BLOCK, BLOCK).astype(BF16)
        for o in range(SPAN)
    ]
    for o in range(1, 4):
        block_send[o - 1] = psi_rows[o]

    def block_copy(o, slot):
        return dp_copy(
            3, block_send.at[o - 1], block_recv.at[slot], lax.rem(d + o, DP), slot
        )

    def total_copy(peer, slot):
        return dp_copy(4, total_recv.at[d], total_recv.at[slot], peer, slot)

    for o in range(1, 4):
        block_copy(o, o - 1).start()
    each(DP - 1, lambda k: total_copy(dp_peer(k), d).start())

    each(GENE - 1, lambda k: part_copy(gene_peer(k), gene_peer(k)).wait_recv())
    sum_all[g] = jnp.sum(part_recv[...], axis=0)

    def sum_copy(peer, slot):
        return gene_copy(3, sum_all.at[g], sum_all.at[slot], peer, slot)

    each(GENE - 1, lambda k: sum_copy(gene_peer(k), g).start())

    stat = jnp.zeros((BLOCK, GENES), F32)
    for o in range(SPAN):
        at = lax.rem(d + o, DP)
        stat = stat + dot(
            psi_rows[o], proj_low[pl.ds(pl.multiple_of(BLOCK * at, BLOCK), BLOCK)], 1, 0
        )
    each(DP - 1, lambda k: data_copy(dp_peer(k), dp_peer(k)).wait_recv())
    data_recv[d] = jnp.zeros((BLOCK, GENES), BF16)
    data = data_own[...]
    for p in range(DP):
        data = data + data_recv[p].astype(F32)
    for o in range(1, 4):
        block_copy(o, o - 1).wait_recv()
        at = lax.rem(d + (DP - o), DP)
        stat = stat + dot(
            block_recv[o - 1],
            proj_low[pl.ds(pl.multiple_of(BLOCK * at, BLOCK), BLOCK)],
            0,
            0,
        )
    proj_out[...] = data - stat

    each(GENE - 1, lambda k: sum_copy(gene_peer(k), gene_peer(k)).wait_recv())
    for p in range(GENE):
        latent_out[8 * (p // 2) : 8 * (p // 2 + 1), 128 * (p % 2) : 128 * (p % 2 + 1)] = sum_all[p]
    each(DP - 1, lambda k: total_copy(dp_peer(k), dp_peer(k)).wait_recv())
    total_out[...] = jnp.sum(total_recv[...], axis=0)

    def sent_dp(k):
        peer = dp_peer(k)
        latent_copy(peer, d).wait_send()
        data_copy(peer, d).wait_send()
        grad_copy(peer, d).wait_send()
        total_copy(peer, d).wait_send()

    def sent_gene(k):
        peer = gene_peer(k)
        gram_copy(peer, g).wait_send()
        psi_copy(peer, g).wait_send()
        part_copy(peer, g).wait_send()
        sum_copy(peer, g).wait_send()

    each(DP - 1, sent_dp)
    each(GENE - 1, sent_gene)
    for o in range(1, 4):
        block_copy(o, o - 1).wait_send()


def on_device(
    y_pool,
    cell_index,
    latent_mean,
    latent_logvar,
    inducing,
    length_sq,
    log_var,
    log_beta,
    proj_mean,
    second_moment,
):
    vmem = pl.BlockSpec(memory_space=pltpu.VMEM)
    smem = pl.BlockSpec(memory_space=pltpu.SMEM)
    hbm = pl.BlockSpec(memory_space=pl.ANY)
    scratch = [
        pltpu.VMEM((IND, GENES), F32),
        pltpu.VMEM((IND, GENES), BF16),
        pltpu.VMEM((IND, GENES), BF16),
        pltpu.VMEM((CELLS, GENES), BF16),
        pltpu.VMEM((IND, CELLS), BF16),
        pltpu.VMEM((DP, 2 * LAT, CELLS), F32),
        pltpu.VMEM((GENE, ROWS, WIDTH), F32),
        pltpu.VMEM((GENE, ROWS, WIDTH), F32),
        pltpu.VMEM((DP, BLOCK, GENES), BF16),
        pltpu.VMEM((DP, BLOCK, GENES), BF16),
        pltpu.VMEM((BLOCK, GENES), F32),
        pltpu.VMEM((STEPS, DEPTH, PAIRS), BF16),
        pltpu.VMEM((DP, CELLS, DEPTH), BF16),
        pltpu.VMEM((DP, LAT, CELLS), F32),
        pltpu.VMEM((STEPS, 8, PAIRS), F32),
        pltpu.VMEM((STEPS, 8, PAIRS), F32),
        pltpu.VMEM((2 * LAT, CELLS), F32),
        pltpu.VMEM((1, CELLS), F32),
        pltpu.VMEM((DP, 2 * LAT, CELLS), F32),
        pltpu.VMEM((DP, 2 * LAT, CELLS), F32),
        pltpu.VMEM((ROWS, WIDTH + 128), F32),
        pltpu.VMEM((GENE, ROWS, WIDTH + 128), F32),
        pltpu.VMEM((GENE, 8, 128), F32),
        pltpu.VMEM((GENE, 8, 128), F32),
        pltpu.VMEM((GENE, 8, 128), F32),
        pltpu.VMEM((3, BLOCK, BLOCK), BF16),
        pltpu.VMEM((3, BLOCK, BLOCK), BF16),
        pltpu.VMEM((DP, 8, 128), F32),
        pltpu.SemaphoreType.DMA((5,)),
        pltpu.SemaphoreType.DMA((5, 2, DP)),
        pltpu.SemaphoreType.DMA((4, 2, GENE)),
    ]
    latent, proj, total = pl.pallas_call(
        kernel,
        out_shape=(
            jax.ShapeDtypeStruct((2 * LAT, CELLS), F32),
            jax.ShapeDtypeStruct((BLOCK, GENES), F32),
            jax.ShapeDtypeStruct((8, 128), F32),
        ),
        in_specs=[hbm, vmem, vmem, vmem, vmem, vmem, smem, smem, hbm, vmem],
        out_specs=(vmem, vmem, vmem),
        scratch_shapes=scratch,
        compiler_params=pltpu.CompilerParams(
            collective_id=0, has_side_effects=True, vmem_limit_bytes=56 * 1024 * 1024
        ),
        name="bound_gradients",
    )(
        y_pool,
        cell_index.reshape(1, CELLS),
        latent_mean,
        latent_logvar,
        inducing,
        length_sq.reshape(1, LAT),
        log_var,
        log_beta,
        proj_mean,
        second_moment,
    )
    noise_prec = jnp.exp(log_beta[0])
    batch_size = CELLS * DP
    gene_count = GENES * GENE
    variance = jnp.exp(latent_logvar)
    grad_latent = latent.reshape(2, LAT, CELLS) + jnp.stack(
        [-latent_mean, -0.5 * (variance - 1.0)]
    )
    grad_proj = (noise_prec / batch_size) * proj
    grad_logbeta = (
        noise_prec / (batch_size * gene_count) * jnp.sum(total)
        - 0.5 * noise_prec * jnp.exp(log_var[0])
        + 0.5
    )
    return (grad_latent, grad_proj, grad_logbeta.reshape(1))


def solution(mesh):
    in_specs = (
        P("dp", "gene"),
        P("dp"),
        P(None, "dp"),
        P(None, "dp"),
        P(),
        P(),
        P(),
        P(),
        P(None, "gene"),
        P("gene", None),
    )
    out_specs = (P(None, None, "dp"), P("dp", "gene"), P())
    return jax.shard_map(
        on_device, mesh=mesh, in_specs=in_specs, out_specs=out_specs, check_vma=False
    )
```

time: 615 us -> 79 us (0.13)
  matrix products: 283 us -> 0 us
  waiting for transfers between devices: 207 us -> 0 us
  Pallas kernels: 0 us -> 69.4 us
  blocking collectives: 65.7 us -> 0 us
  other arithmetic: 26.8 us -> 5.44 us
  between operations: 18.5 us -> 3.8 us
  local copies, waits for them, and re-layouts: 6.8 us -> 0 us
    dot_general x33 -> x0, matrix products: 283 us -> none  [the longest x24 257 us: cell_block_value(): jnp.einsum('bqr,bqm->brm', left_side, right_side, precision=lax.Precision...]
    reduce_scatter x2 -> x0, waiting for transfers between devices: 124 us -> none  [the longest x1 70 us: on_device(): lax.psum_scatter(lax.dot_general(proj_low, proj_low, (((1,), (1,)), ((),...]
    pallas_call x0 -> x1, Pallas kernels: none -> 69.4 us  [on_device(): pl.pallas_call(kernel, out_shape=(jax.ShapeDtypeStruct((2 * LAT, CELLS),...]
    psum x1 -> x0, blocking collectives: 65.7 us -> none  [on_device(): grand_total = lax.psum(partial_totals, ('dp', 'gene'))]
    psum x1 -> x0, waiting for transfers between devices: 48.9 us -> none  [on_device(): latent_sum = lax.psum(partial_grad, 'gene')]
    all_gather x1 -> x0, waiting for transfers between devices: 33.7 us -> none  [on_device(): psi_two_full = lax.all_gather(psi_part, 'gene', axis=0, tiled=True)]
    reduce_sum x28 -> x1, other arithmetic: 12.6 us -> 1.29 us  [on_device(): jnp.sum(total)]
  transfers between devices with their start and end apart: 4 -> 0, of which waited for: 4 -> 0; matrix products, arithmetic and copies ran while one was open for 5% -> 0% of each run, Pallas kernels for 0% -> 0%
where the time goes in v1:
time: 79 us; the launch traced here: 78.7 us
  Pallas kernels  69.4 us (88%)
  other arithmetic  5.44 us (7%)
  between operations  3.8 us (5%)
    pallas_call x1, Pallas kernels, on_device(): pl.pallas_call(kernel, out_shape=(jax.ShapeDtypeStruct((2 * LAT, CELLS),...  69.4 us
    mul x1, other arithmetic, on_device(): grad_proj = noise_prec / batch_size * proj  1.88 us

profile of v1, /device:TPU:1, one launch (start us, length us, event | category | flops | bytes accessed | tf_op | source)
XLA Modules:
  0.0 78.7 jit_solution(17694704548701969408)
XLA Ops:
  2.0 0.8 %multiply_bitcast_fusion = (f32[1,32,256]{2,1,0:T(8,128)S(1)}, f32[1,32,256]{2,1,0:T(8,128)S(1)}) fusion(f32[32,256]{1,0:T(8,128)} %logvar_ref.1, f32[32,256]{1,0:T(8,128)} %mean_ref.1), kind=kLoop, calls=%fused_computation.2 | loop fusion | flops 24576 | bytes 131072 | tf_op jit(solution)/shard_map/stack | solution.py:568
  2.8 69.4 %bound_gradients.1 = (f32[64,256]{1,0:T(8,128)}, f32[128,1024]{1,0:T(8,128)}, f32[8,128]{1,0:T(8,128)}) custom-call(bf16[1024,1024]{1,0:T(8,128)(2,1)} %y_hbm.1, s32[1,256]{1,0:T(1,128)} %bitcast.12, f32[32,256]{1,0:T(8,128)} %mean_ref.1, f32[32,256]{1,0:T(8,128)} %logvar_ref.1, f32[32,1024]{1,0:T(8,128)} %inducing_ref.1, f32[1,32]{1,0:T(1,128)} %bitcast.13, ...), custom_call_target="tpu_custom_call" | custom-call | tf_op jit(solution)/shard_map/bound_gradients/pallas_call | solution.py:538
  72.2 1.3 %reduce_sum.9 = f32[]{:T(128)} reduce(f32[8,128]{1,0:T(8,128)} %get-tuple-element.8, f32[]{:T(128)} %constant.16.clone.1), dimensions={0,1}, to_apply=%region_0.0 | reduce | flops 1023 | bytes 4104 | tf_op jit(solution)/shard_map/reduce_sum | solution.py:573
  74.2 1.5 %maximum_add_fusion = f32[2,32,256]{2,1,0:T(8,128)} fusion(f32[2,32,256]{2,1,0:T(8,128)} %bitcast.11, f32[1,32,256]{2,1,0:T(8,128)S(1)} %get-tuple-element.9, f32[1,32,256]{2,1,0:T(8,128)S(1)} %get-tuple-element.10), kind=kLoop, calls=%fused_computation.1 | loop fusion | flops 32768 | bytes 196608 | tf_op jit(solution)/shard_map/add | solution.py:568
  75.6 1.9 %broadcast_multiply_fusion = f32[128,1024]{1,0:T(8,128)} fusion(f32[128,1024]{1,0:T(8,128)} %get-tuple-element.7, f32[]{:T(128)} %bitcast.5), kind=kLoop, calls=%fused_computation | loop fusion | flops 131072 | bytes 1048580 | tf_op jit(solution)/shard_map/mul | solution.py:571

commit v2 on v1

--- a/solution.py
+++ b/solution.py
@@ -13,6 +13,7 @@
 MESH = pl.DeviceIdType.MESH
 
 DP = 8
+DP_Z = 4
 GENE = 16
 CELLS = 256
 LAT = 32
@@ -25,7 +26,8 @@
 STEPS = 4
 PAIRS = ROWS * WIDTH // STEPS
 DEPTH = 256
-USED = 208
+HALF = 384
+SPLIT = 4
 BLOCK_WEIGHT = (1.0, 2.0, 2.0, 2.0, 1.0)
 
 
@@ -105,8 +107,9 @@
     proj_f32,
     proj_low,
     y_ref,
-    cell_ref,
+    cell_all,
     psi_low_ref,
+    psi_side,
     lat_all,
     gram_send,
     gram_recv,
@@ -114,6 +117,7 @@
     data_recv,
     data_own,
     pair_feat,
+    pair_cols,
     cell_coef,
     inv_width,
     weight_ref,
@@ -122,8 +126,7 @@
     trace_ref,
     grad_send,
     grad_recv,
-    psi_send,
-    psi_recv,
+    psi_all,
     part_send,
     part_recv,
     sum_all,
@@ -133,9 +136,16 @@
     local_sem,
     dp_sems,
     gene_sems,
+    pair_sems,
 ):
     d = lax.axis_index("dp")
     g = lax.axis_index("gene")
+    z = lax.rem(d, DP_Z)
+    side = d - z
+    core = lax.rem(g, 2)
+    place = lax.div(g, 2)
+    group = GENE // 2 * core + place
+    sibling = g + 1 - 2 * core
 
     def remote(src, dst, axis, send_sem, recv_sem, peer):
         return pltpu.make_async_remote_copy(
@@ -153,6 +163,15 @@
     def gene_peer(k):
         return lax.rem(g + 1 + k, GENE)
 
+    def chip_peer(k):
+        return lax.rem(place + 1 + k, GENE // 2)
+
+    def z_peer(k):
+        return side + lax.rem(z + 1 + k, DP_Z)
+
+    def cell_order(k):
+        return lax.rem(side + DP_Z * (1 - lax.div(k, DP_Z)), DP) + lax.rem(z + 1 + k, DP_Z)
+
     def dp_copy(kind, src, dst, peer, slot):
         return remote(src, dst, "dp", dp_sems.at[kind, 0, peer], dp_sems.at[kind, 1, slot], peer)
 
@@ -160,6 +179,9 @@
         return remote(
             src, dst, "gene", gene_sems.at[kind, 0, peer], gene_sems.at[kind, 1, slot], peer
         )
+
+    def pair_copy(kind, src, dst):
+        return remote(src, dst, "gene", pair_sems.at[kind, 0], pair_sems.at[kind, 1], sibling)
 
     quarter = IND // 4
     proj_copies = [
@@ -188,12 +210,11 @@
             barrier, inc=1, device_id={"gene": gene_peer(k)}, device_id_type=MESH
         ),
     )
-    lat_all[d, 0:LAT] = mean_ref[...]
-    lat_all[d, LAT : 2 * LAT] = logvar_ref[...]
+    lat_all[core, d] = jnp.where(core == 0, mean_ref[...], logvar_ref[...])
     pl.semaphore_wait(barrier, DP + GENE - 2)
 
     def latent_copy(peer, slot):
-        return dp_copy(0, lat_all.at[d], lat_all.at[slot], peer, slot)
+        return dp_copy(0, lat_all.at[core, d], lat_all.at[core, slot], peer, slot)
 
     each(DP - 1, lambda k: latent_copy(dp_peer(k), d).start())
 
@@ -213,38 +234,21 @@
         start = pl.multiple_of(BLOCK * at, BLOCK)
         gram = dot(own_rows, proj_low[pl.ds(start, BLOCK)], 1, 1)
         moment_rows = dot(pick_rows, moment_ref[:, pl.ds(start, BLOCK)].astype(BF16), 1, 0)
-        place_row = lax.broadcasted_iota(jnp.int32, (64, BLOCK), 0) + 64 * g
-        place_col = lax.broadcasted_iota(jnp.int32, (64, BLOCK), 1) + BLOCK * at
-        place = jnp.where(place_row == place_col, 1.0, 0.0).astype(BF16)
-        moment_part = moment_rows + dot(moment_cols, place, 0, 0)
+        to_row = lax.broadcasted_iota(jnp.int32, (64, BLOCK), 0) + 64 * g
+        to_col = lax.broadcasted_iota(jnp.int32, (64, BLOCK), 1) + BLOCK * at
+        to_place = jnp.where(to_row == to_col, 1.0, 0.0).astype(BF16)
+        moment_part = moment_rows + dot(moment_cols, to_place, 0, 0)
         block = BLOCK_WEIGHT[o] * (gram + 0.5 * moment_part)
         gram_send[:, :, BLOCK * o : BLOCK * (o + 1)] = block.reshape(GENE, ROWS, BLOCK)
 
+    def group_of(device):
+        return GENE // 2 * lax.rem(device, 2) + lax.div(device, 2)
+
     def gram_copy(peer, slot):
-        return gene_copy(0, gram_send.at[peer], gram_recv.at[slot], peer, slot)
+        return gene_copy(0, gram_send.at[group_of(peer)], gram_recv.at[slot], peer, slot)
 
     each(GENE - 1, lambda k: gram_copy(gene_peer(k), g).start())
-    gram_recv[g] = gram_send[g]
-
-    kernel_log = log_var_ref[0]
-    eye = lax.broadcasted_iota(jnp.int32, (LAT, LAT), 0) == lax.broadcasted_iota(
-        jnp.int32, (LAT, LAT), 1
-    )
-    length = jnp.sum(
-        jnp.where(eye, jnp.broadcast_to(length_ref[...], (LAT, LAT)), 0.0), axis=1, keepdims=True
-    )
-    mean = mean_ref[...]
-    variance = jnp.exp(logvar_ref[...])
-    inverse = 1.0 / (length + variance)
-    constant = kernel_log + 0.5 * jnp.sum(
-        jnp.log(length * inverse) - mean * mean * inverse, axis=0, keepdims=True
-    )
-    coef = cell_coefficients(
-        LOG2E * mean * inverse, (-0.5 * LOG2E) * inverse, LOG2E * constant, 0
-    ).astype(BF16)
-    features = point_features(inducing_ref[...], []).astype(BF16)
-    psi_one = jnp.exp2(dot(features, coef, 0, 0))
-    psi_low_ref[...] = psi_one.astype(BF16)
+    gram_recv[g] = gram_send[group]
 
     eye_cells = lax.broadcasted_iota(jnp.int32, (CELLS, CELLS), 0) == lax.broadcasted_iota(
         jnp.int32, (CELLS, CELLS), 1
@@ -259,27 +263,42 @@
     one_hot = jnp.where(row_number == index_col, 1.0, 0.0).astype(BF16)
     y_copy.wait()
     cell_rows = dot(one_hot, y_ref[...], 1, 0)
-    cell_ref[...] = cell_rows.astype(BF16)
+    cell_all[0] = cell_rows.astype(BF16)
+    across = lax.rem(d + DP_Z, DP)
+
+    def cell_copy():
+        return dp_copy(3, cell_all.at[0], cell_all.at[1], across, 7)
+
+    cell_copy().start()
     squares = jnp.sum((cell_rows * cell_rows).reshape(CELLS // 8, 8, GENES), axis=0)
     square_tile = functools.reduce(
         jnp.add, [squares[:, 128 * k : 128 * (k + 1)] for k in range(GENES // 128)]
     )
 
-    def data_copy(peer, slot):
-        return dp_copy(1, data_send.at[peer], data_recv.at[slot], peer, slot)
-
-    def data_step(k):
-        peer = dp_peer(k)
-        rows = psi_low_ref[pl.ds(pl.multiple_of(BLOCK * peer, BLOCK), BLOCK)]
-        data_send[peer] = dot(rows, cell_ref[...], 1, 0).astype(BF16)
-        data_copy(peer, d).start()
-
-    each(DP - 1, data_step)
-    data_own[...] = dot(
-        psi_low_ref[pl.ds(pl.multiple_of(BLOCK * d, BLOCK), BLOCK)], cell_ref[...], 1, 0
-    )
-
-    cross = dot(proj_low[...], cell_ref[...], 1, 1)
+    kernel_log = log_var_ref[0]
+    eye = lax.broadcasted_iota(jnp.int32, (LAT, LAT), 0) == lax.broadcasted_iota(
+        jnp.int32, (LAT, LAT), 1
+    )
+    length = jnp.sum(
+        jnp.where(eye, jnp.broadcast_to(length_ref[...], (LAT, LAT)), 0.0), axis=1, keepdims=True
+    )
+
+    def first_coefficients(cell_mean, inverse):
+        constant = kernel_log + 0.5 * jnp.sum(
+            jnp.log(length * inverse) - cell_mean * cell_mean * inverse, axis=0, keepdims=True
+        )
+        return cell_coefficients(
+            LOG2E * cell_mean * inverse, (-0.5 * LOG2E) * inverse, LOG2E * constant, 0
+        ).astype(BF16)
+
+    mean = mean_ref[...]
+    variance = jnp.exp(logvar_ref[...])
+    inverse = 1.0 / (length + variance)
+    features = point_features(inducing_ref[...], []).astype(BF16)
+    psi_one = jnp.exp2(dot(features, first_coefficients(mean, inverse), 0, 0))
+    psi_low_ref[...] = psi_one.astype(BF16)
+
+    cross = dot(proj_low[...], cell_all[0], 1, 1)
     product = psi_one * cross
     sum_0, sum_1, sum_2 = moments(dot(features, product.astype(BF16), 1, 0))
     beta = jnp.exp(jnp.full((1, CELLS), log_beta_ref[0], F32))
@@ -298,7 +317,7 @@
     quarter_inv = (-0.25 * LOG2E) / length
 
     def feature_step(i):
-        column = jnp.sum(jnp.where(lane == ROWS * g + i, base, 0.0), axis=1, keepdims=True)
+        column = jnp.sum(jnp.where(lane == ROWS * group + i, base, 0.0), axis=1, keepdims=True)
         for o in range(SPAN):
             at = lax.rem(d + o, DP)
             points = inducing_ref[:, pl.ds(pl.multiple_of(BLOCK * at, BLOCK), BLOCK)]
@@ -307,19 +326,24 @@
             block = point_features(0.5 * (points + column), split_three(pair))
             offset = pl.multiple_of(lax.rem(i, 2) * WIDTH + BLOCK * o, BLOCK)
             pair_feat[lax.div(i, 2), :, pl.ds(offset, BLOCK)] = block.astype(BF16)
+            columns = jnp.concatenate([block[0:96], block[192:224]], axis=0)
+            pair_cols[lax.div(i, 2), pl.ds(offset, BLOCK)] = columns.T.astype(BF16)
 
     each(ROWS, feature_step)
 
-    def coefficient_step(k):
-        at = dp_peer(k)
-
-        @pl.when(k < DP - 1)
-        def _():
-            latent_copy(at, at).wait_recv()
-
-        cell_mean = lat_all[at, 0:LAT]
-        cell_var = jnp.exp(lat_all[at, LAT : 2 * LAT])
-        inverse_w = 1.0 / (length + 2.0 * cell_var)
+    def pair_latent_copy():
+        return pair_copy(0, lat_all.at[core], lat_all.at[core])
+
+    def pair_latent_arrival():
+        return pair_copy(0, lat_all.at[core], lat_all.at[1 - core])
+
+    each(DP - 1, lambda k: latent_copy(dp_peer(k), dp_peer(k)).wait_recv())
+    pair_latent_copy().start()
+    pair_latent_arrival().wait_recv()
+
+    def coefficient_step(at):
+        cell_mean = lat_all[0, at]
+        inverse_w = 1.0 / (length + 2.0 * jnp.exp(lat_all[1, at]))
         inv_width[at] = inverse_w
         const = 2.0 * kernel_log + jnp.sum(
             0.5 * jnp.log(length * inverse_w) - cell_mean * cell_mean * inverse_w,
@@ -339,29 +363,30 @@
         weight_ref[i // 2, :, WIDTH * (i % 2) : WIDTH * (i % 2 + 1)] = jnp.broadcast_to(
             weight[i : i + 1], (8, WIDTH)
         )
-
     psi_acc[...] = jnp.zeros_like(psi_acc)
     trace_ref[...] = jnp.zeros_like(trace_ref)
 
     def grad_copy(peer, slot):
         return dp_copy(2, grad_send.at[peer], grad_recv.at[slot], peer, slot)
 
-    def cell_step(k):
-        at = dp_peer(k)
-        table = jnp.zeros((USED, CELLS), F32)
+    def cell_gradients(at):
+        table = jnp.zeros((CELLS, 128), F32)
         for s in range(STEPS):
             psi = jnp.exp2(dot(cell_coef[at], pair_feat[s], 1, 0))
             psi = psi.reshape(CELLS // 8, 8, PAIRS)
             psi_acc[s] += jnp.sum(psi, axis=0)
             weighted = (psi * weight_ref[s][None]).reshape(CELLS, PAIRS).astype(BF16)
-            table = table + dot(pair_feat[s, 0:USED], weighted, 1, 1)
-        mom_0, mom_1, mom_2 = moments(table)
-        cell_mean = lat_all[at, 0:LAT]
-        cell_var = jnp.exp(lat_all[at, LAT : 2 * LAT])
+            table = table + dot(weighted, pair_cols[s], 1, 0)
+        table = table.T
+        mom_0 = table[96:97]
+        mom_1 = table[0:32] + table[64:96]
+        mom_2 = table[32:64]
+        cell_mean = lat_all[0, at]
+        cell_var = jnp.exp(lat_all[1, at])
         inverse_w = inv_width[at]
         trace_ref[...] += mom_0
-        grad_send[at, 0:LAT] = -beta * inverse_w * (mom_1 - cell_mean * mom_0)
-        grad_send[at, LAT : 2 * LAT] = (
+        by_mean = -beta * inverse_w * (mom_1 - cell_mean * mom_0)
+        by_logvar = (
             -beta
             * cell_var
             * inverse_w
@@ -370,12 +395,56 @@
                 - 0.5 * mom_0
             )
         )
-
-        @pl.when(k < DP - 1)
-        def _():
-            grad_copy(at, d).start()
-
-    each(DP, cell_step)
+        return by_mean, by_logvar
+
+    def cell_step(k):
+        at = cell_order(k)
+        by_mean, by_logvar = cell_gradients(at)
+        grad_send[at, 0:LAT] = by_mean.astype(BF16)
+        grad_send[at, LAT : 2 * LAT] = by_logvar.astype(BF16)
+        grad_copy(at, d).start()
+
+    each(SPLIT, cell_step)
+
+    def data_copy(peer, slot):
+        return dp_copy(
+            1,
+            data_send.at[lax.rem(peer, DP_Z)],
+            data_recv.at[lax.rem(slot, DP_Z)],
+            peer,
+            slot,
+        )
+
+    dp_copy(3, cell_all.at[0], cell_all.at[1], across, 7).wait_recv()
+    side_points = inducing_ref[:, pl.ds(pl.multiple_of(BLOCK * side, BLOCK), BLOCK * DP_Z)]
+    across_mean = lat_all[0, across]
+    across_inverse = 1.0 / (length + jnp.exp(lat_all[1, across]))
+    psi_across = jnp.exp2(
+        dot(
+            point_features(side_points, []).astype(BF16),
+            first_coefficients(across_mean, across_inverse),
+            0,
+            0,
+        )
+    )
+    psi_side[...] = psi_across.astype(BF16)
+
+    def data_rows(at):
+        near = psi_low_ref[pl.ds(pl.multiple_of(BLOCK * (side + at), BLOCK), BLOCK)]
+        far = psi_side[pl.ds(pl.multiple_of(BLOCK * at, BLOCK), BLOCK)]
+        return dot(near, cell_all[0], 1, 0) + dot(far, cell_all[1], 1, 0)
+
+    def data_step(k):
+        at = lax.rem(z + 1 + k, DP_Z)
+        data_send[at] = data_rows(at).astype(BF16)
+        data_copy(z_peer(k), d).start()
+
+    each(DP_Z - 1, data_step)
+
+    each(DP - 1 - SPLIT, lambda k: cell_step(k + SPLIT))
+    by_mean, by_logvar = cell_gradients(d)
+    first_ref[0:LAT] += by_mean
+    first_ref[LAT : 2 * LAT] += by_logvar
 
     total_row = sum_0 - 0.5 * trace_ref[...]
     total_row = total_row[:, 0:128] + total_row[:, 128:256]
@@ -383,26 +452,40 @@
     total_tile = jnp.where(first_row, jnp.broadcast_to(total_row, (8, 128)), 0.0) - (
         0.5 * square_tile
     )
-    for i in range(ROWS):
-        row = jnp.sum(
-            psi_acc[i // 2, :, WIDTH * (i % 2) : WIDTH * (i % 2 + 1)], axis=0, keepdims=True
-        )
-        psi_send[i : i + 1, 0:WIDTH] = row
-    psi_send[:, WIDTH : WIDTH + 128] = total_tile
-
-    def psi_copy(peer, slot):
-        return gene_copy(1, psi_send, psi_recv.at[slot], peer, slot)
-
-    each(GENE - 1, lambda k: psi_copy(gene_peer(k), g).start())
-    psi_recv[g] = psi_send[...]
-
+    rows = jnp.concatenate(
+        [
+            jnp.sum(
+                psi_acc[i // 2, :, WIDTH * (i % 2) : WIDTH * (i % 2 + 1)], axis=0, keepdims=True
+            )
+            for i in range(ROWS)
+        ],
+        axis=0,
+    )
+    wide = jnp.concatenate([rows, jnp.zeros((ROWS, 128), F32)], axis=1)
+    psi_all[core, place] = jnp.concatenate([wide[:, 0:HALF], wide[:, HALF:]], axis=0).astype(BF16)
+
+    def psi_copy(chip, slot):
+        return remote(
+            psi_all.at[core, place],
+            psi_all.at[core, slot],
+            "gene",
+            gene_sems.at[1, 0, chip],
+            gene_sems.at[1, 1, slot],
+            2 * chip + core,
+        )
+
+    each(GENE // 2 - 1, lambda k: psi_copy(chip_peer(k), place).start())
+
+    grad_recv[d] = jnp.zeros((2 * LAT, CELLS), BF16)
     each(DP - 1, lambda k: grad_copy(dp_peer(k), dp_peer(k)).wait_recv())
-    grad_recv[d] = grad_send[d]
-    own_grad = first_ref[...] + jnp.sum(grad_recv[...], axis=0)
+    own_grad = first_ref[...]
+    for p in range(DP):
+        own_grad = own_grad + grad_recv[p].astype(F32)
     for p in range(GENE):
-        part_send[p] = own_grad[
+        part_send[p, 0:8] = own_grad[
             8 * (p // 2) : 8 * (p // 2 + 1), 128 * (p % 2) : 128 * (p % 2 + 1)
         ]
+        part_send[p, 8:16] = total_tile
 
     def part_copy(peer, slot):
         return gene_copy(2, part_send.at[peer], part_recv.at[slot], peer, slot)
@@ -410,56 +493,67 @@
     each(GENE - 1, lambda k: part_copy(gene_peer(k), g).start())
     part_recv[g] = part_send[g]
 
-    each(GENE - 1, lambda k: psi_copy(gene_peer(k), gene_peer(k)).wait_recv())
-    total_recv[d] = jnp.sum(psi_recv[:, :, WIDTH : WIDTH + 128], axis=0)
+    def pair_psi_copy():
+        return pair_copy(1, psi_all.at[core], psi_all.at[core])
+
+    def pair_psi_arrival():
+        return pair_copy(1, psi_all.at[core], psi_all.at[1 - core])
+
+    each(GENE // 2 - 1, lambda k: psi_copy(chip_peer(k), chip_peer(k)).wait_recv())
+    pair_psi_copy().start()
+
+    data_own[...] = data_rows(z)
+
+    pair_psi_arrival().wait_recv()
+    gathered = psi_all[...].astype(F32).reshape(GENE, 2 * ROWS, HALF)
+    left = gathered[:, 0:ROWS].reshape(BLOCK, HALF)
+    right = gathered[:, ROWS : 2 * ROWS].reshape(BLOCK, HALF)
     psi_rows = [
-        psi_recv[:, :, BLOCK * o : BLOCK * (o + 1)].reshape(BLOCK, BLOCK).astype(BF16)
+        (left if o < 3 else right)[:, BLOCK * (o % 3) : BLOCK * (o % 3 + 1)].astype(BF16)
         for o in range(SPAN)
     ]
     for o in range(1, 4):
         block_send[o - 1] = psi_rows[o]
 
     def block_copy(o, slot):
-        return dp_copy(
-            3, block_send.at[o - 1], block_recv.at[slot], lax.rem(d + o, DP), slot
-        )
+        return dp_copy(3, block_send.at[o - 1], block_recv.at[slot], lax.rem(d + o, DP), slot)
+
+    for o in range(1, 4):
+        block_copy(o, o - 1).start()
+
+    each(GENE - 1, lambda k: part_copy(gene_peer(k), gene_peer(k)).wait_recv())
+    part_sum = jnp.sum(part_recv[...], axis=0)
+    sum_all[g] = part_sum[0:8]
+    total_recv[d] = part_sum[8:16]
+
+    def sum_copy(peer, slot):
+        return gene_copy(3, sum_all.at[g], sum_all.at[slot], peer, slot)
 
     def total_copy(peer, slot):
         return dp_copy(4, total_recv.at[d], total_recv.at[slot], peer, slot)
 
-    for o in range(1, 4):
-        block_copy(o, o - 1).start()
+    each(GENE - 1, lambda k: sum_copy(gene_peer(k), g).start())
     each(DP - 1, lambda k: total_copy(dp_peer(k), d).start())
 
-    each(GENE - 1, lambda k: part_copy(gene_peer(k), gene_peer(k)).wait_recv())
-    sum_all[g] = jnp.sum(part_recv[...], axis=0)
-
-    def sum_copy(peer, slot):
-        return gene_copy(3, sum_all.at[g], sum_all.at[slot], peer, slot)
-
-    each(GENE - 1, lambda k: sum_copy(gene_peer(k), g).start())
-
-    stat = jnp.zeros((BLOCK, GENES), F32)
+    stat = data_own[...]
     for o in range(SPAN):
         at = lax.rem(d + o, DP)
-        stat = stat + dot(
+        stat = stat - dot(
             psi_rows[o], proj_low[pl.ds(pl.multiple_of(BLOCK * at, BLOCK), BLOCK)], 1, 0
         )
-    each(DP - 1, lambda k: data_copy(dp_peer(k), dp_peer(k)).wait_recv())
-    data_recv[d] = jnp.zeros((BLOCK, GENES), BF16)
-    data = data_own[...]
-    for p in range(DP):
-        data = data + data_recv[p].astype(F32)
+    each(DP_Z - 1, lambda k: data_copy(z_peer(k), z_peer(k)).wait_recv())
+    for k in range(DP_Z - 1):
+        stat = stat + data_recv[lax.rem(z + 1 + k, DP_Z)].astype(F32)
     for o in range(1, 4):
         block_copy(o, o - 1).wait_recv()
         at = lax.rem(d + (DP - o), DP)
-        stat = stat + dot(
+        stat = stat - dot(
             block_recv[o - 1],
             proj_low[pl.ds(pl.multiple_of(BLOCK * at, BLOCK), BLOCK)],
             0,
             0,
         )
-    proj_out[...] = data - stat
+    proj_out[...] = stat
 
     each(GENE - 1, lambda k: sum_copy(gene_peer(k), gene_peer(k)).wait_recv())
     for p in range(GENE):
@@ -470,21 +564,50 @@
     def sent_dp(k):
         peer = dp_peer(k)
         latent_copy(peer, d).wait_send()
-        data_copy(peer, d).wait_send()
         grad_copy(peer, d).wait_send()
         total_copy(peer, d).wait_send()
 
     def sent_gene(k):
         peer = gene_peer(k)
         gram_copy(peer, g).wait_send()
-        psi_copy(peer, g).wait_send()
         part_copy(peer, g).wait_send()
         sum_copy(peer, g).wait_send()
 
     each(DP - 1, sent_dp)
+    each(DP_Z - 1, lambda k: data_copy(z_peer(k), d).wait_send())
     each(GENE - 1, sent_gene)
+    each(GENE // 2 - 1, lambda k: psi_copy(chip_peer(k), place).wait_send())
     for o in range(1, 4):
         block_copy(o, o - 1).wait_send()
+    cell_copy().wait_send()
+    pair_latent_copy().wait_send()
+    pair_psi_copy().wait_send()
+
+
+def finish(
+    latent_ref,
+    proj_ref,
+    total_ref,
+    mean_ref,
+    logvar_ref,
+    log_var_ref,
+    log_beta_ref,
+    latent_out,
+    proj_out,
+    scalar_out,
+):
+    beta = jnp.exp(jnp.full((8, 128), log_beta_ref[0], F32))
+    amplitude = jnp.exp(jnp.full((8, 128), log_var_ref[0], F32))
+    proj_out[...] = proj_ref[...] * (beta[0:1, 0:1] / (CELLS * DP))
+
+    @pl.when(pl.program_id(0) == 0)
+    def _():
+        latent_out[0] = latent_ref[0:LAT] - mean_ref[...]
+        latent_out[1] = latent_ref[LAT : 2 * LAT] - 0.5 * (jnp.exp(logvar_ref[...]) - 1.0)
+        entries = CELLS * DP * GENES * GENE
+        scalar_out[0] = jnp.sum(
+            beta * total_ref[...] / entries - (0.5 / 1024) * beta * amplitude + 0.5 / 1024
+        )
 
 
 def on_device(
@@ -506,27 +629,28 @@
         pltpu.VMEM((IND, GENES), F32),
         pltpu.VMEM((IND, GENES), BF16),
         pltpu.VMEM((IND, GENES), BF16),
-        pltpu.VMEM((CELLS, GENES), BF16),
+        pltpu.VMEM((2, CELLS, GENES), BF16),
         pltpu.VMEM((IND, CELLS), BF16),
-        pltpu.VMEM((DP, 2 * LAT, CELLS), F32),
+        pltpu.VMEM((DP_Z * BLOCK, CELLS), BF16),
+        pltpu.VMEM((2, DP, LAT, CELLS), F32),
         pltpu.VMEM((GENE, ROWS, WIDTH), F32),
         pltpu.VMEM((GENE, ROWS, WIDTH), F32),
-        pltpu.VMEM((DP, BLOCK, GENES), BF16),
-        pltpu.VMEM((DP, BLOCK, GENES), BF16),
+        pltpu.VMEM((DP_Z, BLOCK, GENES), BF16),
+        pltpu.VMEM((DP_Z, BLOCK, GENES), BF16),
         pltpu.VMEM((BLOCK, GENES), F32),
         pltpu.VMEM((STEPS, DEPTH, PAIRS), BF16),
+        pltpu.VMEM((STEPS, PAIRS, 128), BF16),
         pltpu.VMEM((DP, CELLS, DEPTH), BF16),
         pltpu.VMEM((DP, LAT, CELLS), F32),
         pltpu.VMEM((STEPS, 8, PAIRS), F32),
         pltpu.VMEM((STEPS, 8, PAIRS), F32),
         pltpu.VMEM((2 * LAT, CELLS), F32),
         pltpu.VMEM((1, CELLS), F32),
-        pltpu.VMEM((DP, 2 * LAT, CELLS), F32),
-        pltpu.VMEM((DP, 2 * LAT, CELLS), F32),
-        pltpu.VMEM((ROWS, WIDTH + 128), F32),
-        pltpu.VMEM((GENE, ROWS, WIDTH + 128), F32),
-        pltpu.VMEM((GENE, 8, 128), F32),
-        pltpu.VMEM((GENE, 8, 128), F32),
+        pltpu.VMEM((DP, 2 * LAT, CELLS), BF16),
+        pltpu.VMEM((DP, 2 * LAT, CELLS), BF16),
+        pltpu.VMEM((2, GENE // 2, 2 * ROWS, HALF), BF16),
+        pltpu.VMEM((GENE, 16, 128), F32),
+        pltpu.VMEM((GENE, 16, 128), F32),
         pltpu.VMEM((GENE, 8, 128), F32),
         pltpu.VMEM((3, BLOCK, BLOCK), BF16),
         pltpu.VMEM((3, BLOCK, BLOCK), BF16),
@@ -534,6 +658,7 @@
         pltpu.SemaphoreType.DMA((5,)),
         pltpu.SemaphoreType.DMA((5, 2, DP)),
         pltpu.SemaphoreType.DMA((4, 2, GENE)),
+        pltpu.SemaphoreType.DMA((2, 2)),
     ]
     latent, proj, total = pl.pallas_call(
         kernel,
@@ -561,20 +686,32 @@
         proj_mean,
         second_moment,
     )
-    noise_prec = jnp.exp(log_beta[0])
-    batch_size = CELLS * DP
-    gene_count = GENES * GENE
-    variance = jnp.exp(latent_logvar)
-    grad_latent = latent.reshape(2, LAT, CELLS) + jnp.stack(
-        [-latent_mean, -0.5 * (variance - 1.0)]
-    )
-    grad_proj = (noise_prec / batch_size) * proj
-    grad_logbeta = (
-        noise_prec / (batch_size * gene_count) * jnp.sum(total)
-        - 0.5 * noise_prec * jnp.exp(log_var[0])
-        + 0.5
-    )
-    return (grad_latent, grad_proj, grad_logbeta.reshape(1))
+    steps = 4
+    grad_latent, grad_proj, grad_logbeta = pl.pallas_call(
+        finish,
+        grid=(steps,),
+        out_shape=(
+            jax.ShapeDtypeStruct((2, LAT, CELLS), F32),
+            jax.ShapeDtypeStruct((BLOCK, GENES), F32),
+            jax.ShapeDtypeStruct((1,), F32),
+        ),
+        in_specs=[
+            pl.BlockSpec((2 * LAT, CELLS), lambda i: (0, 0)),
+            pl.BlockSpec((BLOCK // steps, GENES), lambda i: (i, 0)),
+            pl.BlockSpec((8, 128), lambda i: (0, 0)),
+            pl.BlockSpec((LAT, CELLS), lambda i: (0, 0)),
+            pl.BlockSpec((LAT, CELLS), lambda i: (0, 0)),
+            smem,
+            smem,
+        ],
+        out_specs=(
+            pl.BlockSpec((2, LAT, CELLS), lambda i: (0, 0, 0)),
+            pl.BlockSpec((BLOCK // steps, GENES), lambda i: (i, 0)),
+            smem,
+        ),
+        name="finish",
+    )(latent, proj, total, latent_mean, latent_logvar, log_var, log_beta)
+    return (grad_latent, grad_proj, grad_logbeta)
 
 
 def solution(mesh):

time: 79 us -> 63.8 us (0.81)
  Pallas kernels: 69.4 us -> 61.7 us
  other arithmetic: 5.44 us -> 0 us
  between operations: 3.8 us -> 1.93 us
    pallas_call x1, Pallas kernels: 69.4 us -> 58.3 us  [on_device(): pl.pallas_call(kernel, out_shape=(jax.ShapeDtypeStruct((2 * LAT, CELLS),...]
    pallas_call x0 -> x1, Pallas kernels: none -> 3.37 us  [on_device(): pl.pallas_call(finish, grid=(steps,), out_shape=(jax.ShapeDtypeStruct((2,...]
    mul x1 -> x0, other arithmetic: 1.88 us -> none  [on_device(): grad_proj = noise_prec / batch_size * proj]
    add x1 -> x0, other arithmetic: 1.48 us -> none  [on_device(): latent.reshape(2, LAT, CELLS)]
    reduce_sum x1 -> x0, other arithmetic: 1.29 us -> none  [on_device(): jnp.sum(total)]
    another operation x1 -> x0, other arithmetic: 0.79 us -> none  [on_device(): jnp.stack([-latent_mean, -0.5 * (variance - 1.0)])]
where the time goes in v2:
time: 63.8 us; the launch traced here: 63.6 us
  Pallas kernels  61.7 us (97%)
  between operations  1.93 us (3%)
    pallas_call x1, Pallas kernels, on_device(): pl.pallas_call(kernel, out_shape=(jax.ShapeDtypeStruct((2 * LAT, CELLS),...  58.3 us
    pallas_call x1, Pallas kernels, on_device(): pl.pallas_call(finish, grid=(steps,), out_shape=(jax.ShapeDtypeStruct((2,...  3.37 us

profile of v2, /device:TPU:1, one launch (start us, length us, event | category | flops | bytes accessed | tf_op | source)
XLA Modules:
  0.0 63.6 jit_solution(5146235052069939470)
XLA Ops:
  1.9 58.3 %bound_gradients.1 = (f32[64,256]{1,0:T(8,128)}, f32[128,1024]{1,0:T(8,128)}, f32[8,128]{1,0:T(8,128)}) custom-call(bf16[1024,1024]{1,0:T(8,128)(2,1)} %y_hbm.1, s32[1,256]{1,0:T(1,128)} %bitcast.2, f32[32,256]{1,0:T(8,128)} %mean_ref.3, f32[32,256]{1,0:T(8,128)} %logvar_ref.3, f32[32,1024]{1,0:T(8,128)} %inducing_ref.1, f32[1,32]{1,0:T(1,128)} %bitcast.3, ...), custom_call_target="tpu_custom_call" | custom-call | tf_op jit(solution)/shard_map/bound_gradients/pallas_call | solution.py:663
  60.2 3.4 %finish.1 = (f32[2,32,256]{2,1,0:T(8,128)}, f32[128,1024]{1,0:T(8,128)}, f32[1]{0:T(128)}) custom-call(f32[64,256]{1,0:T(8,128)} %get-tuple-element.6.latent_ref, f32[128,1024]{1,0:T(8,128)} %get-tuple-element.7.proj_ref, f32[8,128]{1,0:T(8,128)} %get-tuple-element.8.total_ref, f32[32,256]{1,0:T(8,128)} %mean_ref.3, f32[32,256]{1,0:T(8,128)} %logvar_ref.3, ...), custom_call_target="tpu_custom_call" | custom-call | tf_op jit(solution)/shard_map/finish/pallas_call | solution.py:690

commit v3 on v2

--- a/solution.py
+++ b/solution.py
@@ -28,6 +28,23 @@
 DEPTH = 256
 HALF = 384
 SPLIT = 4
+(
+    ACROSS,
+    LATENT,
+    PAIR_LATENT,
+    PAIR_GRAM,
+    GRAM,
+    CELL,
+    GRAD,
+    DATA,
+    PSI,
+    PAIR_PSI,
+    PART,
+    TURNED,
+    SUM,
+    TOTAL,
+    KINDS,
+) = range(15)
 BLOCK_WEIGHT = (1.0, 2.0, 2.0, 2.0, 1.0)
 
 
@@ -112,6 +129,8 @@
     psi_side,
     lat_all,
     gram_send,
+    gram_pair,
+    gram_out,
     gram_recv,
     data_send,
     data_recv,
@@ -134,14 +153,14 @@
     block_recv,
     total_recv,
     local_sem,
-    dp_sems,
-    gene_sems,
-    pair_sems,
+    sems,
 ):
     d = lax.axis_index("dp")
     g = lax.axis_index("gene")
     z = lax.rem(d, DP_Z)
+    half = lax.div(d, DP_Z)
     side = d - z
+    across = lax.rem(d + DP_Z, DP)
     core = lax.rem(g, 2)
     place = lax.div(g, 2)
     group = GENE // 2 * core + place
@@ -172,16 +191,17 @@
     def cell_order(k):
         return lax.rem(side + DP_Z * (1 - lax.div(k, DP_Z)), DP) + lax.rem(z + 1 + k, DP_Z)
 
-    def dp_copy(kind, src, dst, peer, slot):
-        return remote(src, dst, "dp", dp_sems.at[kind, 0, peer], dp_sems.at[kind, 1, slot], peer)
-
-    def gene_copy(kind, src, dst, peer, slot):
-        return remote(
-            src, dst, "gene", gene_sems.at[kind, 0, peer], gene_sems.at[kind, 1, slot], peer
-        )
+    def dp_copy(kind, src, dst, peer):
+        return remote(src, dst, "dp", sems.at[kind, 0], sems.at[kind, 1], peer)
+
+    def gene_copy(kind, src, dst, peer):
+        return remote(src, dst, "gene", sems.at[kind, 0], sems.at[kind, 1], peer)
 
     def pair_copy(kind, src, dst):
-        return remote(src, dst, "gene", pair_sems.at[kind, 0], pair_sems.at[kind, 1], sibling)
+        return gene_copy(kind, src, dst, sibling)
+
+    def wait_all(kind, side_of, buffer):
+        pltpu.make_async_copy(buffer, buffer, sems.at[kind, side_of]).wait()
 
     quarter = IND // 4
     proj_copies = [
@@ -210,13 +230,14 @@
             barrier, inc=1, device_id={"gene": gene_peer(k)}, device_id_type=MESH
         ),
     )
-    lat_all[core, d] = jnp.where(core == 0, mean_ref[...], logvar_ref[...])
+    lat_all[core, z, half] = jnp.where(core == 0, mean_ref[...], logvar_ref[...])
     pl.semaphore_wait(barrier, DP + GENE - 2)
 
-    def latent_copy(peer, slot):
-        return dp_copy(0, lat_all.at[core, d], lat_all.at[core, slot], peer, slot)
-
-    each(DP - 1, lambda k: latent_copy(dp_peer(k), d).start())
+    def latent_across():
+        mine = lat_all.at[core, z, half]
+        return dp_copy(ACROSS, mine, mine, across)
+
+    latent_across().start()
 
     for k in range(4):
         proj_copies[k].wait()
@@ -241,14 +262,18 @@
         block = BLOCK_WEIGHT[o] * (gram + 0.5 * moment_part)
         gram_send[:, :, BLOCK * o : BLOCK * (o + 1)] = block.reshape(GENE, ROWS, BLOCK)
 
-    def group_of(device):
-        return GENE // 2 * lax.rem(device, 2) + lax.div(device, 2)
-
-    def gram_copy(peer, slot):
-        return gene_copy(0, gram_send.at[group_of(peer)], gram_recv.at[slot], peer, slot)
-
-    each(GENE - 1, lambda k: gram_copy(gene_peer(k), g).start())
-    gram_recv[g] = gram_send[group]
+    chips = GENE // 2
+
+    def pair_gram_copy():
+        return pair_copy(PAIR_GRAM, gram_send.at[pl.ds(chips * (1 - core), chips)], gram_pair)
+
+    pair_gram_copy().start()
+
+    latent_across().wait_recv()
+    each(
+        DP_Z - 1,
+        lambda k: dp_copy(LATENT, lat_all.at[core, z], lat_all.at[core, z], z_peer(k)).start(),
+    )
 
     eye_cells = lax.broadcasted_iota(jnp.int32, (CELLS, CELLS), 0) == lax.broadcasted_iota(
         jnp.int32, (CELLS, CELLS), 1
@@ -264,10 +289,23 @@
     y_copy.wait()
     cell_rows = dot(one_hot, y_ref[...], 1, 0)
     cell_all[0] = cell_rows.astype(BF16)
-    across = lax.rem(d + DP_Z, DP)
+
+    pair_gram_copy().wait_recv()
+    gram_sum = gram_send[pl.ds(chips * core, chips)] + gram_pair[...]
+    gram_sum = jnp.concatenate([gram_sum, jnp.zeros((chips, ROWS, 128), F32)], axis=2)
+    gram_out[...] = jnp.concatenate(
+        [gram_sum[:, :, 0:HALF], gram_sum[:, :, HALF:]], axis=1
+    ).astype(BF16)
+
+    def gram_step(k):
+        chip = chip_peer(k)
+        gene_copy(GRAM, gram_out.at[chip], gram_recv.at[place], 2 * chip + core).start()
+
+    each(chips - 1, gram_step)
+    gram_recv[place] = gram_out[place]
 
     def cell_copy():
-        return dp_copy(3, cell_all.at[0], cell_all.at[1], across, 7)
+        return dp_copy(CELL, cell_all.at[0], cell_all.at[1], across)
 
     cell_copy().start()
     squares = jnp.sum((cell_rows * cell_rows).reshape(CELLS // 8, 8, GENES), axis=0)
@@ -331,19 +369,19 @@
 
     each(ROWS, feature_step)
 
+    def latents(kind, at):
+        return lat_all[kind, lax.rem(at, DP_Z), lax.div(at, DP_Z)]
+
     def pair_latent_copy():
-        return pair_copy(0, lat_all.at[core], lat_all.at[core])
-
-    def pair_latent_arrival():
-        return pair_copy(0, lat_all.at[core], lat_all.at[1 - core])
-
-    each(DP - 1, lambda k: latent_copy(dp_peer(k), dp_peer(k)).wait_recv())
+        return pair_copy(PAIR_LATENT, lat_all.at[core], lat_all.at[core])
+
+    wait_all(LATENT, 1, lat_all.at[core, pl.ds(0, DP_Z - 1)])
     pair_latent_copy().start()
-    pair_latent_arrival().wait_recv()
+    pair_latent_copy().wait_recv()
 
     def coefficient_step(at):
-        cell_mean = lat_all[0, at]
-        inverse_w = 1.0 / (length + 2.0 * jnp.exp(lat_all[1, at]))
+        cell_mean = latents(0, at)
+        inverse_w = 1.0 / (length + 2.0 * jnp.exp(latents(1, at)))
         inv_width[at] = inverse_w
         const = 2.0 * kernel_log + jnp.sum(
             0.5 * jnp.log(length * inverse_w) - cell_mean * cell_mean * inverse_w,
@@ -357,17 +395,15 @@
 
     each(DP, coefficient_step)
 
-    each(GENE - 1, lambda k: gram_copy(gene_peer(k), gene_peer(k)).wait_recv())
-    weight = jnp.sum(gram_recv[...], axis=0)
+    wait_all(GRAM, 1, gram_recv.at[pl.ds(0, chips - 1)])
+    weight = jnp.sum(gram_recv[...].astype(F32), axis=0)
+    weight = jnp.concatenate([weight[0:ROWS], weight[ROWS:, 0 : WIDTH - HALF]], axis=1)
     for i in range(ROWS):
         weight_ref[i // 2, :, WIDTH * (i % 2) : WIDTH * (i % 2 + 1)] = jnp.broadcast_to(
             weight[i : i + 1], (8, WIDTH)
         )
     psi_acc[...] = jnp.zeros_like(psi_acc)
     trace_ref[...] = jnp.zeros_like(trace_ref)
-
-    def grad_copy(peer, slot):
-        return dp_copy(2, grad_send.at[peer], grad_recv.at[slot], peer, slot)
 
     def cell_gradients(at):
         table = jnp.zeros((CELLS, 128), F32)
@@ -381,8 +417,8 @@
         mom_0 = table[96:97]
         mom_1 = table[0:32] + table[64:96]
         mom_2 = table[32:64]
-        cell_mean = lat_all[0, at]
-        cell_var = jnp.exp(lat_all[1, at])
+        cell_mean = latents(0, at)
+        cell_var = jnp.exp(latents(1, at))
         inverse_w = inv_width[at]
         trace_ref[...] += mom_0
         by_mean = -beta * inverse_w * (mom_1 - cell_mean * mom_0)
@@ -402,23 +438,14 @@
         by_mean, by_logvar = cell_gradients(at)
         grad_send[at, 0:LAT] = by_mean.astype(BF16)
         grad_send[at, LAT : 2 * LAT] = by_logvar.astype(BF16)
-        grad_copy(at, d).start()
+        dp_copy(GRAD, grad_send.at[at], grad_recv.at[d], at).start()
 
     each(SPLIT, cell_step)
 
-    def data_copy(peer, slot):
-        return dp_copy(
-            1,
-            data_send.at[lax.rem(peer, DP_Z)],
-            data_recv.at[lax.rem(slot, DP_Z)],
-            peer,
-            slot,
-        )
-
-    dp_copy(3, cell_all.at[0], cell_all.at[1], across, 7).wait_recv()
+    cell_copy().wait_recv()
     side_points = inducing_ref[:, pl.ds(pl.multiple_of(BLOCK * side, BLOCK), BLOCK * DP_Z)]
-    across_mean = lat_all[0, across]
-    across_inverse = 1.0 / (length + jnp.exp(lat_all[1, across]))
+    across_mean = latents(0, across)
+    across_inverse = 1.0 / (length + jnp.exp(latents(1, across)))
     psi_across = jnp.exp2(
         dot(
             point_features(side_points, []).astype(BF16),
@@ -437,11 +464,12 @@
     def data_step(k):
         at = lax.rem(z + 1 + k, DP_Z)
         data_send[at] = data_rows(at).astype(BF16)
-        data_copy(z_peer(k), d).start()
-
-    each(DP_Z - 1, data_step)
-
+        dp_copy(DATA, data_send.at[at], data_recv.at[z], z_peer(k)).start()
+
+    data_step(1)
     each(DP - 1 - SPLIT, lambda k: cell_step(k + SPLIT))
+    data_step(0)
+    data_step(2)
     by_mean, by_logvar = cell_gradients(d)
     first_ref[0:LAT] += by_mean
     first_ref[LAT : 2 * LAT] += by_logvar
@@ -464,20 +492,14 @@
     wide = jnp.concatenate([rows, jnp.zeros((ROWS, 128), F32)], axis=1)
     psi_all[core, place] = jnp.concatenate([wide[:, 0:HALF], wide[:, HALF:]], axis=0).astype(BF16)
 
-    def psi_copy(chip, slot):
-        return remote(
-            psi_all.at[core, place],
-            psi_all.at[core, slot],
-            "gene",
-            gene_sems.at[1, 0, chip],
-            gene_sems.at[1, 1, slot],
-            2 * chip + core,
-        )
-
-    each(GENE // 2 - 1, lambda k: psi_copy(chip_peer(k), place).start())
+    own_psi = psi_all.at[core, place]
+    each(
+        chips - 1,
+        lambda k: gene_copy(PSI, own_psi, own_psi, 2 * chip_peer(k) + core).start(),
+    )
 
     grad_recv[d] = jnp.zeros((2 * LAT, CELLS), BF16)
-    each(DP - 1, lambda k: grad_copy(dp_peer(k), dp_peer(k)).wait_recv())
+    wait_all(GRAD, 1, grad_recv.at[pl.ds(0, DP - 1)])
     own_grad = first_ref[...]
     for p in range(DP):
         own_grad = own_grad + grad_recv[p].astype(F32)
@@ -487,24 +509,22 @@
         ]
         part_send[p, 8:16] = total_tile
 
-    def part_copy(peer, slot):
-        return gene_copy(2, part_send.at[peer], part_recv.at[slot], peer, slot)
-
-    each(GENE - 1, lambda k: part_copy(gene_peer(k), g).start())
+    def part_step(k):
+        peer = gene_peer(k)
+        gene_copy(PART, part_send.at[peer], part_recv.at[g], peer).start()
+
+    each(GENE - 1, part_step)
     part_recv[g] = part_send[g]
 
     def pair_psi_copy():
-        return pair_copy(1, psi_all.at[core], psi_all.at[core])
-
-    def pair_psi_arrival():
-        return pair_copy(1, psi_all.at[core], psi_all.at[1 - core])
-
-    each(GENE // 2 - 1, lambda k: psi_copy(chip_peer(k), chip_peer(k)).wait_recv())
+        return pair_copy(PAIR_PSI, psi_all.at[core], psi_all.at[core])
+
+    wait_all(PSI, 1, psi_all.at[core, pl.ds(0, chips - 1)])
     pair_psi_copy().start()
 
     data_own[...] = data_rows(z)
 
-    pair_psi_arrival().wait_recv()
+    pair_psi_copy().wait_recv()
     gathered = psi_all[...].astype(F32).reshape(GENE, 2 * ROWS, HALF)
     left = gathered[:, 0:ROWS].reshape(BLOCK, HALF)
     right = gathered[:, ROWS : 2 * ROWS].reshape(BLOCK, HALF)
@@ -515,25 +535,20 @@
     for o in range(1, 4):
         block_send[o - 1] = psi_rows[o]
 
-    def block_copy(o, slot):
-        return dp_copy(3, block_send.at[o - 1], block_recv.at[slot], lax.rem(d + o, DP), slot)
-
     for o in range(1, 4):
-        block_copy(o, o - 1).start()
-
-    each(GENE - 1, lambda k: part_copy(gene_peer(k), gene_peer(k)).wait_recv())
+        dp_copy(
+            TURNED, block_send.at[o - 1], block_recv.at[o - 1], lax.rem(d + o, DP)
+        ).start()
+
+    wait_all(PART, 1, part_recv.at[pl.ds(0, GENE - 1)])
     part_sum = jnp.sum(part_recv[...], axis=0)
     sum_all[g] = part_sum[0:8]
     total_recv[d] = part_sum[8:16]
 
-    def sum_copy(peer, slot):
-        return gene_copy(3, sum_all.at[g], sum_all.at[slot], peer, slot)
-
-    def total_copy(peer, slot):
-        return dp_copy(4, total_recv.at[d], total_recv.at[slot], peer, slot)
-
-    each(GENE - 1, lambda k: sum_copy(gene_peer(k), g).start())
-    each(DP - 1, lambda k: total_copy(dp_peer(k), d).start())
+    own_sum = sum_all.at[g]
+    own_total = total_recv.at[d]
+    each(GENE - 1, lambda k: gene_copy(SUM, own_sum, own_sum, gene_peer(k)).start())
+    each(DP - 1, lambda k: dp_copy(TOTAL, own_total, own_total, dp_peer(k)).start())
 
     stat = data_own[...]
     for o in range(SPAN):
@@ -541,11 +556,11 @@
         stat = stat - dot(
             psi_rows[o], proj_low[pl.ds(pl.multiple_of(BLOCK * at, BLOCK), BLOCK)], 1, 0
         )
-    each(DP_Z - 1, lambda k: data_copy(z_peer(k), z_peer(k)).wait_recv())
+    wait_all(DATA, 1, data_recv.at[pl.ds(0, DP_Z - 1)])
     for k in range(DP_Z - 1):
         stat = stat + data_recv[lax.rem(z + 1 + k, DP_Z)].astype(F32)
+    wait_all(TURNED, 1, block_recv)
     for o in range(1, 4):
-        block_copy(o, o - 1).wait_recv()
         at = lax.rem(d + (DP - o), DP)
         stat = stat - dot(
             block_recv[o - 1],
@@ -553,61 +568,39 @@
             0,
             0,
         )
-    proj_out[...] = stat
-
-    each(GENE - 1, lambda k: sum_copy(gene_peer(k), gene_peer(k)).wait_recv())
+    data_own[...] = stat * (beta[0:1, 0:1] / (CELLS * DP))
+    proj_copy = pltpu.make_async_copy(data_own, proj_out, local_sem.at[0])
+    proj_copy.start()
+
+    wait_all(SUM, 1, sum_all.at[pl.ds(0, GENE - 1)])
     for p in range(GENE):
-        latent_out[8 * (p // 2) : 8 * (p // 2 + 1), 128 * (p % 2) : 128 * (p % 2 + 1)] = sum_all[p]
-    each(DP - 1, lambda k: total_copy(dp_peer(k), dp_peer(k)).wait_recv())
-    total_out[...] = jnp.sum(total_recv[...], axis=0)
-
-    def sent_dp(k):
-        peer = dp_peer(k)
-        latent_copy(peer, d).wait_send()
-        grad_copy(peer, d).wait_send()
-        total_copy(peer, d).wait_send()
-
-    def sent_gene(k):
-        peer = gene_peer(k)
-        gram_copy(peer, g).wait_send()
-        part_copy(peer, g).wait_send()
-        sum_copy(peer, g).wait_send()
-
-    each(DP - 1, sent_dp)
-    each(DP_Z - 1, lambda k: data_copy(z_peer(k), d).wait_send())
-    each(GENE - 1, sent_gene)
-    each(GENE // 2 - 1, lambda k: psi_copy(chip_peer(k), place).wait_send())
-    for o in range(1, 4):
-        block_copy(o, o - 1).wait_send()
+        first_ref[8 * (p // 2) : 8 * (p // 2 + 1), 128 * (p % 2) : 128 * (p % 2 + 1)] = sum_all[p]
+    first_ref[0:LAT] -= mean
+    first_ref[LAT : 2 * LAT] -= 0.5 * (variance - 1.0)
+    out_copy = pltpu.make_async_copy(first_ref, latent_out, local_sem.at[1])
+    out_copy.start()
+    wait_all(TOTAL, 1, total_recv.at[pl.ds(0, DP - 1)])
+    factor = beta[:, 0:128] / (CELLS * DP * GENES * GENE)
+    amplitude = jnp.exp(jnp.full((1, 128), kernel_log, F32))
+    rest = (0.5 - 0.5 * beta[:, 0:128] * amplitude) / 1024
+    total_out[0] = jnp.sum(jnp.sum(total_recv[...], axis=0) * factor + rest)
+
+    latent_across().wait_send()
+    pair_gram_copy().wait_send()
     cell_copy().wait_send()
     pair_latent_copy().wait_send()
     pair_psi_copy().wait_send()
-
-
-def finish(
-    latent_ref,
-    proj_ref,
-    total_ref,
-    mean_ref,
-    logvar_ref,
-    log_var_ref,
-    log_beta_ref,
-    latent_out,
-    proj_out,
-    scalar_out,
-):
-    beta = jnp.exp(jnp.full((8, 128), log_beta_ref[0], F32))
-    amplitude = jnp.exp(jnp.full((8, 128), log_var_ref[0], F32))
-    proj_out[...] = proj_ref[...] * (beta[0:1, 0:1] / (CELLS * DP))
-
-    @pl.when(pl.program_id(0) == 0)
-    def _():
-        latent_out[0] = latent_ref[0:LAT] - mean_ref[...]
-        latent_out[1] = latent_ref[LAT : 2 * LAT] - 0.5 * (jnp.exp(logvar_ref[...]) - 1.0)
-        entries = CELLS * DP * GENES * GENE
-        scalar_out[0] = jnp.sum(
-            beta * total_ref[...] / entries - (0.5 / 1024) * beta * amplitude + 0.5 / 1024
-        )
+    wait_all(LATENT, 0, lat_all.at[core, pl.ds(0, DP_Z - 1)])
+    wait_all(GRAM, 0, gram_recv.at[pl.ds(0, chips - 1)])
+    wait_all(GRAD, 0, grad_recv.at[pl.ds(0, DP - 1)])
+    wait_all(DATA, 0, data_recv.at[pl.ds(0, DP_Z - 1)])
+    wait_all(PSI, 0, psi_all.at[core, pl.ds(0, chips - 1)])
+    wait_all(PART, 0, part_recv.at[pl.ds(0, GENE - 1)])
+    wait_all(TURNED, 0, block_recv)
+    wait_all(SUM, 0, sum_all.at[pl.ds(0, GENE - 1)])
+    wait_all(TOTAL, 0, total_recv.at[pl.ds(0, DP - 1)])
+    proj_copy.wait()
+    out_copy.wait()
 
 
 def on_device(
@@ -632,9 +625,11 @@
         pltpu.VMEM((2, CELLS, GENES), BF16),
         pltpu.VMEM((IND, CELLS), BF16),
         pltpu.VMEM((DP_Z * BLOCK, CELLS), BF16),
-        pltpu.VMEM((2, DP, LAT, CELLS), F32),
+        pltpu.VMEM((2, DP_Z, DP // DP_Z, LAT, CELLS), F32),
         pltpu.VMEM((GENE, ROWS, WIDTH), F32),
-        pltpu.VMEM((GENE, ROWS, WIDTH), F32),
+        pltpu.VMEM((GENE // 2, ROWS, WIDTH), F32),
+        pltpu.VMEM((GENE // 2, 2 * ROWS, HALF), BF16),
+        pltpu.VMEM((GENE // 2, 2 * ROWS, HALF), BF16),
         pltpu.VMEM((DP_Z, BLOCK, GENES), BF16),
         pltpu.VMEM((DP_Z, BLOCK, GENES), BF16),
         pltpu.VMEM((BLOCK, GENES), F32),
@@ -656,19 +651,17 @@
         pltpu.VMEM((3, BLOCK, BLOCK), BF16),
         pltpu.VMEM((DP, 8, 128), F32),
         pltpu.SemaphoreType.DMA((5,)),
-        pltpu.SemaphoreType.DMA((5, 2, DP)),
-        pltpu.SemaphoreType.DMA((4, 2, GENE)),
-        pltpu.SemaphoreType.DMA((2, 2)),
+        pltpu.SemaphoreType.DMA((KINDS, 2)),
     ]
-    latent, proj, total = pl.pallas_call(
+    latent, proj, scalar = pl.pallas_call(
         kernel,
         out_shape=(
             jax.ShapeDtypeStruct((2 * LAT, CELLS), F32),
             jax.ShapeDtypeStruct((BLOCK, GENES), F32),
-            jax.ShapeDtypeStruct((8, 128), F32),
+            jax.ShapeDtypeStruct((1,), F32),
         ),
         in_specs=[hbm, vmem, vmem, vmem, vmem, vmem, smem, smem, hbm, vmem],
-        out_specs=(vmem, vmem, vmem),
+        out_specs=(hbm, hbm, smem),
         scratch_shapes=scratch,
         compiler_params=pltpu.CompilerParams(
             collective_id=0, has_side_effects=True, vmem_limit_bytes=56 * 1024 * 1024
@@ -686,32 +679,7 @@
         proj_mean,
         second_moment,
     )
-    steps = 4
-    grad_latent, grad_proj, grad_logbeta = pl.pallas_call(
-        finish,
-        grid=(steps,),
-        out_shape=(
-            jax.ShapeDtypeStruct((2, LAT, CELLS), F32),
-            jax.ShapeDtypeStruct((BLOCK, GENES), F32),
-            jax.ShapeDtypeStruct((1,), F32),
-        ),
-        in_specs=[
-            pl.BlockSpec((2 * LAT, CELLS), lambda i: (0, 0)),
-            pl.BlockSpec((BLOCK // steps, GENES), lambda i: (i, 0)),
-            pl.BlockSpec((8, 128), lambda i: (0, 0)),
-            pl.BlockSpec((LAT, CELLS), lambda i: (0, 0)),
-            pl.BlockSpec((LAT, CELLS), lambda i: (0, 0)),
-            smem,
-            smem,
-        ],
-        out_specs=(
-            pl.BlockSpec((2, LAT, CELLS), lambda i: (0, 0, 0)),
-            pl.BlockSpec((BLOCK // steps, GENES), lambda i: (i, 0)),
-            smem,
-        ),
-        name="finish",
-    )(latent, proj, total, latent_mean, latent_logvar, log_var, log_beta)
-    return (grad_latent, grad_proj, grad_logbeta)
+    return (latent.reshape(2, LAT, CELLS), proj, scalar)
 
 
 def solution(mesh):

time: 63.8 us -> 58.2 us (0.912)
  Pallas kernels: 61.7 us -> 50.8 us
  local copies, waits for them, and re-layouts: 0 us -> 3.36 us
  between operations: 1.93 us -> 3.73 us
    pallas_call x1, Pallas kernels: 58.3 us -> 50.8 us  [on_device(): pl.pallas_call(kernel, out_shape=(jax.ShapeDtypeStruct((2 * LAT, CELLS),...]
    pallas_call x1 -> x0, Pallas kernels: 3.37 us -> none  [on_device(): pl.pallas_call(finish, grid=(steps,), out_shape=(jax.ShapeDtypeStruct((2,...]
    unnamed x0 -> x2, local copies, waits for them, and re-layouts: none -> 3.36 us
where the time goes in v3:
time: 58.2 us; the launch traced here: 57.9 us
  Pallas kernels  50.8 us (87%)
  between operations  3.73 us (6%)
  local copies, waits for them, and re-layouts  3.36 us (6%)
    pallas_call x1, Pallas kernels, on_device(): pl.pallas_call(kernel, out_shape=(jax.ShapeDtypeStruct((2 * LAT, CELLS),...  50.8 us
    unnamed x2, local copies, waits for them, and re-layouts  3.36 us

profile of v3, /device:TPU:1, one launch (start us, length us, event | category | flops | bytes accessed | tf_op | source)
XLA Modules:
  0.0 57.9 jit_solution(3074660000318334367)
XLA Ops:
  1.9 50.8 %bound_gradients.1 = (f32[64,256]{1,0:T(8,128)}, f32[128,1024]{1,0:T(8,128)}, f32[1]{0:T(128)}) custom-call(bf16[1024,1024]{1,0:T(8,128)(2,1)} %y_hbm.1, s32[1,256]{1,0:T(1,128)} %bitcast.4, f32[32,256]{1,0:T(8,128)} %mean_ref.1, f32[32,256]{1,0:T(8,128)} %logvar_ref.1, f32[32,1024]{1,0:T(8,128)} %inducing_ref.1, f32[1,32]{1,0:T(1,128)} %bitcast.5, ...), custom_call_target="tpu_custom_call" | custom-call | tf_op jit(solution)/shard_map/bound_gradients/pallas_call | solution.py:656
  52.8 1.5 %copy.18 = f32[2,32,256]{2,1,0:T(8,128)} copy(f32[2,32,256]{2,1,0:T(8,128)} %bitcast.3) | data formatting | bytes 131072
  54.3 1.9 %copy.19 = f32[128,1024]{1,0:T(8,128)} copy(f32[128,1024]{1,0:T(8,128)} %get-tuple-element.13) | data formatting | bytes 1048576

commit v4 on v3

--- a/solution.py
+++ b/solution.py
@@ -27,6 +27,7 @@
 PAIRS = ROWS * WIDTH // STEPS
 DEPTH = 256
 HALF = 384
+CLOSING = 4
 SPLIT = 4
 (
     ACROSS,
@@ -41,10 +42,13 @@
     PAIR_PSI,
     PART,
     TURNED,
-    SUM,
+    PAIR_TURNED,
+    PAIR_GRAD,
+    PAIR_SUM,
     TOTAL,
+    GRAND,
     KINDS,
-) = range(15)
+) = range(18)
 BLOCK_WEIGHT = (1.0, 2.0, 2.0, 2.0, 1.0)
 
 
@@ -109,22 +113,30 @@
 
 def kernel(
     y_hbm,
+    index_hbm,
+    mean_hbm,
+    logvar_hbm,
+    inducing_hbm,
+    length_hbm,
+    log_var_ref,
+    log_beta_ref,
+    proj_hbm,
+    moment_hbm,
+    latent_out,
+    proj_out,
+    total_out,
     index_ref,
     mean_ref,
     logvar_ref,
     inducing_ref,
     length_ref,
-    log_var_ref,
-    log_beta_ref,
-    proj_hbm,
     moment_ref,
-    latent_out,
-    proj_out,
-    total_out,
     proj_f32,
     proj_low,
     y_ref,
     cell_all,
+    point_feat,
+    psi_one_ref,
     psi_low_ref,
     psi_side,
     lat_all,
@@ -135,6 +147,9 @@
     data_send,
     data_recv,
     data_own,
+    base_ref,
+    norm_ref,
+    row_ref,
     pair_feat,
     pair_cols,
     cell_coef,
@@ -146,12 +161,13 @@
     grad_send,
     grad_recv,
     psi_all,
-    part_send,
-    part_recv,
+    turned_all,
+    half_send,
+    half_recv,
+    part_all,
     sum_all,
-    block_send,
-    block_recv,
     total_recv,
+    grand_recv,
     local_sem,
     sems,
 ):
@@ -165,6 +181,7 @@
     place = lax.div(g, 2)
     group = GENE // 2 * core + place
     sibling = g + 1 - 2 * core
+    chips = GENE // 2
 
     def remote(src, dst, axis, send_sem, recv_sem, peer):
         return pltpu.make_async_remote_copy(
@@ -213,9 +230,19 @@
         for k in range(4)
     ]
     y_copy = pltpu.make_async_copy(y_hbm, y_ref, local_sem.at[4])
-    for copy in proj_copies:
+    small = [
+        (mean_hbm, mean_ref),
+        (logvar_hbm, logvar_ref),
+        (moment_hbm, moment_ref),
+        (inducing_hbm, inducing_ref),
+        (index_hbm, index_ref),
+        (length_hbm, length_ref),
+    ]
+    small_copies = [
+        pltpu.make_async_copy(src, dst, local_sem.at[5 + k]) for k, (src, dst) in enumerate(small)
+    ]
+    for copy in small_copies[0:2] + proj_copies + small_copies[2:] + [y_copy]:
         copy.start()
-    y_copy.start()
 
     barrier = pltpu.get_barrier_semaphore()
     each(
@@ -230,8 +257,22 @@
             barrier, inc=1, device_id={"gene": gene_peer(k)}, device_id_type=MESH
         ),
     )
+    def greet_step(k):
+        pl.semaphore_signal(
+            barrier,
+            inc=1,
+            device_id={
+                "dp": lax.rem(d + DP - 1 - lax.div(k, chips - 1), DP),
+                "gene": 2 * chip_peer(lax.rem(k, chips - 1)) + core,
+            },
+            device_id_type=MESH,
+        )
+
+    each(3 * (chips - 1), greet_step)
+    for copy in small_copies[0:2]:
+        copy.wait()
     lat_all[core, z, half] = jnp.where(core == 0, mean_ref[...], logvar_ref[...])
-    pl.semaphore_wait(barrier, DP + GENE - 2)
+    pl.semaphore_wait(barrier, DP + GENE - 2 + 3 * (chips - 1))
 
     def latent_across():
         mine = lat_all.at[core, z, half]
@@ -245,6 +286,8 @@
             quarter * k : quarter * (k + 1)
         ].astype(BF16)
 
+    for copy in small_copies[2:]:
+        copy.wait()
     own_rows = proj_low[pl.ds(pl.multiple_of(BLOCK * d, BLOCK), BLOCK)]
     row_of = lax.broadcasted_iota(jnp.int32, (BLOCK, 64), 0) + BLOCK * d
     col_of = lax.broadcasted_iota(jnp.int32, (BLOCK, 64), 1) + 64 * g
@@ -262,18 +305,10 @@
         block = BLOCK_WEIGHT[o] * (gram + 0.5 * moment_part)
         gram_send[:, :, BLOCK * o : BLOCK * (o + 1)] = block.reshape(GENE, ROWS, BLOCK)
 
-    chips = GENE // 2
-
     def pair_gram_copy():
         return pair_copy(PAIR_GRAM, gram_send.at[pl.ds(chips * (1 - core), chips)], gram_pair)
 
     pair_gram_copy().start()
-
-    latent_across().wait_recv()
-    each(
-        DP_Z - 1,
-        lambda k: dp_copy(LATENT, lat_all.at[core, z], lat_all.at[core, z], z_peer(k)).start(),
-    )
 
     eye_cells = lax.broadcasted_iota(jnp.int32, (CELLS, CELLS), 0) == lax.broadcasted_iota(
         jnp.int32, (CELLS, CELLS), 1
@@ -313,6 +348,12 @@
         jnp.add, [squares[:, 128 * k : 128 * (k + 1)] for k in range(GENES // 128)]
     )
 
+    latent_across().wait_recv()
+    each(
+        DP_Z - 1,
+        lambda k: dp_copy(LATENT, lat_all.at[core, z], lat_all.at[core, z], z_peer(k)).start(),
+    )
+
     kernel_log = log_var_ref[0]
     eye = lax.broadcasted_iota(jnp.int32, (LAT, LAT), 0) == lax.broadcasted_iota(
         jnp.int32, (LAT, LAT), 1
@@ -332,14 +373,53 @@
     mean = mean_ref[...]
     variance = jnp.exp(logvar_ref[...])
     inverse = 1.0 / (length + variance)
-    features = point_features(inducing_ref[...], []).astype(BF16)
-    psi_one = jnp.exp2(dot(features, first_coefficients(mean, inverse), 0, 0))
-    psi_low_ref[...] = psi_one.astype(BF16)
+    point_feat[...] = point_features(inducing_ref[...], []).astype(BF16)
+    psi_one_ref[...] = jnp.exp2(dot(point_feat[...], first_coefficients(mean, inverse), 0, 0))
+    psi_low_ref[...] = psi_one_ref[...].astype(BF16)
+    beta = jnp.exp(jnp.full((1, CELLS), log_beta_ref[0], F32))
+
+    lane = lax.broadcasted_iota(jnp.int32, (BLOCK, BLOCK), 1)
+    squared = lax.rem(lane, 2 * LAT) >= LAT
+    high_part = lane < 2 * LAT
+    ones = jnp.where((lane >= 64) & (lane < 67), 1.0, 0.0)
+    half_inv = (-0.5 * LOG2E) / length
+
+    def window(o):
+        at = lax.rem(d + o, DP)
+        return inducing_ref[:, pl.ds(pl.multiple_of(BLOCK * at, BLOCK), BLOCK)]
+
+    for o in range(SPAN):
+        points = window(o)
+        norm = jnp.sum(points * points * half_inv, axis=0, keepdims=True)
+        base_ref[o] = jnp.concatenate([points] * 4, axis=0).T
+        norm_ref[o] = jnp.broadcast_to(norm, (BLOCK, BLOCK)).T
+    own_point = base_ref[0, pl.ds(pl.multiple_of(ROWS * group, ROWS), ROWS)]
+    own_norm = norm_ref[0, pl.ds(pl.multiple_of(ROWS * group, ROWS), ROWS)]
+    row_ref[0] = own_point
+    row_ref[1] = own_norm
+
+    def feature_step(i):
+        row = row_ref[0, pl.ds(i, 1)]
+        row_norm = row_ref[1, pl.ds(i, 1)]
+        for o in range(SPAN):
+            middle = 0.5 * (base_ref[o] + row)
+            value = jnp.where(squared, middle * middle, middle)
+            high = value.astype(BF16).astype(F32)
+            pair = split_three(norm_ref[o] + row_norm)
+            extra = ones
+            for k in range(3):
+                extra = jnp.where(lane == 67 + k, pair[k], extra)
+            offset = pl.multiple_of(lax.rem(i, 2) * WIDTH + BLOCK * o, BLOCK)
+            at = pl.ds(offset, BLOCK)
+            step = lax.div(i, 2)
+            pair_feat[step, at, 0:128] = jnp.where(high_part, high, value - high).astype(BF16)
+            pair_feat[step, at, 128:256] = jnp.where(high_part, high, extra).astype(BF16)
+
+    each(ROWS, feature_step)
 
     cross = dot(proj_low[...], cell_all[0], 1, 1)
-    product = psi_one * cross
-    sum_0, sum_1, sum_2 = moments(dot(features, product.astype(BF16), 1, 0))
-    beta = jnp.exp(jnp.full((1, CELLS), log_beta_ref[0], F32))
+    product = psi_one_ref[...] * cross
+    sum_0, sum_1, sum_2 = moments(dot(point_feat[...], product.astype(BF16), 1, 0))
     beta_sq = beta * beta
     first_ref[0:LAT] = beta_sq * inverse * (sum_1 - mean * sum_0)
     first_ref[LAT : 2 * LAT] = (
@@ -350,25 +430,6 @@
         * (inverse * (sum_2 - 2.0 * mean * sum_1 + mean * mean * sum_0) - sum_0)
     )
 
-    base = inducing_ref[:, pl.ds(pl.multiple_of(BLOCK * d, BLOCK), BLOCK)]
-    lane = lax.broadcasted_iota(jnp.int32, (LAT, BLOCK), 1)
-    quarter_inv = (-0.25 * LOG2E) / length
-
-    def feature_step(i):
-        column = jnp.sum(jnp.where(lane == ROWS * group + i, base, 0.0), axis=1, keepdims=True)
-        for o in range(SPAN):
-            at = lax.rem(d + o, DP)
-            points = inducing_ref[:, pl.ds(pl.multiple_of(BLOCK * at, BLOCK), BLOCK)]
-            gap = points - column
-            pair = jnp.sum(gap * gap * quarter_inv, axis=0, keepdims=True)
-            block = point_features(0.5 * (points + column), split_three(pair))
-            offset = pl.multiple_of(lax.rem(i, 2) * WIDTH + BLOCK * o, BLOCK)
-            pair_feat[lax.div(i, 2), :, pl.ds(offset, BLOCK)] = block.astype(BF16)
-            columns = jnp.concatenate([block[0:96], block[192:224]], axis=0)
-            pair_cols[lax.div(i, 2), pl.ds(offset, BLOCK)] = columns.T.astype(BF16)
-
-    each(ROWS, feature_step)
-
     def latents(kind, at):
         return lat_all[kind, lax.rem(at, DP_Z), lax.div(at, DP_Z)]
 
@@ -377,11 +438,37 @@
 
     wait_all(LATENT, 1, lat_all.at[core, pl.ds(0, DP_Z - 1)])
     pair_latent_copy().start()
+    wait_all(GRAM, 1, gram_recv.at[pl.ds(0, chips - 1)])
+    weight = jnp.sum(gram_recv[...].astype(F32), axis=0)
+    weight = jnp.concatenate([weight[0:ROWS], weight[ROWS:, 0 : WIDTH - HALF]], axis=1)
+    weight_ref[...] = weight
+    base = window(0)
+    own_lane = lax.broadcasted_iota(jnp.int32, (LAT, BLOCK), 1) - ROWS * group
+
+    def weight_step(i):
+        column = jnp.sum(jnp.where(own_lane == i, base, 0.0), axis=1, keepdims=True)
+        row = weight_ref[pl.ds(i, 1)]
+        for o in range(SPAN):
+            weight_row = row[:, BLOCK * o : BLOCK * (o + 1)]
+            middle = 0.5 * (window(o) + column)
+            linear = middle * weight_row
+            high, low = split_two(linear)
+            block = jnp.concatenate(
+                [high, middle * linear, low, special(split_two(weight_row), BLOCK)[0:32]], axis=0
+            )
+            offset = pl.multiple_of(lax.rem(i, 2) * WIDTH + BLOCK * o, BLOCK)
+            pair_cols[lax.div(i, 2), :, pl.ds(offset, BLOCK)] = block.astype(BF16)
+
+    each(ROWS, weight_step)
+    psi_acc[...] = jnp.zeros_like(psi_acc)
+    trace_ref[...] = jnp.zeros_like(trace_ref)
+
     pair_latent_copy().wait_recv()
 
     def coefficient_step(at):
         cell_mean = latents(0, at)
-        inverse_w = 1.0 / (length + 2.0 * jnp.exp(latents(1, at)))
+        cell_var = jnp.exp(latents(1, at))
+        inverse_w = 1.0 / (length + 2.0 * cell_var)
         inv_width[at] = inverse_w
         const = 2.0 * kernel_log + jnp.sum(
             0.5 * jnp.log(length * inverse_w) - cell_mean * cell_mean * inverse_w,
@@ -389,32 +476,22 @@
             keepdims=True,
         )
         block = cell_coefficients(
-            (2.0 * LOG2E) * cell_mean * inverse_w, -LOG2E * inverse_w, LOG2E * const, 3
-        )
-        cell_coef[at] = block.T.astype(BF16)
+            (2.0 * LOG2E) * cell_mean * inverse_w,
+            (2.0 * LOG2E) * cell_var * inverse_w / length,
+            LOG2E * const,
+            3,
+        )
+        cell_coef[at] = block.astype(BF16)
 
     each(DP, coefficient_step)
 
-    wait_all(GRAM, 1, gram_recv.at[pl.ds(0, chips - 1)])
-    weight = jnp.sum(gram_recv[...].astype(F32), axis=0)
-    weight = jnp.concatenate([weight[0:ROWS], weight[ROWS:, 0 : WIDTH - HALF]], axis=1)
-    for i in range(ROWS):
-        weight_ref[i // 2, :, WIDTH * (i % 2) : WIDTH * (i % 2 + 1)] = jnp.broadcast_to(
-            weight[i : i + 1], (8, WIDTH)
-        )
-    psi_acc[...] = jnp.zeros_like(psi_acc)
-    trace_ref[...] = jnp.zeros_like(trace_ref)
-
     def cell_gradients(at):
-        table = jnp.zeros((CELLS, 128), F32)
+        table = jnp.zeros((128, CELLS), F32)
         for s in range(STEPS):
-            psi = jnp.exp2(dot(cell_coef[at], pair_feat[s], 1, 0))
-            psi = psi.reshape(CELLS // 8, 8, PAIRS)
-            psi_acc[s] += jnp.sum(psi, axis=0)
-            weighted = (psi * weight_ref[s][None]).reshape(CELLS, PAIRS).astype(BF16)
-            table = table + dot(weighted, pair_cols[s], 1, 0)
-        table = table.T
-        mom_0 = table[96:97]
+            psi = jnp.exp2(dot(pair_feat[s], cell_coef[at], 1, 0))
+            psi_acc[s] += psi[:, 0:128] + psi[:, 128:256]
+            table = table + dot(pair_cols[s], psi.astype(BF16), 1, 0)
+        mom_0 = table[96:97] + table[97:98]
         mom_1 = table[0:32] + table[64:96]
         mom_2 = table[32:64]
         cell_mean = latents(0, at)
@@ -468,102 +545,118 @@
 
     data_step(1)
     each(DP - 1 - SPLIT, lambda k: cell_step(k + SPLIT))
-    data_step(0)
-    data_step(2)
     by_mean, by_logvar = cell_gradients(d)
     first_ref[0:LAT] += by_mean
     first_ref[LAT : 2 * LAT] += by_logvar
 
-    total_row = sum_0 - 0.5 * trace_ref[...]
-    total_row = total_row[:, 0:128] + total_row[:, 128:256]
-    first_row = lax.broadcasted_iota(jnp.int32, (8, 128), 0) == 0
-    total_tile = jnp.where(first_row, jnp.broadcast_to(total_row, (8, 128)), 0.0) - (
-        0.5 * square_tile
-    )
+    add_lanes = jnp.ones((16, 128), BF16)
+    sums = [dot(add_lanes, psi_acc[s].astype(BF16), 1, 1)[0:1] for s in range(STEPS)]
     rows = jnp.concatenate(
-        [
-            jnp.sum(
-                psi_acc[i // 2, :, WIDTH * (i % 2) : WIDTH * (i % 2 + 1)], axis=0, keepdims=True
-            )
-            for i in range(ROWS)
-        ],
-        axis=0,
-    )
-    wide = jnp.concatenate([rows, jnp.zeros((ROWS, 128), F32)], axis=1)
-    psi_all[core, place] = jnp.concatenate([wide[:, 0:HALF], wide[:, HALF:]], axis=0).astype(BF16)
-
+        [sums[i // 2][:, WIDTH * (i % 2) : WIDTH * (i % 2 + 1)] for i in range(ROWS)], axis=0
+    )
+    psi_all[core, place] = rows
     own_psi = psi_all.at[core, place]
+
+    def turned_step(k):
+        chip = chip_peer(k)
+        for o in range(1, 4):
+            pltpu.make_async_remote_copy(
+                src_ref=psi_all.at[core, place, :, pl.ds(BLOCK * o, BLOCK)],
+                dst_ref=turned_all.at[core, o - 1, place],
+                send_sem=sems.at[TURNED, 0],
+                recv_sem=sems.at[TURNED, 1],
+                device_id={"dp": lax.rem(d + o, DP), "gene": 2 * chip + core},
+                device_id_type=MESH,
+            ).start()
+
+    each(chips, turned_step)
     each(
         chips - 1,
         lambda k: gene_copy(PSI, own_psi, own_psi, 2 * chip_peer(k) + core).start(),
     )
+
+    total_row = sum_0 - 0.5 * trace_ref[...]
+    total_row = total_row[:, 0:128] + total_row[:, 128:256]
+    total_row = total_row - 0.5 * jnp.sum(square_tile, axis=0, keepdims=True)
+    first_row = lax.broadcasted_iota(jnp.int32, (8, 128), 0) == 0
+    total_recv[d] = jnp.where(first_row, jnp.broadcast_to(total_row, (8, 128)), 0.0)
+    own_total = total_recv.at[d]
+    each(DP - 1, lambda k: dp_copy(TOTAL, own_total, own_total, dp_peer(k)).start())
+
+    data_step(0)
+    data_step(2)
 
     grad_recv[d] = jnp.zeros((2 * LAT, CELLS), BF16)
     wait_all(GRAD, 1, grad_recv.at[pl.ds(0, DP - 1)])
     own_grad = first_ref[...]
     for p in range(DP):
         own_grad = own_grad + grad_recv[p].astype(F32)
-    for p in range(GENE):
-        part_send[p, 0:8] = own_grad[
-            8 * (p // 2) : 8 * (p // 2 + 1), 128 * (p % 2) : 128 * (p % 2 + 1)
-        ]
-        part_send[p, 8:16] = total_tile
-
-    def part_step(k):
-        peer = gene_peer(k)
-        gene_copy(PART, part_send.at[peer], part_recv.at[g], peer).start()
-
-    each(GENE - 1, part_step)
-    part_recv[g] = part_send[g]
+    first_ref[...] = own_grad
+    give = jnp.where(core == 0, own_grad[LAT : 2 * LAT], own_grad[0:LAT])
+    keep = jnp.where(core == 0, own_grad[0:LAT], own_grad[LAT : 2 * LAT])
+    half_send[...] = give
+
+    def pair_grad_copy():
+        return pair_copy(PAIR_GRAD, half_send, half_recv)
+
+    pair_grad_copy().start()
+
+    data_own[...] = data_rows(z)
+
+    pair_grad_copy().wait_recv()
+    part_all[place] = (keep + half_recv[...]).astype(BF16)
+    own_part = part_all.at[place]
+    each(
+        chips - 1,
+        lambda k: gene_copy(PART, own_part, own_part, 2 * chip_peer(k) + core).start(),
+    )
+
+    wait_all(TOTAL, 1, total_recv.at[pl.ds(0, DP - 1)])
+    grand_recv[g] = jnp.sum(total_recv[...], axis=0)
+    own_grand = grand_recv.at[g]
+    each(GENE - 1, lambda k: gene_copy(GRAND, own_grand, own_grand, gene_peer(k)).start())
 
     def pair_psi_copy():
         return pair_copy(PAIR_PSI, psi_all.at[core], psi_all.at[core])
 
+    def pair_turned_copy():
+        return pair_copy(PAIR_TURNED, turned_all.at[core], turned_all.at[core])
+
     wait_all(PSI, 1, psi_all.at[core, pl.ds(0, chips - 1)])
     pair_psi_copy().start()
-
-    data_own[...] = data_rows(z)
+    wait_all(TURNED, 1, turned_all.at[core])
+    pair_turned_copy().start()
 
     pair_psi_copy().wait_recv()
-    gathered = psi_all[...].astype(F32).reshape(GENE, 2 * ROWS, HALF)
-    left = gathered[:, 0:ROWS].reshape(BLOCK, HALF)
-    right = gathered[:, ROWS : 2 * ROWS].reshape(BLOCK, HALF)
-    psi_rows = [
-        (left if o < 3 else right)[:, BLOCK * (o % 3) : BLOCK * (o % 3 + 1)].astype(BF16)
-        for o in range(SPAN)
-    ]
-    for o in range(1, 4):
-        block_send[o - 1] = psi_rows[o]
-
-    for o in range(1, 4):
-        dp_copy(
-            TURNED, block_send.at[o - 1], block_recv.at[o - 1], lax.rem(d + o, DP)
-        ).start()
-
-    wait_all(PART, 1, part_recv.at[pl.ds(0, GENE - 1)])
-    part_sum = jnp.sum(part_recv[...], axis=0)
-    sum_all[g] = part_sum[0:8]
-    total_recv[d] = part_sum[8:16]
-
-    own_sum = sum_all.at[g]
-    own_total = total_recv.at[d]
-    each(GENE - 1, lambda k: gene_copy(SUM, own_sum, own_sum, gene_peer(k)).start())
-    each(DP - 1, lambda k: dp_copy(TOTAL, own_total, own_total, dp_peer(k)).start())
-
+    psi_rows = psi_all[...].reshape(BLOCK, WIDTH).astype(BF16)
     stat = data_own[...]
     for o in range(SPAN):
         at = lax.rem(d + o, DP)
         stat = stat - dot(
-            psi_rows[o], proj_low[pl.ds(pl.multiple_of(BLOCK * at, BLOCK), BLOCK)], 1, 0
-        )
+            psi_rows[:, BLOCK * o : BLOCK * (o + 1)],
+            proj_low[pl.ds(pl.multiple_of(BLOCK * at, BLOCK), BLOCK)],
+            1,
+            0,
+        )
+    data_own[...] = stat
+
+    wait_all(PART, 1, part_all.at[pl.ds(0, chips - 1)])
+    sum_all[core] = jnp.sum(part_all[...].astype(F32), axis=0)
+
+    def pair_sum_copy():
+        return pair_copy(PAIR_SUM, sum_all.at[core], sum_all.at[core])
+
+    pair_sum_copy().start()
+
     wait_all(DATA, 1, data_recv.at[pl.ds(0, DP_Z - 1)])
+    stat = data_own[...]
     for k in range(DP_Z - 1):
         stat = stat + data_recv[lax.rem(z + 1 + k, DP_Z)].astype(F32)
-    wait_all(TURNED, 1, block_recv)
+    pair_turned_copy().wait_recv()
     for o in range(1, 4):
         at = lax.rem(d + (DP - o), DP)
         stat = stat - dot(
-            block_recv[o - 1],
+            turned_all[:, o - 1].reshape(BLOCK, BLOCK).astype(BF16),
             proj_low[pl.ds(pl.multiple_of(BLOCK * at, BLOCK), BLOCK)],
             0,
             0,
@@ -572,18 +665,17 @@
     proj_copy = pltpu.make_async_copy(data_own, proj_out, local_sem.at[0])
     proj_copy.start()
 
-    wait_all(SUM, 1, sum_all.at[pl.ds(0, GENE - 1)])
-    for p in range(GENE):
-        first_ref[8 * (p // 2) : 8 * (p // 2 + 1), 128 * (p % 2) : 128 * (p % 2 + 1)] = sum_all[p]
-    first_ref[0:LAT] -= mean
-    first_ref[LAT : 2 * LAT] -= 0.5 * (variance - 1.0)
+    pair_sum_copy().wait_recv()
+    first_ref[0:LAT] = sum_all[0] - mean
+    first_ref[LAT : 2 * LAT] = sum_all[1] - 0.5 * (variance - 1.0)
     out_copy = pltpu.make_async_copy(first_ref, latent_out, local_sem.at[1])
     out_copy.start()
-    wait_all(TOTAL, 1, total_recv.at[pl.ds(0, DP - 1)])
+
+    wait_all(GRAND, 1, grand_recv.at[pl.ds(0, GENE - 1)])
     factor = beta[:, 0:128] / (CELLS * DP * GENES * GENE)
     amplitude = jnp.exp(jnp.full((1, 128), kernel_log, F32))
     rest = (0.5 - 0.5 * beta[:, 0:128] * amplitude) / 1024
-    total_out[0] = jnp.sum(jnp.sum(total_recv[...], axis=0) * factor + rest)
+    total_out[0] = jnp.sum(jnp.sum(grand_recv[...], axis=0) * factor + rest)
 
     latent_across().wait_send()
     pair_gram_copy().wait_send()
@@ -595,12 +687,35 @@
     wait_all(GRAD, 0, grad_recv.at[pl.ds(0, DP - 1)])
     wait_all(DATA, 0, data_recv.at[pl.ds(0, DP_Z - 1)])
     wait_all(PSI, 0, psi_all.at[core, pl.ds(0, chips - 1)])
-    wait_all(PART, 0, part_recv.at[pl.ds(0, GENE - 1)])
-    wait_all(TURNED, 0, block_recv)
-    wait_all(SUM, 0, sum_all.at[pl.ds(0, GENE - 1)])
+    wait_all(PART, 0, part_all.at[pl.ds(0, chips - 1)])
+    wait_all(TURNED, 0, turned_all.at[core])
+    pair_turned_copy().wait_send()
+    pair_grad_copy().wait_send()
+    pair_sum_copy().wait_send()
+    wait_all(GRAND, 0, grand_recv.at[pl.ds(0, GENE - 1)])
     wait_all(TOTAL, 0, total_recv.at[pl.ds(0, DP - 1)])
     proj_copy.wait()
     out_copy.wait()
+
+
+def finish(latent_ref, proj_ref, latent_out, proj_out, latent_held, proj_held, done):
+    rows = BLOCK // CLOSING
+    cuts = [pl.ds(rows * k, rows) for k in range(CLOSING)]
+    pairs = [(proj_ref.at[c], proj_held.at[c], proj_out.at[c]) for c in cuts]
+    pairs.append((latent_ref, latent_held, latent_out))
+    loads = [
+        pltpu.make_async_copy(src, held, done.at[0, k]) for k, (src, held, _) in enumerate(pairs)
+    ]
+    stores = [
+        pltpu.make_async_copy(held, dst, done.at[1, k]) for k, (_, held, dst) in enumerate(pairs)
+    ]
+    for load in loads:
+        load.start()
+    for load, store in zip(loads, stores):
+        load.wait()
+        store.start()
+    for store in stores:
+        store.wait()
 
 
 def on_device(
@@ -615,14 +730,21 @@
     proj_mean,
     second_moment,
 ):
-    vmem = pl.BlockSpec(memory_space=pltpu.VMEM)
     smem = pl.BlockSpec(memory_space=pltpu.SMEM)
     hbm = pl.BlockSpec(memory_space=pl.ANY)
     scratch = [
+        pltpu.VMEM((1, CELLS), jnp.int32),
+        pltpu.VMEM((LAT, CELLS), F32),
+        pltpu.VMEM((LAT, CELLS), F32),
+        pltpu.VMEM((LAT, IND), F32),
+        pltpu.VMEM((1, LAT), F32),
+        pltpu.VMEM((IND // GENE, IND), F32),
         pltpu.VMEM((IND, GENES), F32),
         pltpu.VMEM((IND, GENES), BF16),
         pltpu.VMEM((IND, GENES), BF16),
         pltpu.VMEM((2, CELLS, GENES), BF16),
+        pltpu.VMEM((DEPTH, IND), BF16),
+        pltpu.VMEM((IND, CELLS), F32),
         pltpu.VMEM((IND, CELLS), BF16),
         pltpu.VMEM((DP_Z * BLOCK, CELLS), BF16),
         pltpu.VMEM((2, DP_Z, DP // DP_Z, LAT, CELLS), F32),
@@ -633,24 +755,28 @@
         pltpu.VMEM((DP_Z, BLOCK, GENES), BF16),
         pltpu.VMEM((DP_Z, BLOCK, GENES), BF16),
         pltpu.VMEM((BLOCK, GENES), F32),
-        pltpu.VMEM((STEPS, DEPTH, PAIRS), BF16),
-        pltpu.VMEM((STEPS, PAIRS, 128), BF16),
-        pltpu.VMEM((DP, CELLS, DEPTH), BF16),
+        pltpu.VMEM((SPAN, BLOCK, BLOCK), F32),
+        pltpu.VMEM((SPAN, BLOCK, BLOCK), F32),
+        pltpu.VMEM((2, ROWS, BLOCK), F32),
+        pltpu.VMEM((STEPS, PAIRS, DEPTH), BF16),
+        pltpu.VMEM((STEPS, 128, PAIRS), BF16),
+        pltpu.VMEM((DP, DEPTH, CELLS), BF16),
         pltpu.VMEM((DP, LAT, CELLS), F32),
-        pltpu.VMEM((STEPS, 8, PAIRS), F32),
-        pltpu.VMEM((STEPS, 8, PAIRS), F32),
+        pltpu.VMEM((ROWS, WIDTH), F32),
+        pltpu.VMEM((STEPS, PAIRS, 128), F32),
         pltpu.VMEM((2 * LAT, CELLS), F32),
         pltpu.VMEM((1, CELLS), F32),
         pltpu.VMEM((DP, 2 * LAT, CELLS), BF16),
         pltpu.VMEM((DP, 2 * LAT, CELLS), BF16),
-        pltpu.VMEM((2, GENE // 2, 2 * ROWS, HALF), BF16),
-        pltpu.VMEM((GENE, 16, 128), F32),
-        pltpu.VMEM((GENE, 16, 128), F32),
+        pltpu.VMEM((2, GENE // 2, ROWS, WIDTH), F32),
+        pltpu.VMEM((2, 3, GENE // 2, ROWS, BLOCK), F32),
+        pltpu.VMEM((LAT, CELLS), F32),
+        pltpu.VMEM((LAT, CELLS), F32),
+        pltpu.VMEM((GENE // 2, LAT, CELLS), BF16),
+        pltpu.VMEM((2, LAT, CELLS), F32),
+        pltpu.VMEM((DP, 8, 128), F32),
         pltpu.VMEM((GENE, 8, 128), F32),
-        pltpu.VMEM((3, BLOCK, BLOCK), BF16),
-        pltpu.VMEM((3, BLOCK, BLOCK), BF16),
-        pltpu.VMEM((DP, 8, 128), F32),
-        pltpu.SemaphoreType.DMA((5,)),
+        pltpu.SemaphoreType.DMA((11,)),
         pltpu.SemaphoreType.DMA((KINDS, 2)),
     ]
     latent, proj, scalar = pl.pallas_call(
@@ -660,7 +786,7 @@
             jax.ShapeDtypeStruct((BLOCK, GENES), F32),
             jax.ShapeDtypeStruct((1,), F32),
         ),
-        in_specs=[hbm, vmem, vmem, vmem, vmem, vmem, smem, smem, hbm, vmem],
+        in_specs=[hbm] * 6 + [smem, smem, hbm, hbm],
         out_specs=(hbm, hbm, smem),
         scratch_shapes=scratch,
         compiler_params=pltpu.CompilerParams(
@@ -679,6 +805,21 @@
         proj_mean,
         second_moment,
     )
+    latent, proj = pl.pallas_call(
+        finish,
+        out_shape=(
+            jax.ShapeDtypeStruct((2 * LAT, CELLS), F32),
+            jax.ShapeDtypeStruct((BLOCK, GENES), F32),
+        ),
+        in_specs=[hbm, hbm],
+        out_specs=(hbm, hbm),
+        scratch_shapes=[
+            pltpu.VMEM((2 * LAT, CELLS), F32),
+            pltpu.VMEM((BLOCK, GENES), F32),
+            pltpu.SemaphoreType.DMA((2, CLOSING + 1)),
+        ],
+        name="finish",
+    )(latent, proj)
     return (latent.reshape(2, LAT, CELLS), proj, scalar)
 
 

time: 58.2 us -> 52.9 us (0.909)
  local copies, waits for them, and re-layouts: 3.36 us -> 0 us
  Pallas kernels: 50.8 us -> 49 us
    pallas_call x1, Pallas kernels: 50.8 us -> 47.2 us  [on_device(): pl.pallas_call(kernel, out_shape=(jax.ShapeDtypeStruct((2 * LAT, CELLS),...]
    unnamed x2 -> x0, local copies, waits for them, and re-layouts: 3.36 us -> none
    pallas_call x0 -> x1, Pallas kernels: none -> 1.85 us  [on_device(): pl.pallas_call(finish, out_shape=(jax.ShapeDtypeStruct((2 * LAT, CELLS),...]
where the time goes in v4:
time: 52.9 us; the launch traced here: 52.8 us
  Pallas kernels  49 us (93%)
  between operations  3.74 us (7%)
    pallas_call x1, Pallas kernels, on_device(): pl.pallas_call(kernel, out_shape=(jax.ShapeDtypeStruct((2 * LAT, CELLS),...  47.2 us
    pallas_call x1, Pallas kernels, on_device(): pl.pallas_call(finish, out_shape=(jax.ShapeDtypeStruct((2 * LAT, CELLS),...  1.85 us

profile of v4, /device:TPU:1, one launch (start us, length us, event | category | flops | bytes accessed | tf_op | source)
XLA Modules:
  0.0 52.8 jit_solution(7039983584488599151)
XLA Ops:
  1.9 47.2 %bound_gradients.1 = (f32[64,256]{1,0:T(8,128)}, f32[128,1024]{1,0:T(8,128)}, f32[1]{0:T(128)}) custom-call(bf16[1024,1024]{1,0:T(8,128)(2,1)} %y_hbm.1, s32[1,256]{1,0:T(1,128)} %bitcast.3, f32[32,256]{1,0:T(8,128)} %mean_hbm.1, f32[32,256]{1,0:T(8,128)} %logvar_hbm.1, f32[32,1024]{1,0:T(8,128)} %inducing_hbm.1, f32[1,32]{1,0:T(1,128)} %bitcast.4, ...), custom_call_target="tpu_custom_call" | custom-call | tf_op jit(solution)/shard_map/bound_gradients/pallas_call | solution.py:782
  49.1 1.9 %finish.1 = (f32[64,256]{1,0:T(8,128)}, f32[128,1024]{1,0:T(8,128)}) custom-call(f32[64,256]{1,0:T(8,128)} %get-tuple-element.8.latent_ref, f32[128,1024]{1,0:T(8,128)} %get-tuple-element.9.proj_ref), custom_call_target="tpu_custom_call" | custom-call | tf_op jit(solution)/shard_map/finish/pallas_call | solution.py:808

commit v5 on v4

--- a/solution.py
+++ b/solution.py
@@ -28,7 +28,7 @@
 DEPTH = 256
 HALF = 384
 CLOSING = 4
-SPLIT = 4
+FIRST = 64
 (
     ACROSS,
     LATENT,
@@ -46,9 +46,10 @@
     PAIR_GRAD,
     PAIR_SUM,
     TOTAL,
-    GRAND,
+    EARLY,
+    OVER,
     KINDS,
-) = range(18)
+) = range(19)
 BLOCK_WEIGHT = (1.0, 2.0, 2.0, 2.0, 1.0)
 
 
@@ -58,6 +59,11 @@
         return carry
 
     lax.fori_loop(0, count, step, 0)
+
+
+def every(count, body):
+    for k in range(count):
+        body(k)
 
 
 def split_two(value):
@@ -144,6 +150,11 @@
     gram_pair,
     gram_out,
     gram_recv,
+    early_send,
+    early_recv,
+    early_own,
+    over_send,
+    over_recv,
     data_send,
     data_recv,
     data_own,
@@ -167,7 +178,6 @@
     part_all,
     sum_all,
     total_recv,
-    grand_recv,
     local_sem,
     sems,
 ):
@@ -245,13 +255,13 @@
         copy.start()
 
     barrier = pltpu.get_barrier_semaphore()
-    each(
+    every(
         DP - 1,
         lambda k: pl.semaphore_signal(
             barrier, inc=1, device_id={"dp": dp_peer(k)}, device_id_type=MESH
         ),
     )
-    each(
+    every(
         GENE - 1,
         lambda k: pl.semaphore_signal(
             barrier, inc=1, device_id={"gene": gene_peer(k)}, device_id_type=MESH
@@ -262,13 +272,13 @@
             barrier,
             inc=1,
             device_id={
-                "dp": lax.rem(d + DP - 1 - lax.div(k, chips - 1), DP),
-                "gene": 2 * chip_peer(lax.rem(k, chips - 1)) + core,
+                "dp": lax.rem(d + DP - 1 - k // (chips - 1), DP),
+                "gene": 2 * chip_peer(k % (chips - 1)) + core,
             },
             device_id_type=MESH,
         )
 
-    each(3 * (chips - 1), greet_step)
+    every(3 * (chips - 1), greet_step)
     for copy in small_copies[0:2]:
         copy.wait()
     lat_all[core, z, half] = jnp.where(core == 0, mean_ref[...], logvar_ref[...])
@@ -336,7 +346,7 @@
         chip = chip_peer(k)
         gene_copy(GRAM, gram_out.at[chip], gram_recv.at[place], 2 * chip + core).start()
 
-    each(chips - 1, gram_step)
+    every(chips - 1, gram_step)
     gram_recv[place] = gram_out[place]
 
     def cell_copy():
@@ -349,7 +359,7 @@
     )
 
     latent_across().wait_recv()
-    each(
+    every(
         DP_Z - 1,
         lambda k: dp_copy(LATENT, lat_all.at[core, z], lat_all.at[core, z], z_peer(k)).start(),
     )
@@ -429,6 +439,20 @@
         * inverse
         * (inverse * (sum_2 - 2.0 * mean * sum_1 + mean * mean * sum_0) - sum_0)
     )
+
+    def early_step(k):
+        at = lax.rem(z + 1 + k, DP_Z)
+        starts = [pl.multiple_of(BLOCK * (DP_Z * h + at), BLOCK) for h in range(DP // DP_Z)]
+        rows = jnp.concatenate([psi_low_ref[pl.ds(start, FIRST)] for start in starts], axis=0)
+        rows = dot(rows, cell_all[0], 1, 0).astype(BF16)
+        for h in range(DP // DP_Z):
+            early_send[at, h] = rows[FIRST * h : FIRST * (h + 1)]
+
+        @pl.when(k < DP_Z - 1)
+        def _():
+            dp_copy(EARLY, early_send.at[at], early_recv.at[z], z_peer(k)).start()
+
+    each(DP_Z, early_step)
 
     def latents(kind, at):
         return lat_all[kind, lax.rem(at, DP_Z), lax.div(at, DP_Z)]
@@ -517,7 +541,7 @@
         grad_send[at, LAT : 2 * LAT] = by_logvar.astype(BF16)
         dp_copy(GRAD, grad_send.at[at], grad_recv.at[d], at).start()
 
-    each(SPLIT, cell_step)
+    each(DP - 1, cell_step)
 
     cell_copy().wait_recv()
     side_points = inducing_ref[:, pl.ds(pl.multiple_of(BLOCK * side, BLOCK), BLOCK * DP_Z)]
@@ -534,20 +558,48 @@
     psi_side[...] = psi_across.astype(BF16)
 
     def data_rows(at):
-        near = psi_low_ref[pl.ds(pl.multiple_of(BLOCK * (side + at), BLOCK), BLOCK)]
-        far = psi_side[pl.ds(pl.multiple_of(BLOCK * at, BLOCK), BLOCK)]
+        start = pl.multiple_of(BLOCK * (side + at) + FIRST, FIRST)
+        near = psi_low_ref[pl.ds(start, BLOCK - FIRST)]
+        far = psi_side[pl.ds(pl.multiple_of(BLOCK * at + FIRST, FIRST), BLOCK - FIRST)]
         return dot(near, cell_all[0], 1, 0) + dot(far, cell_all[1], 1, 0)
 
     def data_step(k):
         at = lax.rem(z + 1 + k, DP_Z)
         data_send[at] = data_rows(at).astype(BF16)
-        dp_copy(DATA, data_send.at[at], data_recv.at[z], z_peer(k)).start()
-
-    data_step(1)
-    each(DP - 1 - SPLIT, lambda k: cell_step(k + SPLIT))
+
+    each(DP_Z - 1, data_step)
+
+    def data_send_rows():
+        def send_step(k):
+            at = lax.rem(z + 1 + k, DP_Z)
+            dp_copy(DATA, data_send.at[at], data_recv.at[z], z_peer(k)).start()
+
+        every(DP_Z - 1, send_step)
+
     by_mean, by_logvar = cell_gradients(d)
     first_ref[0:LAT] += by_mean
     first_ref[LAT : 2 * LAT] += by_logvar
+
+    grad_recv[d] = jnp.zeros((2 * LAT, CELLS), BF16)
+    wait_all(GRAD, 1, grad_recv.at[pl.ds(0, DP - 1)])
+    own_grad = first_ref[...]
+    for p in range(DP):
+        own_grad = own_grad + grad_recv[p].astype(F32)
+    first_ref[...] = own_grad
+    give = jnp.where(core == 0, own_grad[LAT : 2 * LAT], own_grad[0:LAT])
+    keep = jnp.where(core == 0, own_grad[0:LAT], own_grad[LAT : 2 * LAT])
+    total_row = sum_0 - 0.5 * trace_ref[...]
+    total_row = total_row[:, 0:128] + total_row[:, 128:256]
+    total_row = total_row - 0.5 * jnp.sum(square_tile, axis=0, keepdims=True)
+    total_row = jnp.concatenate([total_row, jnp.zeros((1, 128), F32)], axis=1)
+    total_tile = jnp.broadcast_to(0.125 * total_row, (8, CELLS))
+    half_send[0:LAT] = give
+    half_send[LAT : LAT + 8] = total_tile
+
+    def pair_grad_copy():
+        return pair_copy(PAIR_GRAD, half_send, half_recv)
+
+    pair_grad_copy().start()
 
     add_lanes = jnp.ones((16, 128), BF16)
     sums = [dot(add_lanes, psi_acc[s].astype(BF16), 1, 1)[0:1] for s in range(STEPS)]
@@ -569,52 +621,43 @@
                 device_id_type=MESH,
             ).start()
 
-    each(chips, turned_step)
-    each(
+    every(
         chips - 1,
         lambda k: gene_copy(PSI, own_psi, own_psi, 2 * chip_peer(k) + core).start(),
     )
-
-    total_row = sum_0 - 0.5 * trace_ref[...]
-    total_row = total_row[:, 0:128] + total_row[:, 128:256]
-    total_row = total_row - 0.5 * jnp.sum(square_tile, axis=0, keepdims=True)
-    first_row = lax.broadcasted_iota(jnp.int32, (8, 128), 0) == 0
-    total_recv[d] = jnp.where(first_row, jnp.broadcast_to(total_row, (8, 128)), 0.0)
-    own_total = total_recv.at[d]
-    each(DP - 1, lambda k: dp_copy(TOTAL, own_total, own_total, dp_peer(k)).start())
-
-    data_step(0)
-    data_step(2)
-
-    grad_recv[d] = jnp.zeros((2 * LAT, CELLS), BF16)
-    wait_all(GRAD, 1, grad_recv.at[pl.ds(0, DP - 1)])
-    own_grad = first_ref[...]
-    for p in range(DP):
-        own_grad = own_grad + grad_recv[p].astype(F32)
-    first_ref[...] = own_grad
-    give = jnp.where(core == 0, own_grad[LAT : 2 * LAT], own_grad[0:LAT])
-    keep = jnp.where(core == 0, own_grad[0:LAT], own_grad[LAT : 2 * LAT])
-    half_send[...] = give
-
-    def pair_grad_copy():
-        return pair_copy(PAIR_GRAD, half_send, half_recv)
-
-    pair_grad_copy().start()
-
-    data_own[...] = data_rows(z)
+    every(chips, turned_step)
+
+    data_send_rows()
 
     pair_grad_copy().wait_recv()
-    part_all[place] = (keep + half_recv[...]).astype(BF16)
+    totals = jnp.sum(total_tile + half_recv[LAT : LAT + 8], axis=0, keepdims=True)
+    part_all[place, 0:LAT] = (keep + half_recv[0:LAT]).astype(BF16)
+    part_all[place, LAT : LAT + 16] = special(split_three(totals), CELLS)[0:16].astype(BF16)
     own_part = part_all.at[place]
-    each(
+    every(
         chips - 1,
         lambda k: gene_copy(PART, own_part, own_part, 2 * chip_peer(k) + core).start(),
     )
 
-    wait_all(TOTAL, 1, total_recv.at[pl.ds(0, DP - 1)])
-    grand_recv[g] = jnp.sum(total_recv[...], axis=0)
-    own_grand = grand_recv.at[g]
-    each(GENE - 1, lambda k: gene_copy(GRAND, own_grand, own_grand, gene_peer(k)).start())
+    wait_all(EARLY, 1, early_recv.at[pl.ds(0, DP_Z - 1)])
+    early_recv[z] = early_send[z]
+
+    def early_sum(h):
+        total = early_recv[0, h].astype(F32)
+        for p in range(1, DP_Z):
+            total = total + early_recv[p, h].astype(F32)
+        return total
+
+    early_own[...] = early_sum(half)
+    over_send[...] = early_sum(1 - half).astype(BF16)
+
+    def over_copy():
+        return dp_copy(OVER, over_send, over_recv, across)
+
+    over_copy().start()
+
+    data_own[FIRST:BLOCK] = data_rows(z)
+    data_own[0:FIRST] = early_own[...]
 
     def pair_psi_copy():
         return pair_copy(PAIR_PSI, psi_all.at[core], psi_all.at[core])
@@ -624,6 +667,19 @@
 
     wait_all(PSI, 1, psi_all.at[core, pl.ds(0, chips - 1)])
     pair_psi_copy().start()
+
+    wait_all(PART, 1, part_all.at[pl.ds(0, chips - 1)])
+    part_sum = jnp.sum(part_all[...].astype(F32), axis=0)
+    sum_all[core] = part_sum[0:LAT]
+    total_recv[d] = part_sum[LAT : LAT + 8, 0:128] + part_sum[LAT : LAT + 8, 128:256]
+    own_total = total_recv.at[d]
+
+    def pair_sum_copy():
+        return pair_copy(PAIR_SUM, sum_all.at[core], sum_all.at[core])
+
+    pair_sum_copy().start()
+    every(DP - 1, lambda k: dp_copy(TOTAL, own_total, own_total, dp_peer(k)).start())
+
     wait_all(TURNED, 1, turned_all.at[core])
     pair_turned_copy().start()
 
@@ -640,18 +696,14 @@
         )
     data_own[...] = stat
 
-    wait_all(PART, 1, part_all.at[pl.ds(0, chips - 1)])
-    sum_all[core] = jnp.sum(part_all[...].astype(F32), axis=0)
-
-    def pair_sum_copy():
-        return pair_copy(PAIR_SUM, sum_all.at[core], sum_all.at[core])
-
-    pair_sum_copy().start()
-
     wait_all(DATA, 1, data_recv.at[pl.ds(0, DP_Z - 1)])
+    over_copy().wait_recv()
+    data_own[0:FIRST] += over_recv[...].astype(F32)
+    late = data_own[FIRST:BLOCK]
+    for k in range(DP_Z - 1):
+        late = late + data_recv[lax.rem(z + 1 + k, DP_Z)].astype(F32)
+    data_own[FIRST:BLOCK] = late
     stat = data_own[...]
-    for k in range(DP_Z - 1):
-        stat = stat + data_recv[lax.rem(z + 1 + k, DP_Z)].astype(F32)
     pair_turned_copy().wait_recv()
     for o in range(1, 4):
         at = lax.rem(d + (DP - o), DP)
@@ -671,11 +723,11 @@
     out_copy = pltpu.make_async_copy(first_ref, latent_out, local_sem.at[1])
     out_copy.start()
 
-    wait_all(GRAND, 1, grand_recv.at[pl.ds(0, GENE - 1)])
+    wait_all(TOTAL, 1, total_recv.at[pl.ds(0, DP - 1)])
     factor = beta[:, 0:128] / (CELLS * DP * GENES * GENE)
     amplitude = jnp.exp(jnp.full((1, 128), kernel_log, F32))
     rest = (0.5 - 0.5 * beta[:, 0:128] * amplitude) / 1024
-    total_out[0] = jnp.sum(jnp.sum(grand_recv[...], axis=0) * factor + rest)
+    total_out[0] = jnp.sum(jnp.sum(total_recv[...], axis=0) * factor + rest)
 
     latent_across().wait_send()
     pair_gram_copy().wait_send()
@@ -685,6 +737,8 @@
     wait_all(LATENT, 0, lat_all.at[core, pl.ds(0, DP_Z - 1)])
     wait_all(GRAM, 0, gram_recv.at[pl.ds(0, chips - 1)])
     wait_all(GRAD, 0, grad_recv.at[pl.ds(0, DP - 1)])
+    over_copy().wait_send()
+    wait_all(EARLY, 0, early_recv.at[pl.ds(0, DP_Z - 1)])
     wait_all(DATA, 0, data_recv.at[pl.ds(0, DP_Z - 1)])
     wait_all(PSI, 0, psi_all.at[core, pl.ds(0, chips - 1)])
     wait_all(PART, 0, part_all.at[pl.ds(0, chips - 1)])
@@ -692,7 +746,6 @@
     pair_turned_copy().wait_send()
     pair_grad_copy().wait_send()
     pair_sum_copy().wait_send()
-    wait_all(GRAND, 0, grand_recv.at[pl.ds(0, GENE - 1)])
     wait_all(TOTAL, 0, total_recv.at[pl.ds(0, DP - 1)])
     proj_copy.wait()
     out_copy.wait()
@@ -752,8 +805,13 @@
         pltpu.VMEM((GENE // 2, ROWS, WIDTH), F32),
         pltpu.VMEM((GENE // 2, 2 * ROWS, HALF), BF16),
         pltpu.VMEM((GENE // 2, 2 * ROWS, HALF), BF16),
-        pltpu.VMEM((DP_Z, BLOCK, GENES), BF16),
-        pltpu.VMEM((DP_Z, BLOCK, GENES), BF16),
+        pltpu.VMEM((DP_Z, DP // DP_Z, FIRST, GENES), BF16),
+        pltpu.VMEM((DP_Z, DP // DP_Z, FIRST, GENES), BF16),
+        pltpu.VMEM((FIRST, GENES), F32),
+        pltpu.VMEM((FIRST, GENES), BF16),
+        pltpu.VMEM((FIRST, GENES), BF16),
+        pltpu.VMEM((DP_Z, BLOCK - FIRST, GENES), BF16),
+        pltpu.VMEM((DP_Z, BLOCK - FIRST, GENES), BF16),
         pltpu.VMEM((BLOCK, GENES), F32),
         pltpu.VMEM((SPAN, BLOCK, BLOCK), F32),
         pltpu.VMEM((SPAN, BLOCK, BLOCK), F32),
@@ -770,12 +828,11 @@
         pltpu.VMEM((DP, 2 * LAT, CELLS), BF16),
         pltpu.VMEM((2, GENE // 2, ROWS, WIDTH), F32),
         pltpu.VMEM((2, 3, GENE // 2, ROWS, BLOCK), F32),
-        pltpu.VMEM((LAT, CELLS), F32),
-        pltpu.VMEM((LAT, CELLS), F32),
-        pltpu.VMEM((GENE // 2, LAT, CELLS), BF16),
+        pltpu.VMEM((LAT + 8, CELLS), F32),
+        pltpu.VMEM((LAT + 8, CELLS), F32),
+        pltpu.VMEM((GENE // 2, LAT + 16, CELLS), BF16),
         pltpu.VMEM((2, LAT, CELLS), F32),
         pltpu.VMEM((DP, 8, 128), F32),
-        pltpu.VMEM((GENE, 8, 128), F32),
         pltpu.SemaphoreType.DMA((11,)),
         pltpu.SemaphoreType.DMA((KINDS, 2)),
     ]

time: 52.9 us -> 51.6 us (0.975)
  Pallas kernels: 49 us -> 47.7 us
    pallas_call x1, Pallas kernels: 47.2 us -> 45.9 us  [on_device(): pl.pallas_call(kernel, out_shape=(jax.ShapeDtypeStruct((2 * LAT, CELLS),...]
where the time goes in v5:
time: 51.6 us; the launch traced here: 51.5 us
  Pallas kernels  47.7 us (92%)
  between operations  3.74 us (7%)
    pallas_call x1, Pallas kernels, on_device(): pl.pallas_call(kernel, out_shape=(jax.ShapeDtypeStruct((2 * LAT, CELLS),...  45.9 us
    pallas_call x1, Pallas kernels, on_device(): pl.pallas_call(finish, out_shape=(jax.ShapeDtypeStruct((2 * LAT, CELLS),...  1.85 us

profile of v5, /device:TPU:1, one launch (start us, length us, event | category | flops | bytes accessed | tf_op | source)
XLA Modules:
  0.0 51.5 jit_solution(9285001891394888463)
XLA Ops:
  1.9 45.9 %bound_gradients.1 = (f32[64,256]{1,0:T(8,128)}, f32[128,1024]{1,0:T(8,128)}, f32[1]{0:T(128)}) custom-call(bf16[1024,1024]{1,0:T(8,128)(2,1)} %y_hbm.1, s32[1,256]{1,0:T(1,128)} %bitcast.3, f32[32,256]{1,0:T(8,128)} %mean_hbm.1, f32[32,256]{1,0:T(8,128)} %logvar_hbm.1, f32[32,1024]{1,0:T(8,128)} %inducing_hbm.1, f32[1,32]{1,0:T(1,128)} %bitcast.4, ...), custom_call_target="tpu_custom_call" | custom-call | tf_op jit(solution)/shard_map/bound_gradients/pallas_call | solution.py:839
  47.8 1.9 %finish.1 = (f32[64,256]{1,0:T(8,128)}, f32[128,1024]{1,0:T(8,128)}) custom-call(f32[64,256]{1,0:T(8,128)} %get-tuple-element.8.latent_ref, f32[128,1024]{1,0:T(8,128)} %get-tuple-element.9.proj_ref), custom_call_target="tpu_custom_call" | custom-call | tf_op jit(solution)/shard_map/finish/pallas_call | solution.py:865

commit v6 on v5

--- a/solution.py
+++ b/solution.py
@@ -24,13 +24,13 @@
 SPAN = 5
 WIDTH = SPAN * BLOCK
 STEPS = 4
-PAIRS = ROWS * WIDTH // STEPS
+SHARE = ROWS // STEPS
+PAIRS = SHARE * WIDTH
 DEPTH = 256
 HALF = 384
 CLOSING = 4
 FIRST = 64
 (
-    ACROSS,
     LATENT,
     PAIR_LATENT,
     PAIR_GRAM,
@@ -49,7 +49,7 @@
     EARLY,
     OVER,
     KINDS,
-) = range(19)
+) = range(18)
 BLOCK_WEIGHT = (1.0, 2.0, 2.0, 2.0, 1.0)
 
 
@@ -160,12 +160,11 @@
     data_own,
     base_ref,
     norm_ref,
-    row_ref,
+    own_norm_ref,
     pair_feat,
     pair_cols,
     cell_coef,
     inv_width,
-    weight_ref,
     psi_acc,
     first_ref,
     trace_ref,
@@ -281,14 +280,11 @@
     every(3 * (chips - 1), greet_step)
     for copy in small_copies[0:2]:
         copy.wait()
-    lat_all[core, z, half] = jnp.where(core == 0, mean_ref[...], logvar_ref[...])
+    lat_all[core, d] = jnp.where(core == 0, mean_ref[...], logvar_ref[...])
     pl.semaphore_wait(barrier, DP + GENE - 2 + 3 * (chips - 1))
 
-    def latent_across():
-        mine = lat_all.at[core, z, half]
-        return dp_copy(ACROSS, mine, mine, across)
-
-    latent_across().start()
+    own_latent = lat_all.at[core, d]
+    every(DP - 1, lambda k: dp_copy(LATENT, own_latent, own_latent, dp_peer(k)).start())
 
     for k in range(4):
         proj_copies[k].wait()
@@ -358,12 +354,6 @@
         jnp.add, [squares[:, 128 * k : 128 * (k + 1)] for k in range(GENES // 128)]
     )
 
-    latent_across().wait_recv()
-    every(
-        DP_Z - 1,
-        lambda k: dp_copy(LATENT, lat_all.at[core, z], lat_all.at[core, z], z_peer(k)).start(),
-    )
-
     kernel_log = log_var_ref[0]
     eye = lax.broadcasted_iota(jnp.int32, (LAT, LAT), 0) == lax.broadcasted_iota(
         jnp.int32, (LAT, LAT), 1
@@ -388,44 +378,69 @@
     psi_low_ref[...] = psi_one_ref[...].astype(BF16)
     beta = jnp.exp(jnp.full((1, CELLS), log_beta_ref[0], F32))
 
+    def early_step(k):
+        at = lax.rem(z + 1 + k, DP_Z)
+        starts = [pl.multiple_of(BLOCK * (DP_Z * h + at), BLOCK) for h in range(DP // DP_Z)]
+        rows = jnp.concatenate([psi_low_ref[pl.ds(start, FIRST)] for start in starts], axis=0)
+        rows = dot(rows, cell_all[0], 1, 0).astype(BF16)
+        for h in range(DP // DP_Z):
+            early_send[at, h] = rows[FIRST * h : FIRST * (h + 1)]
+
+        @pl.when(k < DP_Z - 1)
+        def _():
+            dp_copy(EARLY, early_send.at[at], early_recv.at[z], z_peer(k)).start()
+
+    each(DP_Z, early_step)
+
     lane = lax.broadcasted_iota(jnp.int32, (BLOCK, BLOCK), 1)
     squared = lax.rem(lane, 2 * LAT) >= LAT
     high_part = lane < 2 * LAT
-    ones = jnp.where((lane >= 64) & (lane < 67), 1.0, 0.0)
     half_inv = (-0.5 * LOG2E) / length
 
     def window(o):
         at = lax.rem(d + o, DP)
         return inducing_ref[:, pl.ds(pl.multiple_of(BLOCK * at, BLOCK), BLOCK)]
 
+    def in_lanes(start, parts, rest):
+        place = lax.broadcasted_iota(jnp.int32, rest.shape, 1)
+        for k, part in enumerate(parts):
+            rest = jnp.where(place == start + k, part, rest)
+        return rest
+
     for o in range(SPAN):
         points = window(o)
         norm = jnp.sum(points * points * half_inv, axis=0, keepdims=True)
-        base_ref[o] = jnp.concatenate([points] * 4, axis=0).T
-        norm_ref[o] = jnp.broadcast_to(norm, (BLOCK, BLOCK)).T
-    own_point = base_ref[0, pl.ds(pl.multiple_of(ROWS * group, ROWS), ROWS)]
-    own_norm = norm_ref[0, pl.ds(pl.multiple_of(ROWS * group, ROWS), ROWS)]
-    row_ref[0] = own_point
-    row_ref[1] = own_norm
+        base_ref[o] = 0.5 * jnp.concatenate([points] * 4, axis=0).T
+        norm = jnp.broadcast_to(norm, (BLOCK, BLOCK)).T
+        ones = jnp.where((lane >= 64) & (lane < 67), 1.0, 0.0)
+        norm_ref[o] = in_lanes(67, split_three(norm), ones)
+        if o == 0:
+            own_norm_ref[...] = norm
+    own = pl.ds(pl.multiple_of(ROWS * group, ROWS), ROWS)
+    point_rows = base_ref[0, own]
+    norm_rows = in_lanes(70, split_three(own_norm_ref[own]), jnp.zeros((ROWS, BLOCK), F32))
 
     def feature_step(i):
-        row = row_ref[0, pl.ds(i, 1)]
-        row_norm = row_ref[1, pl.ds(i, 1)]
         for o in range(SPAN):
-            middle = 0.5 * (base_ref[o] + row)
+            middle = base_ref[o] + point_rows[i : i + 1]
             value = jnp.where(squared, middle * middle, middle)
             high = value.astype(BF16).astype(F32)
-            pair = split_three(norm_ref[o] + row_norm)
-            extra = ones
-            for k in range(3):
-                extra = jnp.where(lane == 67 + k, pair[k], extra)
-            offset = pl.multiple_of(lax.rem(i, 2) * WIDTH + BLOCK * o, BLOCK)
-            at = pl.ds(offset, BLOCK)
-            step = lax.div(i, 2)
-            pair_feat[step, at, 0:128] = jnp.where(high_part, high, value - high).astype(BF16)
-            pair_feat[step, at, 128:256] = jnp.where(high_part, high, extra).astype(BF16)
-
-    each(ROWS, feature_step)
+            extra = norm_ref[o] + norm_rows[i : i + 1]
+            start = WIDTH * (i % SHARE) + BLOCK * o
+            at = slice(start, start + BLOCK)
+            pair_feat[i // SHARE, at, 0:128] = jnp.where(high_part, high, value - high).astype(BF16)
+            pair_feat[i // SHARE, at, 128:256] = jnp.where(high_part, high, extra).astype(BF16)
+
+    every(ROWS, feature_step)
+
+    def latents(kind, at):
+        return lat_all[kind, at]
+
+    def pair_latent_copy():
+        return pair_copy(PAIR_LATENT, lat_all.at[core], lat_all.at[core])
+
+    wait_all(LATENT, 1, lat_all.at[core, pl.ds(0, DP - 1)])
+    pair_latent_copy().start()
 
     cross = dot(proj_low[...], cell_all[0], 1, 1)
     product = psi_one_ref[...] * cross
@@ -440,50 +455,28 @@
         * (inverse * (sum_2 - 2.0 * mean * sum_1 + mean * mean * sum_0) - sum_0)
     )
 
-    def early_step(k):
-        at = lax.rem(z + 1 + k, DP_Z)
-        starts = [pl.multiple_of(BLOCK * (DP_Z * h + at), BLOCK) for h in range(DP // DP_Z)]
-        rows = jnp.concatenate([psi_low_ref[pl.ds(start, FIRST)] for start in starts], axis=0)
-        rows = dot(rows, cell_all[0], 1, 0).astype(BF16)
-        for h in range(DP // DP_Z):
-            early_send[at, h] = rows[FIRST * h : FIRST * (h + 1)]
-
-        @pl.when(k < DP_Z - 1)
-        def _():
-            dp_copy(EARLY, early_send.at[at], early_recv.at[z], z_peer(k)).start()
-
-    each(DP_Z, early_step)
-
-    def latents(kind, at):
-        return lat_all[kind, lax.rem(at, DP_Z), lax.div(at, DP_Z)]
-
-    def pair_latent_copy():
-        return pair_copy(PAIR_LATENT, lat_all.at[core], lat_all.at[core])
-
-    wait_all(LATENT, 1, lat_all.at[core, pl.ds(0, DP_Z - 1)])
-    pair_latent_copy().start()
     wait_all(GRAM, 1, gram_recv.at[pl.ds(0, chips - 1)])
     weight = jnp.sum(gram_recv[...].astype(F32), axis=0)
     weight = jnp.concatenate([weight[0:ROWS], weight[ROWS:, 0 : WIDTH - HALF]], axis=1)
-    weight_ref[...] = weight
     base = window(0)
     own_lane = lax.broadcasted_iota(jnp.int32, (LAT, BLOCK), 1) - ROWS * group
+    first_rows = lax.broadcasted_iota(jnp.int32, (LAT, BLOCK), 0)
 
     def weight_step(i):
         column = jnp.sum(jnp.where(own_lane == i, base, 0.0), axis=1, keepdims=True)
-        row = weight_ref[pl.ds(i, 1)]
         for o in range(SPAN):
-            weight_row = row[:, BLOCK * o : BLOCK * (o + 1)]
+            weight_row = weight[i : i + 1, BLOCK * o : BLOCK * (o + 1)]
             middle = 0.5 * (window(o) + column)
             linear = middle * weight_row
             high, low = split_two(linear)
-            block = jnp.concatenate(
-                [high, middle * linear, low, special(split_two(weight_row), BLOCK)[0:32]], axis=0
-            )
-            offset = pl.multiple_of(lax.rem(i, 2) * WIDTH + BLOCK * o, BLOCK)
-            pair_cols[lax.div(i, 2), :, pl.ds(offset, BLOCK)] = block.astype(BF16)
-
-    each(ROWS, weight_step)
+            weight_high, weight_low = split_two(weight_row)
+            rest = jnp.where(first_rows == 0, weight_high, 0.0)
+            rest = jnp.where(first_rows == 1, weight_low, rest)
+            block = jnp.concatenate([high, middle * linear, low, rest], axis=0)
+            start = WIDTH * (i % SHARE) + BLOCK * o
+            pair_cols[i // SHARE, :, start : start + BLOCK] = block.astype(BF16)
+
+    every(ROWS, weight_step)
     psi_acc[...] = jnp.zeros_like(psi_acc)
     trace_ref[...] = jnp.zeros_like(trace_ref)
 
@@ -503,7 +496,7 @@
             (2.0 * LOG2E) * cell_mean * inverse_w,
             (2.0 * LOG2E) * cell_var * inverse_w / length,
             LOG2E * const,
-            3,
+            6,
         )
         cell_coef[at] = block.astype(BF16)
 
@@ -604,7 +597,11 @@
     add_lanes = jnp.ones((16, 128), BF16)
     sums = [dot(add_lanes, psi_acc[s].astype(BF16), 1, 1)[0:1] for s in range(STEPS)]
     rows = jnp.concatenate(
-        [sums[i // 2][:, WIDTH * (i % 2) : WIDTH * (i % 2 + 1)] for i in range(ROWS)], axis=0
+        [
+            sums[i // SHARE][:, WIDTH * (i % SHARE) : WIDTH * (i % SHARE + 1)]
+            for i in range(ROWS)
+        ],
+        axis=0,
     )
     psi_all[core, place] = rows
     own_psi = psi_all.at[core, place]
@@ -729,12 +726,11 @@
     rest = (0.5 - 0.5 * beta[:, 0:128] * amplitude) / 1024
     total_out[0] = jnp.sum(jnp.sum(total_recv[...], axis=0) * factor + rest)
 
-    latent_across().wait_send()
     pair_gram_copy().wait_send()
     cell_copy().wait_send()
     pair_latent_copy().wait_send()
     pair_psi_copy().wait_send()
-    wait_all(LATENT, 0, lat_all.at[core, pl.ds(0, DP_Z - 1)])
+    wait_all(LATENT, 0, lat_all.at[core, pl.ds(0, DP - 1)])
     wait_all(GRAM, 0, gram_recv.at[pl.ds(0, chips - 1)])
     wait_all(GRAD, 0, grad_recv.at[pl.ds(0, DP - 1)])
     over_copy().wait_send()
@@ -800,7 +796,7 @@
         pltpu.VMEM((IND, CELLS), F32),
         pltpu.VMEM((IND, CELLS), BF16),
         pltpu.VMEM((DP_Z * BLOCK, CELLS), BF16),
-        pltpu.VMEM((2, DP_Z, DP // DP_Z, LAT, CELLS), F32),
+        pltpu.VMEM((2, DP, LAT, CELLS), F32),
         pltpu.VMEM((GENE, ROWS, WIDTH), F32),
         pltpu.VMEM((GENE // 2, ROWS, WIDTH), F32),
         pltpu.VMEM((GENE // 2, 2 * ROWS, HALF), BF16),
@@ -815,12 +811,11 @@
         pltpu.VMEM((BLOCK, GENES), F32),
         pltpu.VMEM((SPAN, BLOCK, BLOCK), F32),
         pltpu.VMEM((SPAN, BLOCK, BLOCK), F32),
-        pltpu.VMEM((2, ROWS, BLOCK), F32),
+        pltpu.VMEM((BLOCK, BLOCK), F32),
         pltpu.VMEM((STEPS, PAIRS, DEPTH), BF16),
         pltpu.VMEM((STEPS, 128, PAIRS), BF16),
         pltpu.VMEM((DP, DEPTH, CELLS), BF16),
         pltpu.VMEM((DP, LAT, CELLS), F32),
-        pltpu.VMEM((ROWS, WIDTH), F32),
         pltpu.VMEM((STEPS, PAIRS, 128), F32),
         pltpu.VMEM((2 * LAT, CELLS), F32),
         pltpu.VMEM((1, CELLS), F32),

time: 51.6 us -> 49.5 us (0.959)
  Pallas kernels: 47.7 us -> 45.6 us
    pallas_call x1, Pallas kernels: 45.9 us -> 43.8 us  [on_device(): pl.pallas_call(kernel, out_shape=(jax.ShapeDtypeStruct((2 * LAT, CELLS),...]
where the time goes in v6:
time: 49.5 us; the launch traced here: 49.3 us
  Pallas kernels  45.6 us (92%)
  between operations  3.74 us (8%)
    pallas_call x1, Pallas kernels, on_device(): pl.pallas_call(kernel, out_shape=(jax.ShapeDtypeStruct((2 * LAT, CELLS),...  43.8 us
    pallas_call x1, Pallas kernels, on_device(): pl.pallas_call(finish, out_shape=(jax.ShapeDtypeStruct((2 * LAT, CELLS),...  1.85 us

profile of v6, /device:TPU:1, one launch (start us, length us, event | category | flops | bytes accessed | tf_op | source)
XLA Modules:
  0.0 49.3 jit_solution(14503179162799526533)
XLA Ops:
  1.9 43.8 %bound_gradients.1 = (f32[64,256]{1,0:T(8,128)}, f32[128,1024]{1,0:T(8,128)}, f32[1]{0:T(128)}) custom-call(bf16[1024,1024]{1,0:T(8,128)(2,1)} %y_hbm.1, s32[1,256]{1,0:T(1,128)} %bitcast.3, f32[32,256]{1,0:T(8,128)} %mean_hbm.1, f32[32,256]{1,0:T(8,128)} %logvar_hbm.1, f32[32,1024]{1,0:T(8,128)} %inducing_hbm.1, f32[1,32]{1,0:T(1,128)} %bitcast.4, ...), custom_call_target="tpu_custom_call" | custom-call | tf_op jit(solution)/shard_map/bound_gradients/pallas_call | solution.py:834
  45.7 1.9 %finish.1 = (f32[64,256]{1,0:T(8,128)}, f32[128,1024]{1,0:T(8,128)}) custom-call(f32[64,256]{1,0:T(8,128)} %get-tuple-element.8.latent_ref, f32[128,1024]{1,0:T(8,128)} %get-tuple-element.9.proj_ref), custom_call_target="tpu_custom_call" | custom-call | tf_op jit(solution)/shard_map/finish/pallas_call | solution.py:860

commit v7 on v6

--- a/solution.py
+++ b/solution.py
@@ -215,7 +215,8 @@
         return side + lax.rem(z + 1 + k, DP_Z)
 
     def cell_order(k):
-        return lax.rem(side + DP_Z * (1 - lax.div(k, DP_Z)), DP) + lax.rem(z + 1 + k, DP_Z)
+        far = 1 - lax.div(DP - 2 - k, DP_Z)
+        return lax.rem(side + DP_Z * far, DP) + lax.rem(z + 1 + k + far, DP_Z)
 
     def dp_copy(kind, src, dst, peer):
         return remote(src, dst, "dp", sems.at[kind, 0], sems.at[kind, 1], peer)
@@ -455,6 +456,28 @@
         * (inverse * (sum_2 - 2.0 * mean * sum_1 + mean * mean * sum_0) - sum_0)
     )
 
+    pair_latent_copy().wait_recv()
+
+    def coefficient_step(at):
+        cell_mean = latents(0, at)
+        cell_var = jnp.exp(latents(1, at))
+        inverse_w = 1.0 / (length + 2.0 * cell_var)
+        inv_width[at] = inverse_w
+        const = 2.0 * kernel_log + jnp.sum(
+            0.5 * jnp.log(length * inverse_w) - cell_mean * cell_mean * inverse_w,
+            axis=0,
+            keepdims=True,
+        )
+        block = cell_coefficients(
+            (2.0 * LOG2E) * cell_mean * inverse_w,
+            (2.0 * LOG2E) * cell_var * inverse_w / length,
+            LOG2E * const,
+            6,
+        )
+        cell_coef[at] = block.astype(BF16)
+
+    each(DP, coefficient_step)
+
     wait_all(GRAM, 1, gram_recv.at[pl.ds(0, chips - 1)])
     weight = jnp.sum(gram_recv[...].astype(F32), axis=0)
     weight = jnp.concatenate([weight[0:ROWS], weight[ROWS:, 0 : WIDTH - HALF]], axis=1)
@@ -479,28 +502,6 @@
     every(ROWS, weight_step)
     psi_acc[...] = jnp.zeros_like(psi_acc)
     trace_ref[...] = jnp.zeros_like(trace_ref)
-
-    pair_latent_copy().wait_recv()
-
-    def coefficient_step(at):
-        cell_mean = latents(0, at)
-        cell_var = jnp.exp(latents(1, at))
-        inverse_w = 1.0 / (length + 2.0 * cell_var)
-        inv_width[at] = inverse_w
-        const = 2.0 * kernel_log + jnp.sum(
-            0.5 * jnp.log(length * inverse_w) - cell_mean * cell_mean * inverse_w,
-            axis=0,
-            keepdims=True,
-        )
-        block = cell_coefficients(
-            (2.0 * LOG2E) * cell_mean * inverse_w,
-            (2.0 * LOG2E) * cell_var * inverse_w / length,
-            LOG2E * const,
-            6,
-        )
-        cell_coef[at] = block.astype(BF16)
-
-    each(DP, coefficient_step)
 
     def cell_gradients(at):
         table = jnp.zeros((128, CELLS), F32)

time: 49.5 us -> 48.8 us (0.986)
  Pallas kernels: 45.6 us -> 44.9 us
    pallas_call x1, Pallas kernels: 43.8 us -> 43 us  [on_device(): pl.pallas_call(kernel, out_shape=(jax.ShapeDtypeStruct((2 * LAT, CELLS),...]
where the time goes in v7:
time: 48.8 us; the launch traced here: 48.6 us
  Pallas kernels  44.9 us (92%)
  between operations  3.74 us (8%)
    pallas_call x1, Pallas kernels, on_device(): pl.pallas_call(kernel, out_shape=(jax.ShapeDtypeStruct((2 * LAT, CELLS),...  43 us
    pallas_call x1, Pallas kernels, on_device(): pl.pallas_call(finish, out_shape=(jax.ShapeDtypeStruct((2 * LAT, CELLS),...  1.85 us

profile of v7, /device:TPU:1, one launch (start us, length us, event | category | flops | bytes accessed | tf_op | source)
XLA Modules:
  0.0 48.6 jit_solution(15555899465834091931)
XLA Ops:
  1.9 43.0 %bound_gradients.1 = (f32[64,256]{1,0:T(8,128)}, f32[128,1024]{1,0:T(8,128)}, f32[1]{0:T(128)}) custom-call(bf16[1024,1024]{1,0:T(8,128)(2,1)} %y_hbm.1, s32[1,256]{1,0:T(1,128)} %bitcast.3, f32[32,256]{1,0:T(8,128)} %mean_hbm.1, f32[32,256]{1,0:T(8,128)} %logvar_hbm.1, f32[32,1024]{1,0:T(8,128)} %inducing_hbm.1, f32[1,32]{1,0:T(1,128)} %bitcast.4, ...), custom_call_target="tpu_custom_call" | custom-call | tf_op jit(solution)/shard_map/bound_gradients/pallas_call | solution.py:835
  45.0 1.9 %finish.1 = (f32[64,256]{1,0:T(8,128)}, f32[128,1024]{1,0:T(8,128)}) custom-call(f32[64,256]{1,0:T(8,128)} %get-tuple-element.8.latent_ref, f32[128,1024]{1,0:T(8,128)} %get-tuple-element.9.proj_ref), custom_call_target="tpu_custom_call" | custom-call | tf_op jit(solution)/shard_map/finish/pallas_call | solution.py:861

commit v8 on v7

--- a/solution.py
+++ b/solution.py
@@ -570,6 +570,8 @@
 
         every(DP_Z - 1, send_step)
 
+    data_send_rows()
+
     by_mean, by_logvar = cell_gradients(d)
     first_ref[0:LAT] += by_mean
     first_ref[LAT : 2 * LAT] += by_logvar
@@ -624,8 +626,6 @@
         lambda k: gene_copy(PSI, own_psi, own_psi, 2 * chip_peer(k) + core).start(),
     )
     every(chips, turned_step)
-
-    data_send_rows()
 
     pair_grad_copy().wait_recv()
     totals = jnp.sum(total_tile + half_recv[LAT : LAT + 8], axis=0, keepdims=True)

time: 48.8 us -> 48.8 us (level)
  no operation moved by 1% of the time
where the time goes in v8:
time: 48.8 us; the launch traced here: 48.6 us
  Pallas kernels  44.9 us (92%)
  between operations  3.74 us (8%)
    pallas_call x1, Pallas kernels, on_device(): pl.pallas_call(kernel, out_shape=(jax.ShapeDtypeStruct((2 * LAT, CELLS),...  43 us
    pallas_call x1, Pallas kernels, on_device(): pl.pallas_call(finish, out_shape=(jax.ShapeDtypeStruct((2 * LAT, CELLS),...  1.85 us

profile of v8, /device:TPU:1, one launch (start us, length us, event | category | flops | bytes accessed | tf_op | source)
XLA Modules:
  0.0 48.6 jit_solution(13328918430225231597)
XLA Ops:
  1.9 43.0 %bound_gradients.1 = (f32[64,256]{1,0:T(8,128)}, f32[128,1024]{1,0:T(8,128)}, f32[1]{0:T(128)}) custom-call(bf16[1024,1024]{1,0:T(8,128)(2,1)} %y_hbm.1, s32[1,256]{1,0:T(1,128)} %bitcast.3, f32[32,256]{1,0:T(8,128)} %mean_hbm.1, f32[32,256]{1,0:T(8,128)} %logvar_hbm.1, f32[32,1024]{1,0:T(8,128)} %inducing_hbm.1, f32[1,32]{1,0:T(1,128)} %bitcast.4, ...), custom_call_target="tpu_custom_call" | custom-call | tf_op jit(solution)/shard_map/bound_gradients/pallas_call | solution.py:835
  45.0 1.9 %finish.1 = (f32[64,256]{1,0:T(8,128)}, f32[128,1024]{1,0:T(8,128)}) custom-call(f32[64,256]{1,0:T(8,128)} %get-tuple-element.8.latent_ref, f32[128,1024]{1,0:T(8,128)} %get-tuple-element.9.proj_ref), custom_call_target="tpu_custom_call" | custom-call | tf_op jit(solution)/shard_map/finish/pallas_call | solution.py:861
